TPU v7x, 32 devices: a whole 2x2x4 slice. The times are simulated.
32 devices in a mesh: rep: 8 (over z, y), grp: 4 (over x, core).
Axes of the slice: x: 2, y: 2, z: 4, core: 2. Of those that a mesh axis runs over, the one named last changes fastest.
Arguments:
- tokens: bfloat16 [32768, 1024], P(('rep', 'grp')), may hold values from -6 to 6
- segments: int32 [32768], P(('rep', 'grp')), may hold values from 0 to 79, never falling along the last dimension, each value on 1 to 800 neighbouring positions
- attn_gain: bfloat16 [1024], P('grp'), may hold values from 0.3984375 to 1.59375
- w_query: bfloat16 [1024, 1024], P('grp'), may hold values from -0.1875 to 0.1875
- w_key: bfloat16 [1024, 512], P('grp'), may hold values from -0.1875 to 0.1875
- w_value: bfloat16 [1024, 512], P('grp'), may hold values from -0.1875 to 0.1875
- query_gain: bfloat16 [64], P('grp'), may hold values from 0.099609375 to 1.8984375
- key_gain: bfloat16 [64], P('grp'), may hold values from 0.099609375 to 1.8984375
- w_out: bfloat16 [1024, 1024], P('grp'), may hold values from -0.75 to 0.75
- ffn_gain: bfloat16 [1024], P('grp'), may hold values from 0.3984375 to 1.59375
- w_gate: bfloat16 [1024, 4608], P('grp'), may hold values from -0.1875 to 0.1875
- w_up: bfloat16 [1024, 4608], P('grp'), may hold values from -0.1875 to 0.1875
- w_down: bfloat16 [4608, 1024], P('grp'), may hold values from -0.09375 to 0.09375
- out_grad: bfloat16 [32768, 1024], P(('rep', 'grp')), may hold values from -6 to 6
Outputs:
- outputs: bfloat16 [32768, 1024], P(('rep', 'grp'))
- input_grad: bfloat16 [32768, 1024], P(('rep', 'grp'))
- attn_gain_grad: float32 [1024], P('grp')
- query_wgrad: float32 [1024, 1024], P('grp')
- key_wgrad: float32 [1024, 512], P('grp')
- value_wgrad: float32 [1024, 512], P('grp')
- query_gain_grad: float32 [64], P('grp')
- key_gain_grad: float32 [64], P('grp')
- out_wgrad: float32 [1024, 1024], P('grp')
- ffn_gain_grad: float32 [1024], P('grp')
- gate_wgrad: float32 [1024, 4608], P('grp')
- up_wgrad: float32 [1024, 4608], P('grp')
- down_wgrad: float32 [4608, 1024], P('grp')
Inputs may be any that keep to these rules, and one draw needn't show every extreme that they name: `segments`: document numbers never fall along the tokens; each document has 1 to 800 tokens, and some document has exactly 800.
All inputs are finite; a program needn't handle non-finite values.
Results may differ from a plain program's by a relative error of at most 0.017.
Values may be sent and summed in bfloat16 or wider, within the bound.
No kernel may reach another device: no remote copies, remote signals or barrier semaphores. Data moves between devices by JAX's collectives and lax.ppermute only.
A program may use at most 320 MiB of HBM per device.

v0:
```python
import jax
import jax.numpy as jnp
from jax import lax
from jax.sharding import PartitionSpec as P

H = 16
KV = 8
HD = 64
SEQ = 1024


epsilon = 1e-05
theta_base = 1000000.0


def rms_scale(values):
    return lax.rsqrt(jnp.mean(values * values, axis=-1, keepdims=True) + epsilon)


def norm_back(grad_unit, unit, inverse):
    return inverse * (grad_unit - unit * jnp.mean(grad_unit * unit, axis=-1, keepdims=True))


def doc_positions(segment_rows):
    seq_len = segment_rows.shape[-1]
    places = jnp.arange(seq_len, dtype=jnp.int32)
    keep_mask = (segment_rows[:, :, None] == segment_rows[:, None, :]) & (
        places[None, None, :] <= places[None, :, None]
    )
    return (jnp.sum(keep_mask.astype(jnp.int32), axis=-1) - 1).astype(jnp.float32)


def rope_tables(positions):
    half_width = HD // 2
    freqs = theta_base ** (-(2.0 * jnp.arange(half_width, dtype=jnp.float32)) / HD)
    angles = positions[:, None] * freqs[None, :]
    return (jnp.cos(angles), jnp.sin(angles))


def rotate(values, cos_table, sin_table):
    half_width = values.shape[-1] // 2
    first_half = values[..., :half_width]
    second_half = values[..., half_width:]
    cos_rows = cos_table[:, None, :]
    sin_rows = sin_table[:, None, :]
    return jnp.concatenate(
        [
            first_half * cos_rows - second_half * sin_rows,
            second_half * cos_rows + first_half * sin_rows,
        ],
        axis=-1,
    )


def head_norm_back(grad_rot, unit, inverse, gain, cos_table, sin_table):
    grad_norm = rotate(grad_rot, cos_table, -sin_table)
    gain_grad = jnp.sum(grad_norm * unit, axis=(0, 1))
    return (norm_back(grad_norm * gain, unit, inverse), gain_grad)


def outer_sum(left, right):
    return lax.dot_general(
        left, right, (((0,), (0,)), ((), ())), preferred_element_type=jnp.float32
    )


def back_dot(grad, weight):
    return lax.dot_general(
        grad, weight, (((1,), (1,)), ((), ())), preferred_element_type=jnp.float32
    )


def block_mask(segment, row_start, block_rows):
    key_count = segment.shape[0]
    row_ids = row_start + jnp.arange(block_rows, dtype=jnp.int32)
    row_segs = lax.dynamic_slice_in_dim(segment, row_start, block_rows)
    return (row_segs[:, None] == segment[None, :]) & (
        jnp.arange(key_count, dtype=jnp.int32)[None, :] <= row_ids[:, None]
    )


def masked_scores(query_block, keys, keep_mask, score_scale):
    raw = (
        jnp.einsum("qcrd,kcd->crqk", query_block, keys, preferred_element_type=jnp.float32)
        * score_scale
    )
    return jnp.where(keep_mask[None, None], raw, -1e30)


def attend_sequence(query, keys, values, segment, block_rows, score_scale):
    key_count = query.shape[0]
    block_count = key_count // block_rows
    query_blocks = query.reshape((block_count, block_rows) + query.shape[1:])
    row_starts = jnp.arange(block_count, dtype=jnp.int32) * block_rows

    def one_block(items):
        query_block, row_start = items
        scores = masked_scores(
            query_block, keys, block_mask(segment, row_start, block_rows), score_scale
        )
        row_max = jnp.max(scores, axis=-1, keepdims=True)
        exp_scores = jnp.exp(scores - row_max)
        row_total = jnp.sum(exp_scores, axis=-1, keepdims=True)
        weights_low = (exp_scores / row_total).astype(jnp.bfloat16)
        mixed = jnp.einsum(
            "crqk,kcd->qcrd", weights_low, values, preferred_element_type=jnp.float32
        )
        return (mixed.astype(jnp.bfloat16), row_max[..., 0] + jnp.log(row_total[..., 0]))

    mixed_blocks, lse_blocks = lax.map(one_block, (query_blocks, row_starts))
    return (mixed_blocks.reshape(query.shape), lse_blocks)


def attend_back(query, keys, values, mixed_grad, lse_blocks, segment, block_rows, score_scale):
    key_count = query.shape[0]
    block_count = key_count // block_rows
    query_blocks = query.reshape((block_count, block_rows) + query.shape[1:])
    grad_blocks = mixed_grad.reshape((block_count, block_rows) + query.shape[1:])
    row_starts = jnp.arange(block_count, dtype=jnp.int32) * block_rows

    def one_block(carry, items):
        key_grad, value_grad = carry
        query_block, grad_block, lse_block, row_start = items
        scores = masked_scores(
            query_block, keys, block_mask(segment, row_start, block_rows), score_scale
        )
        probs = jnp.exp(scores - lse_block[..., None])
        prob_grad = jnp.einsum(
            "qcrd,kcd->crqk", grad_block, values, preferred_element_type=jnp.float32
        )
        inner = jnp.sum(probs * prob_grad, axis=-1, keepdims=True)
        score_grad = (probs * (prob_grad - inner)).astype(jnp.bfloat16)
        query_grad = (
            jnp.einsum("crqk,kcd->qcrd", score_grad, keys, preferred_element_type=jnp.float32)
            * score_scale
        )
        key_grad = (
            key_grad
            + jnp.einsum(
                "crqk,qcrd->kcd", score_grad, query_block, preferred_element_type=jnp.float32
            )
            * score_scale
        )
        value_grad = value_grad + jnp.einsum(
            "crqk,qcrd->kcd",
            probs.astype(jnp.bfloat16),
            grad_block,
            preferred_element_type=jnp.float32,
        )
        return ((key_grad, value_grad), query_grad)

    zero_kv = jnp.zeros(keys.shape, jnp.float32)
    (key_grad, value_grad), query_grads = lax.scan(
        one_block, (zero_kv, zero_kv), (query_blocks, grad_blocks, lse_blocks, row_starts)
    )
    return (query_grads.reshape(query.shape), key_grad, value_grad)


def on_device(
    tokens,
    segments,
    attn_gain,
    w_query,
    w_key,
    w_value,
    query_gain,
    key_gain,
    w_out,
    ffn_gain,
    w_gate,
    w_up,
    w_down,
    out_grad,
):
    token_count = tokens.shape[0]
    seq_count = token_count // SEQ
    group_heads = H // KV
    block_rows = min(512, SEQ)
    score_scale = HD ** (-0.5)
    attn_full = (
        lax.all_gather(attn_gain, "grp", axis=0, tiled=True),
        lax.all_gather(w_query, "grp", axis=0, tiled=True),
        lax.all_gather(w_key, "grp", axis=0, tiled=True),
        lax.all_gather(w_value, "grp", axis=0, tiled=True),
        lax.all_gather(query_gain, "grp", axis=0, tiled=True),
        lax.all_gather(key_gain, "grp", axis=0, tiled=True),
        lax.all_gather(w_out, "grp", axis=0, tiled=True),
    )
    inputs = tokens.astype(jnp.float32)
    seg_rows = segments.reshape(seq_count, SEQ)
    positions = doc_positions(seg_rows).reshape(token_count)
    cos_table, sin_table = rope_tables(positions)
    first_inv = rms_scale(inputs)
    first_unit = inputs * first_inv
    first_low = (first_unit * attn_full[0].astype(jnp.float32)).astype(jnp.bfloat16)
    query_proj = jnp.dot(first_low, attn_full[1], preferred_element_type=jnp.float32).reshape(
        token_count, H, HD
    )
    key_proj = jnp.dot(first_low, attn_full[2], preferred_element_type=jnp.float32).reshape(
        token_count, KV, HD
    )
    value_low = jnp.dot(first_low, attn_full[3], preferred_element_type=jnp.float32).astype(
        jnp.bfloat16
    )
    query_inv = rms_scale(query_proj)
    query_unit = query_proj * query_inv
    query_low = rotate(query_unit * attn_full[4].astype(jnp.float32), cos_table, sin_table).astype(
        jnp.bfloat16
    )
    key_inv = rms_scale(key_proj)
    key_unit = key_proj * key_inv
    key_low = rotate(key_unit * attn_full[5].astype(jnp.float32), cos_table, sin_table).astype(
        jnp.bfloat16
    )
    query_seq = query_low.reshape(seq_count, SEQ, KV, group_heads, HD)
    key_seq = key_low.reshape(seq_count, SEQ, KV, HD)
    value_seq = value_low.reshape(seq_count, SEQ, KV, HD)

    def forward_sequence(items):
        return attend_sequence(items[0], items[1], items[2], items[3], block_rows, score_scale)

    mixed_seq, lse_seq = lax.map(forward_sequence, (query_seq, key_seq, value_seq, seg_rows))
    mixed_low = mixed_seq.reshape(token_count, H * HD)
    residual = inputs + jnp.dot(mixed_low, attn_full[6], preferred_element_type=jnp.float32)
    ffn_full = (
        lax.all_gather(ffn_gain, "grp", axis=0, tiled=True),
        lax.all_gather(w_gate, "grp", axis=0, tiled=True),
        lax.all_gather(w_up, "grp", axis=0, tiled=True),
        lax.all_gather(w_down, "grp", axis=0, tiled=True),
    )
    second_inv = rms_scale(residual)
    second_unit = residual * second_inv
    second_low = (second_unit * ffn_full[0].astype(jnp.float32)).astype(jnp.bfloat16)
    gate_val = jnp.dot(second_low, ffn_full[1], preferred_element_type=jnp.float32)
    up_val = jnp.dot(second_low, ffn_full[2], preferred_element_type=jnp.float32)
    sigmoid_gate = jax.nn.sigmoid(gate_val)
    silu_gate = gate_val * sigmoid_gate
    inner_low = (silu_gate * up_val).astype(jnp.bfloat16)
    outputs = (
        residual + jnp.dot(inner_low, ffn_full[3], preferred_element_type=jnp.float32)
    ).astype(jnp.bfloat16)
    ffn_back = (
        lax.all_gather(ffn_gain, "grp", axis=0, tiled=True),
        lax.all_gather(w_gate, "grp", axis=0, tiled=True),
        lax.all_gather(w_up, "grp", axis=0, tiled=True),
        lax.all_gather(w_down, "grp", axis=0, tiled=True),
    )
    down_wgrad = outer_sum(inner_low, out_grad)
    inner_grad = back_dot(out_grad, ffn_back[3])
    gate_grad = (
        inner_grad * up_val * sigmoid_gate * (1.0 + gate_val * (1.0 - sigmoid_gate))
    ).astype(jnp.bfloat16)
    up_grad = (inner_grad * silu_gate).astype(jnp.bfloat16)
    gate_wgrad = outer_sum(second_low, gate_grad)
    up_wgrad = outer_sum(second_low, up_grad)
    second_grad = back_dot(gate_grad, ffn_back[1]) + back_dot(up_grad, ffn_back[2])
    ffn_gain_grad = jnp.sum(second_grad * second_unit, axis=0)
    residual_grad = out_grad.astype(jnp.float32) + norm_back(
        second_grad * ffn_back[0].astype(jnp.float32), second_unit, second_inv
    )
    ffn_owned = (
        lax.psum_scatter(
            ffn_gain_grad.astype(jnp.bfloat16), "grp", scatter_dimension=0, tiled=True
        ).astype(jnp.float32),
        lax.psum_scatter(
            gate_wgrad.astype(jnp.bfloat16), "grp", scatter_dimension=0, tiled=True
        ).astype(jnp.float32),
        lax.psum_scatter(
            up_wgrad.astype(jnp.bfloat16), "grp", scatter_dimension=0, tiled=True
        ).astype(jnp.float32),
        lax.psum_scatter(
            down_wgrad.astype(jnp.bfloat16), "grp", scatter_dimension=0, tiled=True
        ).astype(jnp.float32),
    )
    ffn_done = lax.psum((ffn_owned[0], ffn_owned[1], ffn_owned[2], ffn_owned[3]), "rep")
    residual_low = residual_grad.astype(jnp.bfloat16)
    attn_back = (
        lax.all_gather(attn_gain, "grp", axis=0, tiled=True),
        lax.all_gather(w_query, "grp", axis=0, tiled=True),
        lax.all_gather(w_key, "grp", axis=0, tiled=True),
        lax.all_gather(w_value, "grp", axis=0, tiled=True),
        lax.all_gather(query_gain, "grp", axis=0, tiled=True),
        lax.all_gather(key_gain, "grp", axis=0, tiled=True),
        lax.all_gather(w_out, "grp", axis=0, tiled=True),
    )
    out_wgrad = outer_sum(mixed_low, residual_low)
    mixed_grad = back_dot(residual_low, attn_back[6]).astype(jnp.bfloat16)
    grad_seq = mixed_grad.reshape(seq_count, SEQ, KV, group_heads, HD)

    def backward_sequence(items):
        return attend_back(
            items[0], items[1], items[2], items[3], items[4], items[5], block_rows, score_scale
        )

    query_grad_seq, key_grad_seq, value_grad_seq = lax.map(
        backward_sequence, (query_seq, key_seq, value_seq, grad_seq, lse_seq, seg_rows)
    )
    query_proj_grad, query_gain_grad = head_norm_back(
        query_grad_seq.reshape(token_count, H, HD),
        query_unit,
        query_inv,
        attn_back[4].astype(jnp.float32),
        cos_table,
        sin_table,
    )
    key_proj_grad, key_gain_grad = head_norm_back(
        key_grad_seq.reshape(token_count, KV, HD),
        key_unit,
        key_inv,
        attn_back[5].astype(jnp.float32),
        cos_table,
        sin_table,
    )
    query_grad_low = query_proj_grad.reshape(token_count, H * HD).astype(jnp.bfloat16)
    key_grad_low = key_proj_grad.reshape(token_count, KV * HD).astype(jnp.bfloat16)
    value_grad_low = value_grad_seq.reshape(token_count, KV * HD).astype(jnp.bfloat16)
    query_wgrad = outer_sum(first_low, query_grad_low)
    key_wgrad = outer_sum(first_low, key_grad_low)
    value_wgrad = outer_sum(first_low, value_grad_low)
    first_grad = (
        back_dot(query_grad_low, attn_back[1])
        + back_dot(key_grad_low, attn_back[2])
        + back_dot(value_grad_low, attn_back[3])
    )
    attn_gain_grad = jnp.sum(first_grad * first_unit, axis=0)
    input_grad = (
        residual_grad
        + norm_back(first_grad * attn_back[0].astype(jnp.float32), first_unit, first_inv)
    ).astype(jnp.bfloat16)
    attn_owned = (
        lax.psum_scatter(
            attn_gain_grad.astype(jnp.bfloat16), "grp", scatter_dimension=0, tiled=True
        ).astype(jnp.float32),
        lax.psum_scatter(
            query_wgrad.astype(jnp.bfloat16), "grp", scatter_dimension=0, tiled=True
        ).astype(jnp.float32),
        lax.psum_scatter(
            key_wgrad.astype(jnp.bfloat16), "grp", scatter_dimension=0, tiled=True
        ).astype(jnp.float32),
        lax.psum_scatter(
            value_wgrad.astype(jnp.bfloat16), "grp", scatter_dimension=0, tiled=True
        ).astype(jnp.float32),
        lax.psum_scatter(
            query_gain_grad.astype(jnp.bfloat16), "grp", scatter_dimension=0, tiled=True
        ).astype(jnp.float32),
        lax.psum_scatter(
            key_gain_grad.astype(jnp.bfloat16), "grp", scatter_dimension=0, tiled=True
        ).astype(jnp.float32),
        lax.psum_scatter(
            out_wgrad.astype(jnp.bfloat16), "grp", scatter_dimension=0, tiled=True
        ).astype(jnp.float32),
    )
    attn_done = lax.psum(
        (
            attn_owned[0],
            attn_owned[1],
            attn_owned[2],
            attn_owned[3],
            attn_owned[4],
            attn_owned[5],
            attn_owned[6],
        ),
        "rep",
    )
    grads_done = attn_done + ffn_done
    return (
        outputs,
        input_grad,
        grads_done[0],
        grads_done[1],
        grads_done[2],
        grads_done[3],
        grads_done[4],
        grads_done[5],
        grads_done[6],
        grads_done[7],
        grads_done[8],
        grads_done[9],
        grads_done[10],
    )


def solution(mesh):
    placed = (
        P(("rep", "grp"), None),
        P(("rep", "grp")),
        P("grp"),
        P("grp", None),
        P("grp", None),
        P("grp", None),
        P("grp"),
        P("grp"),
        P("grp", None),
        P("grp"),
        P("grp", None),
        P("grp", None),
        P("grp", None),
        P(("rep", "grp"), None),
    )
    return jax.shard_map(
        on_device,
        mesh=mesh,
        in_specs=placed,
        out_specs=(
            P(("rep", "grp"), None),
            P(("rep", "grp"), None),
            P("grp"),
            P("grp", None),
            P("grp", None),
            P("grp", None),
            P("grp"),
            P("grp"),
            P("grp", None),
            P("grp"),
            P("grp", None),
            P("grp", None),
            P("grp", None),
        ),
        check_vma=False,
    )
```

profile of v0, /device:TPU:0, one launch (start us, length us, event | category | flops | bytes accessed | tf_op | source)
XLA Modules:
  0.0 1719.5 jit_solution(10442079736387149550)
XLA Ops:
  51.6 20.0 %all-gather.10.cloned.1.call-done = bf16[1024,1024]{1,0:T(8,128)(2,1)} async-done(((bf16[256,1024]{1,0:T(8,128)(2,1)}), bf16[1024,1024]{1,0:T(8,128)(2,1)}) %all-gather.10.cloned.1.call-update) | async-done | bytes 2097168 | tf_op jit(solution)/shard_map/all_gather | solution.py:182
  85.8 102.6 %while.47 = (s32[]{:T(128)}, bf16[2,512,8,2,64]{1,4,3,2,0:T(8,128)(2,1)}, f32[2,8,2,512]{3,2,1,0:T(2,128)S(1)}, s32[2]{0:T(128)S(1)}, s32[1024]{0:T(1024)S(1)}, ...) while((s32[]{:T(128)}, ...), condition=%wide.region_7.8_spmd, body=%wide.region_4.7_spmd.sunk | while | flops 2250236416 | bytes 128203024 | solution.py:110
  89.7 14.1 bitcast_reduce_fusion.2
  103.8 17.7 %fusion.136 = f32[8,2,512]{2,1,0:T(2,128)S(1)} fusion(f32[8,512,2,1024]{3,1,2,0:T(8,128)} %get-tuple-element.535, f32[8,2,512]{2,1,0:T(2,128)S(1)} %get-tuple-element.536, pred[512,1024]{1,0:T(8,128)(4,1)S(1)} %fusion.135), kind=kLoop, calls=%fused_computation.5.clone.1 | loop fusion | flops 33546240 | bytes 34144256 | tf_op jit(solution)/shard_map/while/body/eval_jaxpr/while/body/eval_jaxpr/reduce_sum | solution.py:103
  121.5 14.3 fusion.137
  154.9 15.4 fusion.136
  170.3 16.3 fusion.137
  204.5 16.3 fusion.78
  227.1 17.1 fusion.77
  244.2 48.7 %all-gather.22.cloned.1.call-done = bf16[4608,1024]{1,0:T(8,128)(2,1)} async-done(((bf16[1152,1024]{1,0:T(8,128)(2,1)}), bf16[4608,1024]{1,0:T(8,128)(2,1)}) %all-gather.22.cloned.1.call-update) | async-done | bytes 9437200 | tf_op jit(solution)/shard_map/all_gather | solution.py:229
  292.9 30.5 %multiply_convert_fusion = (bf16[1024,4608]{1,0:T(8,128)(2,1)}, bf16[1024,4608]{1,0:T(8,128)(2,1)}, bf16[1024,4608]{1,0:T(8,128)(2,1)}) fusion(f32[1024,4608]{1,0:T(8,128)} %fusion.77, f32[1024,4608]{1,0:T(8,128)} %fusion.78, bf16[1024,1024]{1,0:T(8,128)(2,1)S(1)} %copy-done.19, bf16[4608,1024]{1,0:T(8,128)(2,1)} %all-gather.22.cloned.1.call-done), kind=kOutput, calls=%fused_computation.59 | convolution fusion | flops 9734455296 | bytes 77594624 | tf_op jit(solution)/shard_map/dot_general | solution.py:68
  323.4 14.2 fusion.79
  337.6 17.1 multiply_reduce_fusion
  375.1 300.6 %while.48 = (s32[]{:T(128)}, f32[1024,8,64]{0,2,1:T(8,128)}, f32[1024,8,64]{0,2,1:T(8,128)}, f32[2,512,8,2,64]{1,0,4,3,2:T(2,128)}, bf16[2,512,8,2,64]{1,4,3,2,0...) while((s32[]{:T(128)}, f32[1024,8,64]{0,2,1:T(8,128)}, ...), condition=%wide.region_12.13_spmd.clone, body=%wide.region_10.12_spmd.clone.sunk | while | flops 5499249152 | bytes 347322624 | solution.py:153
  379.2 14.4 fusion.146
  393.6 16.6 bitcast_add_fusion.5
  410.2 25.3 %fusion.148 = (f32[8,2,512]{2,1,0:T(2,128)S(1)}, f32[8,512,2,1024]{3,1,2,0:T(8,128)}) fusion(f32[8,512,2,1024]{3,1,2,0:T(8,128)} %fusion.146, f32[8,2,512]{2,1,0:T(2,128)S(1)} %dynamic-slice_bitcast_fusion.2, pred[512,1024]{1,0:T(8,128)(4,1)S(1)} %fusion.147, bf16[1024,8,64]{0,2,1:T(8,128)(2,1)S(1)} %get-tuple-element.621, ...), kind=kOutput, calls=%fused_computation.24.clone.1 | convolution fusion | flops 1115676672 | bytes 69795840 | tf_op jit(solution)/shard_map/while/body/eval_jaxpr/while/body/eval_jaxpr/qcrd,kcd->crqk/dot_general | solution.py:128
  435.4 27.8 %fusion.149 = bf16[8,2,512,1024]{3,2,1,0:T(8,128)(2,1)} fusion(f32[8,512,2,1024]{3,1,2,0:T(8,128)} %get-tuple-element.548, f32[8,512,2,1024]{3,1,2,0:T(8,128)} %fusion.146, f32[8,2,512]{2,1,0:T(2,128)S(1)} %get-tuple-element.549, f32[8,2,512]{2,1,0:T(2,128)S(1)} %dynamic-slice_bitcast_fusion.2, pred[512,1024]{1,0:T(8,128)(4,1)S(1)} %fusion.147), kind=kLoop, calls=%fused_computation.26.clone.1 | loop fusion | flops 50331648 | bytes 84475904 | tf_op jit(solution)/shard_map/while/body/eval_jaxpr/while/body/eval_jaxpr/convert_element_type | solution.py:132
  486.5 38.2 %dynamic_update_slice.34 = f32[2,512,8,2,64]{1,0,4,3,2:T(2,128)} dynamic-update-slice(f32[2,512,8,2,64]{1,0,4,3,2:T(2,128)} %get-tuple-element.600, f32[1,512,8,2,64]{1,0,4,3,2:T(1,128)} %copy.118, s32[]{:T(128)S(6)} %copy.137, s32[]{:T(128)} %constant.90.clone.1..sunk.1, s32[]{:T(128)} %constant.90.clone.1..sunk.1, s32[]{:T(128)} %constant.90.clone.1..sunk.1, s32[]{:T(128)} %constant.90.clone.1..sunk.1) | dynamic-update-slice | bytes 4194308 | tf_op jit(solution)/shard_map/while/body/eval_jaxpr/while/body/jit(dynamic_update_index_in_dim)/dynamic_update_slice | solution.py:153
  528.6 14.4 fusion.146
  543.0 17.2 %bitcast_add_fusion.5 = f32[1024,8,64]{0,2,1:T(8,128)} fusion(f32[1024,8,64]{0,2,1:T(8,128)} %get-tuple-element.599, f32[8,512,2,1024]{3,1,2,0:T(8,128)} %fusion.146, f32[8,2,512]{2,1,0:T(2,128)S(1)} %dynamic-slice_bitcast_fusion.2, pred[512,1024]{1,0:T(8,128)(4,1)S(1)} %fusion.147, pred[]{:T(512)S(6)} %compare.3, ...), kind=kOutput, calls=%fused_computation.32.clone.1 | convolution fusion | flops 1108344832 | bytes 39354372 | tf_op jit(solution)/shard_map/while/body/eval_jaxpr/while/body/eval_jaxpr/crqk,qcrd->kcd/dot_general | solution.py:144
  560.2 25.3 %fusion.148 = (f32[8,2,512]{2,1,0:T(2,128)S(1)}, f32[8,512,2,1024]{3,1,2,0:T(8,128)}) fusion(f32[8,512,2,1024]{3,1,2,0:T(8,128)} %fusion.146, f32[8,2,512]{2,1,0:T(2,128)S(1)} %dynamic-slice_bitcast_fusion.2, pred[512,1024]{1,0:T(8,128)(4,1)S(1)} %fusion.147, bf16[1024,8,64]{0,2,1:T(8,128)(2,1)S(1)} %get-tuple-element.621, ...), kind=kOutput, calls=%fused_computation.24.clone.1 | convolution fusion | flops 1115676672 | bytes 69795840 | tf_op jit(solution)/shard_map/while/body/eval_jaxpr/while/body/eval_jaxpr/qcrd,kcd->crqk/dot_general | solution.py:128
  585.5 27.8 %fusion.149 = bf16[8,2,512,1024]{3,2,1,0:T(8,128)(2,1)} fusion(f32[8,512,2,1024]{3,1,2,0:T(8,128)} %get-tuple-element.548, f32[8,512,2,1024]{3,1,2,0:T(8,128)} %fusion.146, f32[8,2,512]{2,1,0:T(2,128)S(1)} %get-tuple-element.549, f32[8,2,512]{2,1,0:T(2,128)S(1)} %dynamic-slice_bitcast_fusion.2, pred[512,1024]{1,0:T(8,128)(4,1)S(1)} %fusion.147), kind=kLoop, calls=%fused_computation.26.clone.1 | loop fusion | flops 50331648 | bytes 84475904 | tf_op jit(solution)/shard_map/while/body/eval_jaxpr/while/body/eval_jaxpr/convert_element_type | solution.py:132
  637.2 38.2 %dynamic_update_slice.34 = f32[2,512,8,2,64]{1,0,4,3,2:T(2,128)} dynamic-update-slice(f32[2,512,8,2,64]{1,0,4,3,2:T(2,128)} %get-tuple-element.600, f32[1,512,8,2,64]{1,0,4,3,2:T(1,128)} %copy.118, s32[]{:T(128)S(6)} %copy.137, s32[]{:T(128)} %constant.90.clone.1..sunk.1, s32[]{:T(128)} %constant.90.clone.1..sunk.1, s32[]{:T(128)} %constant.90.clone.1..sunk.1, s32[]{:T(128)} %constant.90.clone.1..sunk.1) | dynamic-update-slice | bytes 4194308 | tf_op jit(solution)/shard_map/while/body/eval_jaxpr/while/body/jit(dynamic_update_index_in_dim)/dynamic_update_slice | solution.py:153
  711.9 16.3 convolution_convert_fusion.1
  728.3 16.3 convolution_convert_fusion
  744.7 17.2 convolution_convert_fusion.2
  763.2 16.9 add_convert_fusion
  804.8 79.5 %reduce-scatter.16.cloned.1.call-done = bf16[256,4608]{1,0:T(8,128)(2,1)} async-done(((bf16[1024,4608]{1,0:T(8,128)(2,1)}), bf16[256,4608]{1,0:T(8,128)(2,1)}) %reduce-scatter.16.cloned.1.call-update) | async-done | bytes 2359312 | tf_op jit(solution)/shard_map/reduce_scatter | solution.py:265
  884.3 81.1 %reduce-scatter.18.cloned.1.call-done = bf16[256,4608]{1,0:T(8,128)(2,1)} async-done(((bf16[1024,4608]{1,0:T(8,128)(2,1)}), bf16[256,4608]{1,0:T(8,128)(2,1)}) %reduce-scatter.18.cloned.1.call-update) | async-done | bytes 2359312 | tf_op jit(solution)/shard_map/reduce_scatter | solution.py:268
  965.3 80.9 %reduce-scatter.20.cloned.1.call-done = bf16[1152,1024]{1,0:T(8,128)(2,1)} async-done(((bf16[4608,1024]{1,0:T(8,128)(2,1)}), bf16[1152,1024]{1,0:T(8,128)(2,1)}) %reduce-scatter.20.cloned.1.call-update) | async-done | bytes 2359312 | tf_op jit(solution)/shard_map/reduce_scatter | solution.py:271
  1046.3 666.3 %all-reduce.10 = (f32[256]{0:T(256)}, f32[256,1024]{1,0:T(8,128)}, f32[256,512]{1,0:T(8,128)}, f32[256,512]{1,0:T(8,128)}, f32[16]{0:T(128)}, /*index=5*/f32[16]...) all-reduce(f32[256]{0:T(256)S(1)} %get-tuple-element.423, ...), channel_id=1, replica_groups=mesh['rep'=8,'grp'=4] {'rep'}, use_global_device_ids=true, to_apply=%region_18.19 | all-reduce | flops 4325920 | bytes 25956608 | tf_op jit(solution)/shard_map/psum | solution.py:353
  (272 shorter events, 232.0 us)
Async XLA Ops:
  7.2 36.4 %all-gather.12.cloned.1.call-start = ((), (), s32[]{:S(2)}) async-start(), calls=%async_computation.8 | async-start | bytes 1310720 | tf_op jit(solution)/shard_map/all_gather | solution.py:183
  7.9 14.8 copy-start.54
  8.0 14.8 copy-start.55
  8.0 26.2 %copy-start.30 = (s32[1024]{0:T(1024)S(1)}, s32[1024]{0:T(1024)}, u32[]{:S(2)}) copy-start(s32[1024]{0:T(1024)} %param.19) | copy-start | bytes 12292
  8.0 40.1 %all-gather.14.cloned.1.call-start = ((), (), s32[]{:S(2)}) async-start(), calls=%async_computation.9 | async-start | bytes 1310720 | tf_op jit(solution)/shard_map/all_gather | solution.py:184
  8.7 62.9 %all-gather.10.cloned.1.call-start = ((), (), s32[]{:S(2)}) async-start(), calls=%async_computation.7 | async-start | bytes 2621440 | tf_op jit(solution)/shard_map/all_gather | solution.py:182
  9.5 185.8 %all-gather.16.cloned.1.call-start = ((), (), s32[]{:S(2)}) async-start(), calls=%async_computation.10 | async-start | bytes 2621440 | tf_op jit(solution)/shard_map/all_gather | solution.py:187
  10.0 193.1 %all-gather.20.cloned.1.call-start = ((), (), s32[]{:S(2)}) async-start(), calls=%async_computation.12 | async-start | bytes 11796480 | tf_op jit(solution)/shard_map/all_gather | solution.py:228
  10.6 216.4 %all-gather.18.cloned.1.call-start = ((), (), s32[]{:S(2)}) async-start(), calls=%async_computation.11 | async-start | bytes 11796480 | tf_op jit(solution)/shard_map/all_gather | solution.py:227
  11.2 281.7 %all-gather.22.cloned.1.call-start = ((), (), s32[]{:S(2)}) async-start(), calls=%async_computation.13 | async-start | bytes 11796480 | tf_op jit(solution)/shard_map/all_gather | solution.py:229
  12.0 792.8 %reduce-scatter.10.cloned.1.call-start = ((), (), s32[]{:S(2)}) async-start(), calls=%async_computation.15 | async-start | bytes 1310720 | tf_op jit(solution)/shard_map/reduce_scatter | solution.py:337
  22.2 53.6 %copy-start.42 = (f32[64]{0:T(128)}, f32[64]{0:T(128)S(1)}, u32[]{:S(2)}) copy-start(f32[64]{0:T(128)S(1)} %convert_element_type.171) | copy-start | bytes 772
  22.8 23.5 %copy-start.44 = (f32[64]{0:T(128)}, f32[64]{0:T(128)S(1)}, u32[]{:S(2)}) copy-start(f32[64]{0:T(128)S(1)} %convert_element_type.174) | copy-start | bytes 772
  33.5 38.1 %copy-start.36 = (f32[4,1,256]{2,1,0:T(1,128)}, f32[4,1,256]{2,1,0:T(1,128)S(1)}, u32[]{:S(2)}) copy-start(f32[4,1,256]{2,1,0:T(1,128)S(1)} %convert_element_type.212) | copy-start | bytes 12292
  37.6 34.0 %copy-start.6 = (bf16[1024,1024]{0,1:T(8,128)(2,1)}, bf16[1024,1024]{0,1:T(8,128)(2,1)S(1)}, u32[]{:S(2)}) copy-start(bf16[1024,1024]{0,1:T(8,128)(2,1)S(1)} %copy.70) | copy-start | bytes 6291460
  38.1 33.5 %copy-start.38 = (f32[1024]{0:T(1024)}, f32[1024]{0:T(1024)S(1)}, u32[]{:S(2)}) copy-start(f32[1024]{0:T(1024)S(1)} %add_rsqrt_fusion.3) | copy-start | bytes 12292
  43.6 33.9 %copy-start.17 = (f32[1024,32]{0,1:T(8,128)}, f32[1024,32]{0,1:T(8,128)S(1)}, u32[]{:S(2)}) copy-start(f32[1024,32]{0,1:T(8,128)S(1)} %get-tuple-element.411) | copy-start | bytes 393220
  103.8 17.7 %copy-start.8 = (bf16[1024,8,64]{0,2,1:T(8,128)(2,1)S(1)}, bf16[1024,8,64]{0,2,1:T(8,128)(2,1)}, u32[]{:S(2)}) copy-start(bf16[1024,8,64]{0,2,1:T(8,128)(2,1)} %get-tuple-element.579) | copy-start | bytes 3145732 | tf_op jit(solution)/shard_map/while/body/eval_jaxpr/while
  103.8 17.7 %copy-start.21 = (bf16[2,512,8,2,64]{1,4,3,2,0:T(8,128)(2,1)S(1)}, bf16[2,512,8,2,64]{1,4,3,2,0:T(8,128)(2,1)}, u32[]{:S(2)}) copy-start(bf16[2,512,8,2,64]{1,4,3,2,0:T(8,128)(2,1)} %get-tuple-element.562) | copy-start | bytes 6291460 | tf_op jit(solution)/shard_map/while/body/eval_jaxpr/while
  154.9 15.4 copy-start.8
  154.9 15.4 copy-start.21
  220.7 72.1 %copy-start.19 = (bf16[1024,1024]{1,0:T(8,128)(2,1)S(1)}, bf16[1024,1024]{1,0:T(8,128)(2,1)}, u32[]{:S(2)}) copy-start(bf16[1024,1024]{1,0:T(8,128)(2,1)} %param.31) | copy-start | bytes 6291460
  323.4 14.2 copy-start.15
  337.6 17.2 copy-start.16
  375.1 300.7 %copy-start.18 = (f32[1024,32]{0,1:T(8,128)S(1)}, f32[1024,32]{0,1:T(8,128)}, u32[]{:S(2)}) copy-start(f32[1024,32]{0,1:T(8,128)} %copy-done.17) | copy-start | bytes 393220
  375.1 300.6 %copy-start.25 = (f32[1024,32]{0,1:T(8,128)S(1)}, f32[1024,32]{0,1:T(8,128)}, u32[]{:S(2)}) copy-start(f32[1024,32]{0,1:T(8,128)} %get-tuple-element.409) | copy-start | bytes 393220
  682.7 122.1 %reduce-scatter.12.cloned.1.call-start = ((), (), s32[]{:S(2)}) async-start(), calls=%async_computation.16 | async-start | bytes 1310720 | tf_op jit(solution)/shard_map/reduce_scatter | solution.py:340
  686.8 117.9 %reduce-scatter.14.cloned.1.call-start = ((), (), s32[]{:S(2)}) async-start(), calls=%async_computation.17 | async-start | bytes 2621440 | tf_op jit(solution)/shard_map/reduce_scatter | solution.py:349
  693.7 111.1 %reduce-scatter.8.cloned.1.call-start = ((), (), s32[]{:S(2)}) async-start(), calls=%async_computation.14 | async-start | bytes 2621440 | tf_op jit(solution)/shard_map/reduce_scatter | solution.py:334
  711.9 172.4 %reduce-scatter.16.cloned.1.call-start = ((), (), s32[]{:S(2)}) async-start(), calls=%async_computation.18 | async-start | bytes 11796480 | tf_op jit(solution)/shard_map/reduce_scatter | solution.py:265
  728.3 237.1 %reduce-scatter.18.cloned.1.call-start = ((), (), s32[]{:S(2)}) async-start(), calls=%async_computation.19 | async-start | bytes 11796480 | tf_op jit(solution)/shard_map/reduce_scatter | solution.py:268
  744.6 301.6 %reduce-scatter.20.cloned.1.call-start = ((), (), s32[]{:S(2)}) async-start(), calls=%async_computation.20 | async-start | bytes 11796480 | tf_op jit(solution)/shard_map/reduce_scatter | solution.py:271
  (44 other events, 194.3 us)
Sparse Core Ops, SparseCore 0:
  9.6 19.4 all-gather.11
  30.6 16.7 all-gather.13
  49.0 22.5 all-gather.9
  73.0 22.5 all-gather.15
  97.0 64.2 all-gather.19
  162.8 64.2 all-gather.17
  228.6 64.2 all-gather.21
  682.8 24.8 reduce-scatter.9
  710.4 24.8 reduce-scatter.11
  737.7 31.4 reduce-scatter.13
  771.9 31.4 reduce-scatter.7
  805.8 78.4 reduce-scatter.15
  886.9 78.4 reduce-scatter.17
  967.8 78.4 reduce-scatter.19
where the time goes:
time: 1730 us; the launch traced here: 1720 us
  blocking collectives  691 us (40%)
  matrix products  409 us (24%)
  waiting for transfers between devices  321 us (19%)
  local copies, waits for them, and re-layouts  154 us (9%)
  other arithmetic  118 us (7%)
    psum x1, blocking collectives, on_device(): lax.psum((attn_owned[0], attn_owned[1], attn_owned[2], attn_owned[3], att...  666 us
    dynamic_update_slice x4, local copies, waits for them, and re-layouts, attend_back(): lax.scan(one_block, (zero_kv, zero_kv), (query_blocks, grad_blocks, lse_b...  86.6 us
    reduce_scatter x1, waiting for transfers between devices, on_device(): lax.psum_scatter(up_wgrad.astype(jnp.bfloat16), 'grp', scatter_dimension=...  81.1 us
    reduce_scatter x1, waiting for transfers between devices, on_device(): lax.psum_scatter(down_wgrad.astype(jnp.bfloat16), 'grp', scatter_dimensio...  80.9 us
    reduce_scatter x1, waiting for transfers between devices, on_device(): lax.psum_scatter(gate_wgrad.astype(jnp.bfloat16), 'grp', scatter_dimensio...  79.5 us
    dot_general x7, matrix products, back_dot(): lax.dot_general(grad, weight, (((1,), (1,)), ((), ())), preferred_element...  71.5 us
    dot_general x7, matrix products, outer_sum(): lax.dot_general(left, right, (((0,), (0,)), ((), ())), preferred_element_...  64.9 us
    dot_general x4, matrix products, masked_scores(): jnp.einsum('qcrd,kcd->crqk', query_block, keys, preferred_element_type=jn...  56.9 us
  transfers between devices with their start and end apart: 14, of which 6 were waited for; matrix products, arithmetic and copies ran while one was open for 17% of the time, Pallas kernels for 0%

commit v1 on v0

v1 whole, which is shorter than its diff:
```python
import jax
import jax.numpy as jnp
from jax import lax
from jax.experimental import pallas as pl
from jax.experimental.pallas import tpu as pltpu
from jax.sharding import PartitionSpec as P

D = 1024
H = 16
KV = 8
HD = 64
FF = 4608
SEQ = 1024
GRP = 4
CHUNKS = 3
TILE = FF // GRP // CHUNKS
ROWS = D // GRP
PAIR = 2 * TILE
GROUP_Q = H // GRP * HD
GROUP_K = KV // GRP * HD
GROUP_QK = GROUP_Q + GROUP_K
GROUP_ALL = GROUP_QK + GROUP_K
BLOCK = 256

epsilon = 1e-05
theta_base = 1000000.0
score_scale = HD ** (-0.5)
log2_e = 1.4426950408889634
ln_2 = 0.6931471805599453

f32 = jnp.float32
bf16 = jnp.bfloat16


def dot_nn(left, right):
    return lax.dot_general(left, right, (((1,), (0,)), ((), ())), preferred_element_type=f32)


def dot_nt(left, right):
    return lax.dot_general(left, right, (((1,), (1,)), ((), ())), preferred_element_type=f32)


def dot_tn(left, right):
    return lax.dot_general(left, right, (((0,), (0,)), ((), ())), preferred_element_type=f32)


def rms_scale(values):
    return lax.rsqrt(jnp.mean(values * values, axis=-1, keepdims=True) + epsilon)


def norm_back(grad_unit, unit, inverse):
    return inverse * (grad_unit - unit * jnp.mean(grad_unit * unit, axis=-1, keepdims=True))


def block_of(ref, block, rows):
    return ref.at[pl.ds(pl.multiple_of(block * rows, rows), rows)]


def tie(*values):
    return lax.optimization_barrier(values)


def split_two(values):
    high = values.astype(bf16)
    return high, (values - high.astype(f32)).astype(bf16)


def head_mean(values, spread):
    high, rest = split_two(values)
    return dot_nn(high, spread) + dot_nn(rest, spread)


def swap_halves(values):
    width = values.shape[-1]
    lane = lax.broadcasted_iota(jnp.int32, values.shape, 1)
    ahead = pltpu.roll(values, width - 32, 1)
    behind = pltpu.roll(values, 32, 1)
    return jnp.where((lane & 63) < 32, ahead, behind)


def three_lanes(values):
    high = values.astype(bf16).astype(f32)
    rest = values - high
    mid = rest.astype(bf16).astype(f32)
    lane = lax.broadcasted_iota(jnp.int32, values.shape, 1)
    out = jnp.where(lane == 0, high, jnp.where(lane == 1, mid, jnp.where(lane == 2, rest - mid, 0.0)))
    return out.astype(bf16)


def three_ones(rows):
    lane = lax.broadcasted_iota(jnp.int32, (rows, HD), 1)
    return jnp.where(lane < 3, 1.0, 0.0).astype(bf16)


def fill_mask(mask, seg_col, seg_row):
    count = mask.shape[0]
    for start in range(0, count, BLOCK):
        rows = lax.broadcasted_iota(jnp.int32, (BLOCK, count), 0) + start
        cols = lax.broadcasted_iota(jnp.int32, (BLOCK, count), 1)
        keep = (seg_col[start : start + BLOCK, :] == seg_row[...]) & (cols <= rows)
        mask[start : start + BLOCK, :] = jnp.where(keep, 1.0, 0.0)


def place_rows(place_ref, held, pieces, start=0, stop=None):
    own, core, far, far_core = pieces
    g, low = place_ref[0], place_ref[1]
    rows = held.shape[0] // GRP
    quarter = rows // 4
    block_of(held, g, rows)[...] = own
    block_of(held, g ^ 1, rows)[...] = core
    for q, piece in ((2, far), (3, far_core)):
        for k in range(4):
            block_of(held, (g ^ q) * 4 + (low ^ k), quarter)[...] = piece[k]


def pack_kernel(place_ref, w_query, w_key, w_value, w_out, out, quarter):
    for a in range(GRP):
        start = a * GROUP_ALL
        out[:, start : start + GROUP_Q] = w_query[:, a * GROUP_Q : (a + 1) * GROUP_Q]
        out[:, start + GROUP_Q : start + GROUP_QK] = w_key[:, a * GROUP_K : (a + 1) * GROUP_K]
        out[:, start + GROUP_QK : start + GROUP_ALL] = w_value[:, a * GROUP_K : (a + 1) * GROUP_K]
    out[:, GRP * GROUP_ALL :] = w_out[...]
    quarter[...] = block_of(out, place_ref[1], ROWS // 4)[...]


def quarters_kernel(place_ref, gate, up, down, *outs):
    part = ROWS // 4
    for i, out in enumerate(outs):
        for k, weight in ((0, gate), (1, up)):
            for a in range(GRP):
                first = (a * CHUNKS + i) * TILE
                start = (k * GRP + a) * part
                out[start : start + part, :] = weight[:, first : first + TILE]
        out[2 * GRP * part :, :] = down[i * TILE : (i + 1) * TILE, :].T


def first_kernel(tokens, grad, gain, first, first_t, grad_t):
    inputs = tokens[...].astype(f32)
    low = (inputs * rms_scale(inputs) * gain[...]).astype(bf16)
    first[...] = low
    first_t[...] = low.T
    grad_t[...] = grad[...].T


def attend_kernel(
    place_ref, first, own, core, far, far_core, cos, sin, gain, seg_col, seg_row, spread,
    proj, qk_low, v_low, mixed, lse, weights, mask, ones_v,
):
    count = first.shape[0]
    place_rows(place_ref, weights, (own[...], core[...], far, far_core))

    @pl.when(pl.program_id(0) == 0)
    def _():
        fill_mask(mask, seg_col, seg_row)

    @pl.loop(0, count // BLOCK)
    def _(block):
        rows = pl.ds(pl.multiple_of(block * BLOCK, BLOCK), BLOCK)
        values = dot_nn(first[rows, :], weights[...])
        qk = values[:, :GROUP_QK]
        proj[rows, :] = qk
        inverse = lax.rsqrt(head_mean(qk * qk, spread[...]) + epsilon)
        normed = qk * inverse * gain[...]
        cos_rows = jnp.concatenate([cos[rows, :]] * (GROUP_QK // 128), axis=1)
        sin_rows = jnp.concatenate([sin[rows, :]] * (GROUP_QK // 128), axis=1)
        qk_low[rows, :] = (normed * cos_rows + swap_halves(normed) * sin_rows).astype(bf16)
        v_low[rows, :] = values[:, GROUP_QK:].astype(bf16)

    for j in range(GROUP_K // HD):
        ones_v[:, :HD] = v_low[:, j * HD : (j + 1) * HD]
        ones_v[:, HD:] = jnp.ones((count, HD), bf16)
        keys = qk_low[:, GROUP_Q + j * HD : GROUP_Q + (j + 1) * HD]
        for start in range(0, count, BLOCK):
            stop = start + BLOCK
            pair = jnp.concatenate(
                [
                    qk_low[start:stop, (2 * j + i) * HD : (2 * j + i + 1) * HD]
                    for i in range(2)
                ],
                axis=0,
            )
            scores = dot_nt(pair, keys[:stop])
            keep = mask[start:stop, :stop]
            weights_low = (jnp.exp2(scores) * jnp.concatenate([keep, keep], axis=0)).astype(bf16)
            summed = dot_nn(weights_low, ones_v[:stop, :])
            total = summed[:, HD:]
            part = (summed[:, :HD] / total).astype(bf16)
            log_total = jnp.log2(total)
            for i in range(2):
                lanes = slice((2 * j + i) * HD, (2 * j + i + 1) * HD)
                mixed[start:stop, lanes] = part[i * BLOCK : (i + 1) * BLOCK]
                lse[start:stop, lanes] = log_total[i * BLOCK : (i + 1) * BLOCK]


def attend_back_kernel(
    place_ref, residual_low, w_out, weights, first_t, proj, qk_low, v_low, mixed, lse, cos, sin, gain,
    seg_col, seg_row, spread,
    first_low, kept, sent, gain_grad,
    mask, mixed_grad, delta, grads, key_grad, value_grad, low_grads, key_ext, value_ext, first_grad,
):
    count = residual_low.shape[0]
    step = pl.program_id(0)

    @pl.when(step == 0)
    def _():
        fill_mask(mask, seg_col, seg_row)
        first_grad[...] = jnp.zeros_like(first_grad)
        gain_grad[...] = jnp.zeros_like(gain_grad)

    @pl.loop(0, count // BLOCK)
    def _(block):
        rows = pl.ds(pl.multiple_of(block * BLOCK, BLOCK), BLOCK)
        low = dot_nt(residual_low[rows, :], w_out[...]).astype(bf16)
        mixed_grad[rows, :] = low
        product = low.astype(f32) * mixed[rows, :].astype(f32)
        delta[rows, :] = head_mean(product, spread[:GROUP_Q, :GROUP_Q]) * HD

    for j in range(GROUP_K // HD):
        key_ext[:, :HD] = qk_low[:, GROUP_Q + j * HD : GROUP_Q + (j + 1) * HD]
        key_ext[:, HD:] = three_ones(count)
        value_ext[:, :HD] = v_low[:, j * HD : (j + 1) * HD]
        value_ext[:, HD:] = three_ones(count)
        key_grad[...] = jnp.zeros_like(key_grad)
        value_grad[...] = jnp.zeros_like(value_grad)
        for start in range(0, count, BLOCK):
            stop = start + BLOCK
            query_rows, grad_rows = [], []
            for i in range(2):
                lanes = slice((2 * j + i) * HD, (2 * j + i + 1) * HD)
                query_rows.append(
                    jnp.concatenate(
                        [qk_low[start:stop, lanes], three_lanes(-lse[start:stop, lanes])], axis=1
                    )
                )
                grad_rows.append(
                    jnp.concatenate(
                        [mixed_grad[start:stop, lanes], three_lanes(-delta[start:stop, lanes])],
                        axis=1,
                    )
                )
            query_ext = jnp.concatenate(query_rows, axis=0)
            grad_ext = jnp.concatenate(grad_rows, axis=0)
            keep = mask[start:stop, :stop]
            probs = jnp.exp2(dot_nt(query_ext, key_ext[:stop, :])) * jnp.concatenate(
                [keep, keep], axis=0
            )
            score_grad = (probs * dot_nt(grad_ext, value_ext[:stop, :])).astype(bf16)
            query_grad = dot_nn(score_grad, key_ext[:stop, :]) * score_scale
            for i in range(2):
                lanes = slice((2 * j + i) * HD, (2 * j + i + 1) * HD)
                grads[start:stop, lanes] = query_grad[i * BLOCK : (i + 1) * BLOCK, :HD]
            key_grad[:stop, :] += dot_tn(score_grad, query_ext)
            value_grad[:stop, :] += dot_tn(probs.astype(bf16), grad_ext)
        grads[:, GROUP_Q + j * HD : GROUP_Q + (j + 1) * HD] = key_grad[:, :HD] * ln_2
        low_grads[:, GROUP_QK + j * HD : GROUP_QK + (j + 1) * HD] = value_grad[:, :HD].astype(bf16)

    @pl.loop(0, count // BLOCK)
    def _(block):
        rows = pl.ds(pl.multiple_of(block * BLOCK, BLOCK), BLOCK)
        cos_rows = jnp.concatenate([cos[rows, :]] * (GROUP_QK // 128), axis=1)
        sin_rows = jnp.concatenate([sin[rows, :]] * (GROUP_QK // 128), axis=1)
        turned = grads[rows, :]
        turned = turned * cos_rows - swap_halves(turned) * sin_rows
        qk = proj[rows, :]
        inverse = lax.rsqrt(head_mean(qk * qk, spread[...]) + epsilon)
        unit = qk * inverse
        gain_grad[...] += jnp.sum(turned * unit, axis=0, keepdims=True)
        scaled = turned * gain[...]
        back = inverse * (scaled - unit * head_mean(scaled * unit, spread[...]))
        low_grads[rows, :GROUP_QK] = back.astype(bf16)
        first_grad[rows, :] += dot_nt(low_grads[rows, :], weights[...])

    for x in range(2):
        for c in range(2):
            rows = pl.ds(pl.multiple_of((place_ref[0] ^ (2 * x + c)) * ROWS, ROWS), ROWS)
            part = dot_nn(first_t[rows, :], low_grads[...]).astype(bf16)
            if c == 0:
                kept[x] = part
            else:
                sent[x] = part

    @pl.when(step == pl.num_programs(0) - 1)
    def _():
        first_low[...] = first_grad[...].astype(bf16)


def middle_kernel(
    place_ref, mixed0, mixed1, tokens, gain, own, core, far, far_core, residual, second, second_t, w_out
):
    @pl.when(pl.program_id(0) == 0)
    def _():
        place_rows(place_ref, w_out, (own[...], core[...], far, far_core))

    mixed = jnp.concatenate([mixed0[...], mixed1[...]], axis=1)
    total = tokens[...].astype(f32) + dot_nn(mixed, w_out[...])
    residual[...] = total
    low = (total * rms_scale(total) * gain[...]).astype(bf16)
    second[...] = low
    second_t[...] = low.T


def ffn_kernel(
    place_ref, second, second_t, grad, grad_t,
    gate0, gate1, up0, up1, core_gate0, core_gate1, core_up0, core_up1, far, far_core,
    down, core_down,
    out, second_grad, gu_kept, gu_sent, dn_kept, dn_sent,
    w_both, w_down, inner_low, both_low, out_sum, grad_sum,
):
    step = pl.program_id(0)
    g, low = place_ref[0], place_ref[1]
    odd = (g & 1) == 1
    count = second.shape[0]
    block_rows = min(512, count)
    quarter = ROWS // 4
    for j, (gate, up, core_gate, core_up) in enumerate(
        ((gate0, up0, core_gate0, core_up0), (gate1, up1, core_gate1, core_up1))
    ):
        for k, own, core in ((0, gate, core_gate), (1, up, core_up)):
            lanes = slice(k * PAIR + j * TILE, k * PAIR + (j + 1) * TILE)
            w_both[pl.ds(pl.multiple_of(g * ROWS, ROWS), ROWS), lanes] = own[...]
            w_both[pl.ds(pl.multiple_of((g ^ 1) * ROWS, ROWS), ROWS), lanes] = core[...]
            for q, piece in ((2, far), (3, far_core)):
                for part in range(4):
                    start = ((g ^ q) * 4 + (low ^ part)) * quarter
                    rows = pl.ds(pl.multiple_of((k * GRP + 2 * step + j) * quarter, quarter), quarter)
                    w_both[pl.ds(pl.multiple_of(start, quarter), quarter), lanes] = piece[part, rows, :]

    @pl.when(step == 0)
    def _():
        w_down[g] = down[...]
        w_down[g ^ 1] = core_down[...]
        for q, piece in ((2, far), (3, far_core)):
            for part in range(4):
                lanes = pl.ds(pl.multiple_of((low ^ part) * (D // 4), D // 4), D // 4)
                w_down[g ^ q, :, lanes] = piece[part, 2 * ROWS :, :].T
        out_sum[...] = jnp.zeros_like(out_sum)
        grad_sum[...] = jnp.zeros_like(grad_sum)

    @pl.loop(0, count // block_rows)
    def _(block):
        rows = pl.ds(pl.multiple_of(block * block_rows, block_rows), block_rows)
        both = dot_nn(second[rows, :], w_both[...])
        gate = both[:, :PAIR]
        up = both[:, PAIR:]
        downs = w_down[pl.ds(2 * step, 2)].reshape(PAIR, D)
        inner_grad = dot_nt(grad[rows, :], downs)
        sigmoid = jax.nn.sigmoid(gate)
        silu = gate * sigmoid
        inner = (silu * up).astype(bf16)
        inner_low[rows, :] = inner
        both_low[rows, :PAIR] = (inner_grad * up * (sigmoid + silu * (1.0 - sigmoid))).astype(bf16)
        both_low[rows, PAIR:] = (inner_grad * silu).astype(bf16)
        out_sum[rows, :] += dot_nn(inner, downs)
        grad_sum[rows, :] += dot_nt(both_low[rows, :], w_both[...])

    for x in range(2):
        for c in range(2):
            rows = pl.ds(pl.multiple_of((g ^ (2 * x + c)) * ROWS, ROWS), ROWS)
            part = dot_nn(second_t[rows, :], both_low[...]).astype(bf16)
            target = gu_kept if c == 0 else gu_sent
            for k in range(2):
                for j in range(2):
                    start = k * PAIR + j * TILE
                    target[x, k, j] = part[:, start : start + TILE]

    @pl.loop(0, D // ROWS)
    def _(block):
        rows = pl.ds(pl.multiple_of(block * ROWS, ROWS), ROWS)
        part = dot_nn(grad_t[rows, :], inner_low[...]).astype(bf16)
        dn_kept[0, rows, :] = jnp.where(odd, part[:, TILE:], part[:, :TILE])
        dn_sent[0, rows, :] = jnp.where(odd, part[:, :TILE], part[:, TILE:])

    @pl.when(step == 1)
    def _():
        out[...] = out_sum[...].astype(bf16)
        second_grad[...] = grad_sum[...].astype(bf16)


def after_kernel(
    residual, grad, gain, out0, out1, out2, sg0, sg1, sg2, outputs, residual_grad, residual_low, gain_grad
):
    @pl.when(pl.program_id(0) == 0)
    def _():
        gain_grad[...] = jnp.zeros_like(gain_grad)

    total = residual[...]
    outputs[...] = (
        total + (out0[...].astype(f32) + out1[...].astype(f32) + out2[...].astype(f32))
    ).astype(bf16)
    second_grad = sg0[...].astype(f32) + sg1[...].astype(f32) + sg2[...].astype(f32)
    inverse = rms_scale(total)
    unit = total * inverse
    gain_grad[...] += jnp.sum(second_grad * unit, axis=0, keepdims=True)
    back = grad[...].astype(f32) + norm_back(second_grad * gain[...], unit, inverse)
    residual_grad[...] = back
    residual_low[...] = back.astype(bf16)


def last_kernel(tokens, residual_grad, gain, fg0, fg1, input_grad, gain_grad):
    @pl.when(pl.program_id(0) == 0)
    def _():
        gain_grad[...] = jnp.zeros_like(gain_grad)

    inputs = tokens[...].astype(f32)
    first_grad = fg0[...].astype(f32) + fg1[...].astype(f32)
    inverse = rms_scale(inputs)
    unit = inputs * inverse
    gain_grad[...] += jnp.sum(first_grad * unit, axis=0, keepdims=True)
    input_grad[...] = (
        residual_grad[...] + norm_back(first_grad * gain[...], unit, inverse)
    ).astype(bf16)


def finish_kernel(gate, up, down, *refs):
    gate_out, up_out, down_out = refs[-3:]
    gate_out[...] = gate[...].astype(f32)
    up_out[...] = up[...].astype(f32)
    down_out[...] = down[...].astype(f32).T


def split_kernel(block, query, key, value):
    query[...] = block[:, :GROUP_Q].astype(f32)
    key[...] = block[:, GROUP_Q:GROUP_QK].astype(f32)
    value[...] = block[:, GROUP_QK:].astype(f32)


struct = jax.ShapeDtypeStruct


def whole(shape):
    return pl.BlockSpec(
        shape, lambda *at: (0,) * len(shape), pipeline_mode=pl.Buffered(buffer_count=1)
    )


def params(megabytes):
    return pltpu.CompilerParams(
        dimension_semantics=("arbitrary",), vmem_limit_bytes=megabytes * 1024 * 1024
    )


def cost(flops, bytes_accessed):
    return pl.CostEstimate(
        flops=int(flops), bytes_accessed=int(bytes_accessed), transcendentals=0
    )


def rows_spec(width, rows=BLOCK):
    return pl.BlockSpec((rows, width), lambda t, *_: (t, 0))


def lanes_spec(rows, width):
    return pl.BlockSpec((rows, width), lambda t, *_: (0, t))


def pack(place, w_query, w_key, w_value, w_out):
    width = GRP * GROUP_ALL + D
    return pl.pallas_call(
        pack_kernel,
        grid_spec=pltpu.PrefetchScalarGridSpec(
            num_scalar_prefetch=1,
            grid=(1,),
            in_specs=[whole((ROWS, H * HD)), whole((ROWS, KV * HD)), whole((ROWS, KV * HD)), whole((ROWS, D))],
            out_specs=[whole((ROWS, width)), whole((ROWS // 4, width))],
        ),
        out_shape=[struct((ROWS, width), bf16), struct((ROWS // 4, width), bf16)],
        compiler_params=params(60),
        cost_estimate=cost(1e5, 3e6),
        name="pack",
    )(place, w_query, w_key, w_value, w_out)


def quarters(place, w_gate, w_up, w_down):
    part = ROWS // 4
    rows = 2 * GRP * part + D // 4
    return pl.pallas_call(
        quarters_kernel,
        grid_spec=pltpu.PrefetchScalarGridSpec(
            num_scalar_prefetch=1,
            grid=(1,),
            in_specs=[
                pl.BlockSpec((part, FF), lambda t, p: (p[1], 0)),
                pl.BlockSpec((part, FF), lambda t, p: (p[1], 0)),
                pl.BlockSpec((FF // GRP, D // 4), lambda t, p: (0, p[1])),
            ],
            out_specs=[whole((rows, TILE))] * CHUNKS,
        ),
        out_shape=[struct((rows, TILE), bf16)] * CHUNKS,
        compiler_params=params(60),
        cost_estimate=cost(1e5, 4e6),
        name="quarters",
    )(place, w_gate, w_up, w_down)


def first_norm(tokens, grad, gain):
    count = tokens.shape[0]
    return pl.pallas_call(
        first_kernel,
        grid=(count // BLOCK,),
        in_specs=[rows_spec(D), rows_spec(D), whole((1, D))],
        out_specs=[rows_spec(D), lanes_spec(D, BLOCK), lanes_spec(D, BLOCK)],
        out_shape=[struct((count, D), bf16), struct((D, count), bf16), struct((D, count), bf16)],
        compiler_params=params(60),
        cost_estimate=cost(1e7, 1e7),
        name="first_norm",
    )(tokens, grad, gain)


def attend(part, place, first, pieces, cos, sin, gain, seg_col, seg_row, spread):
    count = first.shape[0]
    steps = GRP // 2
    own, core, far, far_core = pieces
    far_spec = pl.BlockSpec((4, ROWS // 4, GROUP_ALL), lambda t, p: (0, 0, part * steps + t))
    own_spec = pl.BlockSpec((ROWS, GROUP_ALL), lambda t, p: (0, part * steps + t))
    return pl.pallas_call(
        attend_kernel,
        grid_spec=pltpu.PrefetchScalarGridSpec(
            num_scalar_prefetch=1,
            grid=(steps,),
            in_specs=[
                whole((count, D)),
                own_spec,
                own_spec,
                far_spec,
                far_spec,
                whole((count, 128)),
                whole((count, 128)),
                whole((1, GROUP_QK)),
                whole((count, 1)),
                whole((1, count)),
                whole((GROUP_QK, GROUP_QK)),
            ],
            out_specs=[
                lanes_spec(count, GROUP_QK),
                lanes_spec(count, GROUP_QK),
                lanes_spec(count, GROUP_K),
                lanes_spec(count, GROUP_Q),
                lanes_spec(count, GROUP_Q),
                lanes_spec(D, GROUP_ALL),
            ],
            scratch_shapes=[
                pltpu.VMEM((count, count), f32),
                pltpu.VMEM((count, 2 * HD), bf16),
            ],
        ),
        out_shape=[
            struct((count, steps * GROUP_QK), f32),
            struct((count, steps * GROUP_QK), bf16),
            struct((count, steps * GROUP_K), bf16),
            struct((count, steps * GROUP_Q), bf16),
            struct((count, steps * GROUP_Q), f32),
            struct((D, steps * GROUP_ALL), bf16),
        ],
        compiler_params=params(60),
        cost_estimate=cost(1e10, 1.2e7),
        name="attend",
    )(place, first, own, core, far, far_core, cos, sin, gain, seg_col, seg_row, spread)


def middle(place, mixed, tokens, gain, pieces):
    count = tokens.shape[0]
    own, core, far, far_core = pieces
    one = pl.Buffered(buffer_count=1)
    own_spec = pl.BlockSpec((ROWS, D), lambda t, p: (0, 2), pipeline_mode=one)
    far_spec = pl.BlockSpec((4, ROWS // 4, D), lambda t, p: (0, 0, 2), pipeline_mode=one)
    return pl.pallas_call(
        middle_kernel,
        grid_spec=pltpu.PrefetchScalarGridSpec(
            num_scalar_prefetch=1,
            grid=(count // BLOCK,),
            in_specs=[
                rows_spec(D // 2),
                rows_spec(D // 2),
                rows_spec(D),
                whole((1, D)),
                own_spec,
                own_spec,
                far_spec,
                far_spec,
            ],
            out_specs=[rows_spec(D), rows_spec(D), lanes_spec(D, BLOCK), whole((D, D))],
        ),
        out_shape=[
            struct((count, D), f32),
            struct((count, D), bf16),
            struct((D, count), bf16),
            struct((D, D), bf16),
        ],
        compiler_params=params(60),
        cost_estimate=cost(2e9, 1.6e7),
        name="middle",
    )(place, *mixed, tokens, gain, own, core, far, far_core)


def ffn(place, second, second_t, grad, grad_t, weights, i):
    count = second.shape[0]
    (gate, up, core_gate, core_up, down, core_down), (far, far_core) = weights
    tile = [
        pl.BlockSpec((ROWS, TILE), lambda t, p, j=j: (0, (2 * t + j) * CHUNKS + i))
        for j in range(2)
    ]
    one = pl.Buffered(buffer_count=1)
    down_spec = pl.BlockSpec((TILE, D), lambda t, p: (i, 0), pipeline_mode=one)
    gu_spec = pl.BlockSpec((2, 2, 2, ROWS, TILE), lambda t, p: (0, 0, t, 0, 0))
    dn_spec = pl.BlockSpec((1, D, TILE), lambda t, p: (t ^ (p[0] >> 1), 0, 0))
    return pl.pallas_call(
        ffn_kernel,
        grid_spec=pltpu.PrefetchScalarGridSpec(
            num_scalar_prefetch=1,
            grid=(2,),
            in_specs=[
                whole((count, D)),
                whole((D, count)),
                whole((count, D)),
                whole((D, count)),
            ]
            + tile * 4
            + [whole(far.shape)] * 2
            + [down_spec] * 2,
            out_specs=[whole((count, D)), whole((count, D)), gu_spec, gu_spec, dn_spec, dn_spec],
            scratch_shapes=[
                pltpu.VMEM((D, 2 * PAIR), bf16),
                pltpu.VMEM((GRP, TILE, D), bf16),
                pltpu.VMEM((count, PAIR), bf16),
                pltpu.VMEM((count, 2 * PAIR), bf16),
                pltpu.VMEM((count, D), f32),
                pltpu.VMEM((count, D), f32),
            ],
        ),
        out_shape=[
            struct((count, D), bf16),
            struct((count, D), bf16),
            struct((2, 2, GRP, ROWS, TILE), bf16),
            struct((2, 2, GRP, ROWS, TILE), bf16),
            struct((2, D, TILE), bf16),
            struct((2, D, TILE), bf16),
        ],
        compiler_params=params(60),
        cost_estimate=cost(2.9e10, 3.6e7),
        name="ffn",
    )(
        place, second, second_t, grad, grad_t,
        gate, gate, up, up, core_gate, core_gate, core_up, core_up,
        far, far_core, down, core_down,
    )


def after_ffn(residual, grad, gain, outs, second_grads):
    count = residual.shape[0]
    return pl.pallas_call(
        after_kernel,
        grid=(count // BLOCK,),
        in_specs=[rows_spec(D), rows_spec(D), whole((1, D))] + [rows_spec(D)] * 6,
        out_specs=[rows_spec(D), rows_spec(D), rows_spec(D), whole((1, D))],
        out_shape=[
            struct((count, D), bf16),
            struct((count, D), f32),
            struct((count, D), bf16),
            struct((1, D), f32),
        ],
        compiler_params=params(60),
        cost_estimate=cost(2e7, 2.4e7),
        name="after_ffn",
    )(residual, grad, gain, *outs, *second_grads)


def attend_back(
    part, place, residual_low, w_out, weights, first_t, proj, qk_low, v_low, mixed, lse, cos, sin,
    gain, seg_col, seg_row, spread,
):
    count = residual_low.shape[0]
    steps = GRP // 2
    step_cols = lambda width, rows=count: pl.BlockSpec((rows, width), lambda t, p: (0, t))
    grad_spec = pl.BlockSpec((2, ROWS, GROUP_ALL), lambda t, p: (0, 0, t))
    return pl.pallas_call(
        attend_back_kernel,
        grid_spec=pltpu.PrefetchScalarGridSpec(
            num_scalar_prefetch=1,
            grid=(steps,),
            in_specs=[
                whole((count, D)),
                pl.BlockSpec((ROWS, D), lambda t, p: (part * steps + t, 0)),
                step_cols(GROUP_ALL, D),
                whole((D, count)),
                step_cols(GROUP_QK),
                step_cols(GROUP_QK),
                step_cols(GROUP_K),
                step_cols(GROUP_Q),
                step_cols(GROUP_Q),
                whole((count, 128)),
                whole((count, 128)),
                whole((1, GROUP_QK)),
                whole((count, 1)),
                whole((1, count)),
                whole((GROUP_QK, GROUP_QK)),
            ],
            out_specs=[whole((count, D)), grad_spec, grad_spec, whole((1, GROUP_QK))],
            scratch_shapes=[
                pltpu.VMEM((count, count), f32),
                pltpu.VMEM((count, GROUP_Q), bf16),
                pltpu.VMEM((count, GROUP_Q), f32),
                pltpu.VMEM((count, GROUP_QK), f32),
                pltpu.VMEM((count, 2 * HD), f32),
                pltpu.VMEM((count, 2 * HD), f32),
                pltpu.VMEM((count, GROUP_ALL), bf16),
                pltpu.VMEM((count, 2 * HD), bf16),
                pltpu.VMEM((count, 2 * HD), bf16),
                pltpu.VMEM((count, D), f32),
            ],
        ),
        out_shape=[
            struct((count, D), bf16),
            struct((2, ROWS, steps * GROUP_ALL), bf16),
            struct((2, ROWS, steps * GROUP_ALL), bf16),
            struct((1, GROUP_QK), f32),
        ],
        compiler_params=params(60),
        cost_estimate=cost(3e10, 2e7),
        name="attend_back",
    )(
        place, residual_low, w_out, weights, first_t, proj, qk_low, v_low, mixed, lse, cos, sin,
        gain, seg_col, seg_row, spread,
    )


def last_norm(tokens, residual_grad, gain, first_grads):
    count = tokens.shape[0]
    return pl.pallas_call(
        last_kernel,
        grid=(count // BLOCK,),
        in_specs=[rows_spec(D), rows_spec(D), whole((1, D)), rows_spec(D), rows_spec(D)],
        out_specs=[rows_spec(D), whole((1, D))],
        out_shape=[struct((count, D), bf16), struct((1, D), f32)],
        compiler_params=params(60),
        cost_estimate=cost(2e7, 1.2e7),
        name="last_norm",
    )(tokens, residual_grad, gain, *first_grads)


def finish(i, total, held):
    both_spec = pl.BlockSpec((ROWS, TILE), lambda t: (0, t * CHUNKS + i))
    any_spec = pl.BlockSpec(memory_space=pl.ANY)
    return pl.pallas_call(
        finish_kernel,
        grid=(GRP,),
        in_specs=[
            pl.BlockSpec((ROWS, TILE), lambda t: (t, 0)),
            pl.BlockSpec((ROWS, TILE), lambda t: (GRP + t, 0)),
            pl.BlockSpec((ROWS, TILE), lambda t: (2 * GRP + t, 0)),
        ]
        + [any_spec] * len(held),
        out_specs=[both_spec, both_spec, pl.BlockSpec((TILE, ROWS), lambda t: (i, t))],
        out_shape=[
            struct((ROWS, FF), f32),
            struct((ROWS, FF), f32),
            struct((FF // GRP, D), f32),
        ],
        input_output_aliases={3 + k: k for k in range(len(held))},
        compiler_params=params(60),
        cost_estimate=cost(1e6, 8e6),
        name="finish",
    )(total, total, total, *held)


def split_sums(halves):
    def one(half, held):
        at = lambda width: pl.BlockSpec((ROWS, width), lambda t: (0, GRP // 2 * half + t))
        return pl.pallas_call(
            lambda block, *refs: split_kernel(block, *refs[-3:]),
            grid=(GRP // 2,),
            in_specs=[lanes_spec(ROWS, GROUP_ALL)]
            + [pl.BlockSpec(memory_space=pl.ANY)] * len(held),
            out_specs=[at(GROUP_Q), at(GROUP_K), at(GROUP_K)],
            out_shape=[
                struct((ROWS, H * HD), f32),
                struct((ROWS, KV * HD), f32),
                struct((ROWS, KV * HD), f32),
            ],
            input_output_aliases={1 + k: k for k in range(len(held))},
            compiler_params=params(60),
            cost_estimate=cost(1e6, 4e6),
            name="split_sums",
        )(halves[half], *held)

    return one(1, one(0, ()))


class Job:
    def __init__(self, stages):
        self.stages, self.done, self.result = stages, False, None
        self.advance(None)

    def advance(self, came):
        try:
            self.wanted = self.stages.send(came)
        except StopIteration as stop:
            self.done, self.wanted, self.result = True, [], stop.value

    def start(self, payloads):
        self.flight = [send(values) for values, (_, send) in zip(payloads, self.wanted)]


def on_device(rep_count):
    core_pairs = [(i, i ^ 1) for i in range(GRP)]
    far_pairs = [(i, i ^ 2) for i in range(GRP)]
    rep_bits = rep_count.bit_length() - 1

    def to_core(values):
        return lax.ppermute(values, "grp", core_pairs)

    def to_far(values):
        return lax.ppermute(values, "grp", far_pairs)

    def by_xor(mask):
        pairs = [(i, i ^ mask) for i in range(rep_count)]
        return lambda values: lax.ppermute(values, "rep", pairs)

    def to_rep(bit):
        return by_xor(1 << bit)

    def ordered(upper, own, other):
        return jnp.concatenate([jnp.where(upper, other, own), jnp.where(upper, own, other)], axis=0)

    def low_sum(terms):
        return sum(term.astype(f32) for term in terms).astype(bf16)

    def half_of(values, upper, axis=0):
        half = values.shape[axis] // 2
        return lax.dynamic_slice_in_dim(values, upper * half, half, axis)

    def reduce_stages(kept, sent, early=()):
        rep = lax.axis_index("rep")
        upper_of = lambda bit: (rep >> bit) & 1
        flat = lambda values: values.reshape(-1, values.shape[-1])
        wide = lambda values: values.reshape(2, -1, values.shape[-1])
        join = lambda parts, axis=0: jnp.concatenate(parts, axis=axis) if len(parts) > 1 else parts[0]
        came = yield [(values, to_core) for values in sent]
        if early:
            both = join(
                [low_sum([wide(mine), wide(other)]) for mine, other in zip(kept, came)], axis=1
            )
            terms = [both]
            for bit in early:
                upper = upper_of(bit)
                away = low_sum([half_of(term, 1 - upper, 1) for term in terms])
                terms = [half_of(term, upper, 1) for term in terms]
                terms += yield [(away, to_rep(bit))]
            away = low_sum([term[1] for term in terms])
            terms = [term[0] for term in terms]
        else:
            away = join(
                [low_sum([flat(mine[1]), flat(other[1])]) for mine, other in zip(kept, came)]
            )
            terms = [
                join([flat(values[0]) for values in kept]),
                join([flat(values[0]) for values in came]),
            ]
        terms += yield [(away, to_far)]
        late = [bit for bit in range(rep_bits) if bit not in early]
        for bit in late:
            upper = upper_of(bit)
            away = low_sum([half_of(term, 1 - upper) for term in terms])
            terms = [half_of(term, upper) for term in terms]
            terms += yield [(away, to_rep(bit))]
        total = low_sum(terms)
        for bit in reversed(list(early) + late):
            (got,) = yield [(total, to_rep(bit))]
            total = ordered(upper_of(bit) == 1, total, got)
        return total

    def small_stages(values):
        for send in [to_core, to_far] + [to_rep(bit) for bit in range(rep_bits)]:
            (got,) = yield [(values, send)]
            values = values + got
        return values

    def beside(run, inputs, starting, ending):
        starting = [job for job in starting if not job.done]
        ending = [job for job in ending if not job.done]
        payloads = [[values for values, _ in job.wanted] for job in starting]
        inputs, payloads = tie(tuple(inputs), payloads)
        for job, group in zip(starting, payloads):
            job.start(group)
        outs = run(*inputs)
        outs, came = tie(outs, [job.flight for job in ending])
        for job, group in zip(ending, came):
            job.advance(group)
        return outs

    def finish_jobs(jobs):
        while not all(job.done for job in jobs):
            left = [job for job in jobs if not job.done]
            payloads = tie(*[[values for values, _ in job.wanted] for job in left])
            for job, group in zip(left, payloads):
                job.start(group)
            for job, group in zip(left, tie(*[job.flight for job in left])):
                job.advance(group)
        return [job.result for job in jobs]

    def body(
        tokens, segments, attn_gain, w_query, w_key, w_value, query_gain, key_gain, w_out, ffn_gain,
        w_gate, w_up, w_down, out_grad,
    ):
        count = tokens.shape[0]
        g = lax.axis_index("grp").astype(jnp.int32)
        low = (lax.axis_index("rep") & 3).astype(jnp.int32)
        place = jnp.stack([g, low])

        to_y, to_z = to_rep(0), to_rep(1)

        def spread_one(quarter):
            return to_y(quarter), to_z(quarter)

        def spread_two(by_y, by_z):
            half = by_y.shape[0] // 2
            return to_z(by_y[:half]), to_y(by_z[half:])

        def far_of(quarter, by_y, by_z, first_half, second_half):
            return jnp.stack(
                [quarter, by_y, by_z, jnp.concatenate([first_half, second_half], axis=0)]
            )

        gains = jnp.concatenate([attn_gain, ffn_gain, query_gain, key_gain, jnp.zeros((96,), bf16)])
        own_attn, q_attn = pack(place, w_query, w_key, w_value, w_out)

        given, q_attn = tie((place, w_gate, w_up, w_down, segments), q_attn)
        x_attn = to_far(q_attn)
        q_ffn = quarters(*given[:4])
        gains = lax.all_gather(gains, "grp", axis=0, tiled=False).astype(f32)
        attn_full = gains[:, :ROWS].reshape(1, D)
        ffn_full = gains[:, ROWS : 2 * ROWS].reshape(1, D)
        query_full = gains[:, 2 * ROWS : 2 * ROWS + 16].reshape(1, HD)
        key_full = gains[:, 2 * ROWS + 16 : 2 * ROWS + 32].reshape(1, HD)
        x_attn, q_ffn, attn_full, segments = tie(x_attn, q_ffn, attn_full, given[4])

        yz_attn, x0 = spread_one(x_attn), to_far(q_ffn[0])
        core_attn = to_core(own_attn)
        first, first_t, grad_t = first_norm(tokens, out_grad, attn_full)
        yz_attn, x0, core_attn, first, segments = tie(yz_attn, x0, core_attn, first, segments)

        two_attn, x1 = spread_two(*yz_attn), to_far(q_ffn[1])
        places = jnp.arange(count, dtype=jnp.int32)
        seg_col = segments.reshape(count, 1)
        seg_row = segments.reshape(1, count)
        keep = (seg_col == seg_row) & (places[None, :] <= places[:, None])
        position = (jnp.sum(keep.astype(jnp.int32), axis=1) - 1).astype(f32)
        freqs = theta_base ** (-(2.0 * jnp.arange(HD // 2, dtype=f32)) / HD)
        angles = position[:, None] * freqs[None, :]
        cos, sin = jnp.cos(angles), jnp.sin(angles)
        cos = jnp.concatenate([cos, cos, cos, cos], axis=1)
        sin = jnp.concatenate([-sin, sin, -sin, sin], axis=1)
        lane = jnp.arange(GROUP_QK, dtype=jnp.int32) // HD
        spread = jnp.where(lane[:, None] == lane[None, :], 1.0 / HD, 0.0).astype(bf16)
        head_gain = jnp.concatenate([query_full] * (H // GRP) + [key_full] * (KV // GRP), axis=1)
        fold = jnp.where(jnp.arange(GROUP_QK) < GROUP_Q, score_scale * log2_e, 1.0)[None, :]
        two_attn, x1, cos, sin, spread, head_gain = tie(two_attn, x1, cos, sin, spread, head_gain)

        far_attn = far_of(x_attn, *yz_attn, *two_attn)
        far_core_attn = to_core(far_attn)
        attn_pieces = (own_attn, core_attn, far_attn, far_core_attn)
        inputs = (place, first, attn_pieces, cos, sin, head_gain * fold, seg_col, seg_row, spread)
        inputs, x0, x1, q2 = tie(inputs, x0, x1, q_ffn[2])
        yz0, x2 = spread_one(x0), to_far(q2)
        saved0, inputs, yz0, x1, x2, owns = tie(
            attend(0, *inputs), inputs, yz0, x1, x2, [w_gate, w_up, w_down]
        )
        two0, yz1, yz2 = spread_two(*yz0), spread_one(x1), spread_one(x2)
        cores = [to_core(values) for values in owns]
        saved1, two0, yz1, yz2, cores = tie(attend(1, *inputs), two0, yz1, yz2, cores)
        far0 = far_of(x0, *yz0, *two0)
        mixed = (saved0[3], saved1[3])
        far0, yz1, yz2, mixed = tie(far0, yz1, yz2, mixed)
        two1, two2 = spread_two(*yz1), spread_two(*yz2)
        far_core0 = to_core(far0)
        middle_out, far_core0, two1, two2 = tie(
            middle(place, mixed, tokens, ffn_full, attn_pieces), far_core0, two1, two2
        )
        residual, second, second_t, out_weights = middle_out
        far1, far2 = far_of(x1, *yz1, *two1), far_of(x2, *yz2, *two2)
        second, far1, far2 = tie(second, far1, far2)
        core_gate, core_up, core_down = cores
        near = (w_gate, w_up, core_gate, core_up, w_down, core_down)
        fars = [(far0, far_core0), None, None]

        outs, second_grads, jobs = [], [], []
        for i in range(CHUNKS):
            (out, second_grad, gu_kept, gu_sent, dn_kept, dn_sent) = beside(
                lambda *given, i=i: ffn(*given, i),
                (place, second, second_t, out_grad, grad_t, (near, fars[i])),
                jobs,
                jobs,
            )
            if i == 0:
                out, *far_cores = tie(out, to_core(far1), to_core(far2))
                fars[1:] = [(far1, far_cores[0]), (far2, far_cores[1])]
            outs.append(out)
            second_grads.append(second_grad)
            early = (1,) if i == CHUNKS - 1 else ()
            jobs.append(Job(reduce_stages([gu_kept, dn_kept], [gu_sent, dn_sent], early)))

        outputs, residual_grad, residual_low, ffn_gain_grad = beside(
            after_ffn, (residual, out_grad, ffn_full, outs, second_grads), jobs[2:], jobs[2:]
        )

        def out_back(mixed, residual_low):
            wgrad = dot_tn(jnp.concatenate(mixed, axis=1), residual_low)
            wgrad = wgrad.astype(bf16).reshape(GRP, ROWS, D)
            at = lambda q: lax.dynamic_slice_in_dim(wgrad, g ^ q, 1, 0)
            return jnp.concatenate([at(0), at(2)], axis=0), jnp.concatenate([at(1), at(3)], axis=0)

        out_kept, out_sent = out_back(mixed, residual_low)
        jobs.append(Job(reduce_stages([out_kept], [out_sent])))

        first_grads, head_grads = [], []
        for part, saved in enumerate((saved0, saved1)):
            first_grad, kept, sent, head_grad = beside(
                lambda *given, part=part: attend_back(part, *given),
                (
                    place, residual_low, out_weights, saved[5], first_t, *saved[:5],
                    cos, sin, head_gain, seg_col, seg_row, spread,
                ),
                jobs,
                jobs,
            )
            first_grads.append(first_grad)
            head_grads.append(head_grad)
            jobs.append(Job(reduce_stages([kept], [sent])))
        input_grad, attn_gain_grad = beside(
            last_norm, (tokens, residual_grad, attn_full, first_grads), jobs, jobs
        )

        head_grad = (head_grads[0] + head_grads[1]).reshape(GROUP_QK // HD, HD)
        small = jnp.concatenate(
            [
                attn_gain_grad[0],
                ffn_gain_grad[0],
                jnp.sum(head_grad[: GROUP_Q // HD], axis=0),
                jnp.sum(head_grad[GROUP_Q // HD :], axis=0),
            ]
        )
        jobs.append(Job(small_stages(small.reshape(1, -1))))
        sum0, sum1, sum2, out_sum, attn0, attn1, small = finish_jobs(jobs)
        mine = lambda start, size: lax.dynamic_slice_in_dim(small[0], start + g * size, size, 0)
        held = ()
        for i, total in enumerate((sum0, sum1, sum2)):
            held = finish(i, total, held)
        gate_grad, up_grad, down_grad = held
        query_grad, key_grad, value_grad = split_sums((attn0, attn1))
        return (
            outputs,
            input_grad,
            mine(0, ROWS),
            query_grad,
            key_grad,
            value_grad,
            mine(2 * D, HD // GRP),
            mine(2 * D + HD, HD // GRP),
            out_sum.astype(f32),
            mine(D, ROWS),
            gate_grad,
            up_grad,
            down_grad,
        )

    return body


def solution(mesh):
    tokens_spec, weight_spec, vector_spec = P(("rep", "grp"), None), P("grp", None), P("grp")
    return jax.shard_map(
        on_device(mesh.shape["rep"]),
        mesh=mesh,
        in_specs=(
            tokens_spec,
            P(("rep", "grp")),
            vector_spec,
            weight_spec,
            weight_spec,
            weight_spec,
            vector_spec,
            vector_spec,
            weight_spec,
            vector_spec,
            weight_spec,
            weight_spec,
            weight_spec,
            tokens_spec,
        ),
        out_specs=(
            tokens_spec,
            tokens_spec,
            vector_spec,
            weight_spec,
            weight_spec,
            weight_spec,
            vector_spec,
            vector_spec,
            weight_spec,
            vector_spec,
            weight_spec,
            weight_spec,
            weight_spec,
        ),
        check_vma=False,
    )
```

time: 1730 us -> 790 us (0.46)
  blocking collectives: 691 us -> 7.33 us
  matrix products: 409 us -> 2.37 us
  Pallas kernels: 0 us -> 318 us
  waiting for transfers between devices: 321 us -> 198 us
  local copies, waits for them, and re-layouts: 154 us -> 43.3 us
  starting transfers between devices: 0.55 us -> 79.9 us
    psum x1 -> x0, blocking collectives: 666 us -> none  [on_device(): lax.psum((attn_owned[0], attn_owned[1], attn_owned[2], attn_owned[3], att...]
    dot_general x35 -> x1, matrix products: 409 us -> 2.37 us  [dot_tn(): lax.dot_general(left, right, (((0,), (0,)), ((), ())), preferred_element_...]
    pallas_call x0 -> x18, Pallas kernels: none -> 318 us  [the longest x3 134 us: ffn(): pl.pallas_call(ffn_kernel, grid_spec=pltpu.PrefetchScalarGridSpec(num_sca...]
    reduce_scatter x7 -> x0, waiting for transfers between devices: 242 us -> none  [the longest x1 81.1 us: on_device(): lax.psum_scatter(up_wgrad.astype(jnp.bfloat16), 'grp', scatter_dimension=...]
    ppermute x0 -> x84, waiting for transfers between devices: none -> 198 us  [the longest x55 170 us: by_xor(): return lambda values: lax.ppermute(values, 'rep', pairs)]
    dynamic_update_slice x4 -> x0, local copies, waits for them, and re-layouts: 86.6 us -> none  [attend_back(): lax.scan(one_block, (zero_kv, zero_kv), (query_blocks, grad_blocks, lse_b...]
    ppermute x0 -> x84, starting transfers between devices: none -> 79.9 us  [the longest x55 63.3 us: by_xor(): return lambda values: lax.ppermute(values, 'rep', pairs)]
    all_gather x7 -> x0, waiting for transfers between devices: 75.1 us -> none  [the longest x1 48.7 us: on_device(): lax.all_gather(w_down, 'grp', axis=0, tiled=True)]
  transfers between devices with their start and end apart: 14 -> 84, of which waited for: 6 -> 29; matrix products, arithmetic and copies ran while one was open for 17% -> 8% of each run, Pallas kernels for 0% -> 40%
where the time goes in v1:
time: 790 us; the launch traced here: 779 us
  Pallas kernels  318 us (40%)
  waiting for transfers between devices  198 us (25%)
  other arithmetic  128 us (16%)
  starting transfers between devices  79.9 us (10%)
  local copies, waits for them, and re-layouts  43.3 us (5%)
    ppermute x55, waiting for transfers between devices, by_xor(): return lambda values: lax.ppermute(values, 'rep', pairs)  170 us
    pallas_call x3, Pallas kernels, ffn(): pl.pallas_call(ffn_kernel, grid_spec=pltpu.PrefetchScalarGridSpec(num_sca...  134 us
    pallas_call x2, Pallas kernels, attend_back(): pl.pallas_call(attend_back_kernel, grid_spec=pltpu.PrefetchScalarGridSpec...  85.8 us
    convert_element_type x33, other arithmetic, low_sum(): return sum((term.astype(f32) for term in terms)).astype(bf16)  72.1 us
    ppermute x55, starting transfers between devices, by_xor(): return lambda values: lax.ppermute(values, 'rep', pairs)  63.3 us
    pallas_call x2, Pallas kernels, attend(): pl.pallas_call(attend_kernel, grid_spec=pltpu.PrefetchScalarGridSpec(num_...  40.2 us
    ppermute x11, waiting for transfers between devices, to_far(): return lax.ppermute(values, 'grp', far_pairs)  25.2 us
  transfers between devices with their start and end apart: 84, of which 29 were waited for; matrix products, arithmetic and copies ran while one was open for 8% of the time, Pallas kernels for 40%

profile of v1, /device:TPU:0, one launch (start us, length us, event | category | flops | bytes accessed | tf_op | source)
XLA Modules:
  0.0 779.0 jit_solution(10602717224399895465)
XLA Ops:
  11.3 7.3 all-gather.1
  26.4 5.6 first_norm.1
  59.7 20.0 %attend.2 = (f32[1024,768]{1,0:T(8,128)}, bf16[1024,768]{1,0:T(8,128)(2,1)}, bf16[1024,256]{1,0:T(8,128)(2,1)}, bf16[1024,512]{1,0:T(8,128)(2,1)}, f32[1024,512]{1,0:T(8,128)}, /*index=5*/bf16[1024,1024]{1,0:T(8,128)(2,1)}) custom-call(s32[2]{0:T(128)} %pad_add_fusion.place_ref, bf16[1024,1024]{1,0:T(8,128)(2,1)} %get-tuple-element.462.first, ...), custom_call_target="tpu_custom_call" | custom-call | flops 10000000000 | bytes 12000000 | tf_op jit(solution)/shard_map/attend/pallas_call | solution.py:515
  83.5 7.3 collective-permute-done.13
  94.7 11.3 %collective-permute-done.15 = bf16[768,384]{1,0:T(8,128)(2,1)S(1)} collective-permute-done((bf16[768,384]{1,0:T(8,128)(2,1)}, bf16[768,384]{1,0:T(8,128)(2,1)S(1)}, u32[]{:S(2)}, u32[]{:S(2)}) %collective-permute-start.15) | collective-permute-done | bytes 589856 | tf_op jit(solution)/shard_map/ppermute | solution.py:816
  108.4 20.2 %attend.3 = (f32[1024,768]{1,0:T(8,128)}, bf16[1024,768]{1,0:T(8,128)(2,1)}, bf16[1024,256]{1,0:T(8,128)(2,1)}, bf16[1024,512]{1,0:T(8,128)(2,1)}, f32[1024,512]{1,0:T(8,128)}, /*index=5*/bf16[1024,1024]{1,0:T(8,128)(2,1)}) custom-call(s32[2]{0:T(128)} %pad_add_fusion.place_ref, bf16[1024,1024]{1,0:T(8,128)(2,1)} %get-tuple-element.462.first, ...), custom_call_target="tpu_custom_call" | custom-call | flops 10000000000 | bytes 12000000 | tf_op jit(solution)/shard_map/attend/pallas_call | solution.py:515
  139.2 9.6 %middle.1 = (f32[1024,1024]{1,0:T(8,128)}, bf16[1024,1024]{1,0:T(8,128)(2,1)}, bf16[1024,1024]{1,0:T(8,128)(2,1)}, bf16[1024,1024]{1,0:T(8,128)(2,1)}) custom-call(s32[2]{0:T(128)} %pad_add_fusion.place_ref, bf16[1024,512]{1,0:T(8,128)(2,1)} %get-tuple-element.635.mixed0.mixed, bf16[1024,512]{1,0:T(8,128)(2,1)} %get-tuple-element.670.mixed1.mixed, ...), custom_call_target="tpu_custom_call" | custom-call | flops 2000000000 | bytes 16000000 | tf_op jit(solution)/shard_map/middle/pallas_call | solution.py:566
  156.7 44.6 %ffn.3 = (bf16[1024,1024]{1,0:T(8,128)(2,1)}, bf16[1024,1024]{1,0:T(8,128)(2,1)}, bf16[2,2,4,256,384]{4,3,2,1,0:T(8,128)(2,1)}, bf16[2,2,4,256,384]{4,3,2,1,0:T(...) custom-call(s32[2]{0:T(128)} %pad_add_fusion.place_ref, ...), custom_call_target="tpu_custom_call" | custom-call | flops 28999999488 | bytes 36000000 | tf_op jit(solution)/shard_map/ffn/pallas_call | solution.py:606
  201.9 45.0 %ffn.4 = (bf16[1024,1024]{1,0:T(8,128)(2,1)}, bf16[1024,1024]{1,0:T(8,128)(2,1)}, bf16[2,2,4,256,384]{4,3,2,1,0:T(8,128)(2,1)}, bf16[2,2,4,256,384]{4,3,2,1,0:T(...) custom-call(s32[2]{0:T(128)} %pad_add_fusion.place_ref, ...), custom_call_target="tpu_custom_call" | custom-call | flops 28999999488 | bytes 36000000 | tf_op jit(solution)/shard_map/ffn/pallas_call | solution.py:606
  253.0 44.6 %ffn.5 = (bf16[1024,1024]{1,0:T(8,128)(2,1)}, bf16[1024,1024]{1,0:T(8,128)(2,1)}, bf16[2,2,4,256,384]{4,3,2,1,0:T(8,128)(2,1)}, bf16[2,2,4,256,384]{4,3,2,1,0:T(...) custom-call(s32[2]{0:T(128)} %pad_add_fusion.place_ref, ...), custom_call_target="tpu_custom_call" | custom-call | flops 28999999488 | bytes 36000000 | tf_op jit(solution)/shard_map/ffn/pallas_call | solution.py:606
  297.6 8.4 %collective-permute-done.30 = bf16[3072,384]{1,0:T(8,128)(2,1)} collective-permute-done((bf16[3072,384]{1,0:T(8,128)(2,1)}, bf16[3072,384]{1,0:T(8,128)(2,1)}, u32[]{:S(2)}, u32[]{:S(2)}) %collective-permute-start.30) | collective-permute-done | bytes 2359328 | tf_op jit(solution)/shard_map/ppermute | solution.py:812
  317.1 11.0 %after_ffn.1 = (bf16[1024,1024]{1,0:T(8,128)(2,1)}, f32[1024,1024]{1,0:T(8,128)}, bf16[1024,1024]{1,0:T(8,128)(2,1)}, f32[1,1024]{1,0:T(1,128)}) custom-call(f32[1024,1024]{1,0:T(8,128)} %get-tuple-element.593.residual, bf16[1024,1024]{1,0:T(8,128)(2,1)} %grad.5, f32[1,1024]{1,0:T(1,128)} %bitcast.218, bf16[1024,1024]{1,0:T(8,128)(2,1)} %get-tuple-element.596.out0, ...), custom_call_target="tpu_custom_call" | custom-call | flops 20000000 | bytes 24000000 | tf_op jit(solution)/shard_map/after_ffn/pallas_call | solution.py:650
  330.3 4.6 add_convert_fusion.6
  350.6 9.9 %fusion.1 = (bf16[2,1536,384]{2,1,0:T(8,128)(2,1)}, bf16[2,1536,384]{2,1,0:T(8,128)(2,1)}) fusion(s32[]{:T(128)S(6)} %select_n.429, bf16[2,2048,384]{2,1,0:T(8,128)(2,1)S(1)} %bitcast.190, bf16[2,1024,384]{2,1,0:T(8,128)(2,1)S(1)} %add_convert_fusion.1, s32[]{:T(128)S(6)} %select_n.422), kind=kLoop, calls=%fused_computation.43 | loop fusion | flops 9437184 | bytes 9437192 | tf_op jit(solution)/shard_map/concatenate | solution.py:836
  364.1 42.7 %attend_back.2 = (bf16[1024,1024]{1,0:T(8,128)(2,1)}, bf16[2,256,1024]{2,1,0:T(8,128)(2,1)}, bf16[2,256,1024]{2,1,0:T(8,128)(2,1)}, f32[1,384]{1,0:T(1,128)}) custom-call(s32[2]{0:T(128)} %pad_add_fusion.place_ref, bf16[1024,1024]{1,0:T(8,128)(2,1)} %get-tuple-element.663.residual_low, bf16[1024,1024]{1,0:T(8,128)(2,1)} %get-tuple-element.664.w_out, ...), custom_call_target="tpu_custom_call" | custom-call | flops 30000001024 | bytes 20000000 | tf_op jit(solution)/shard_map/attend_back/pallas_call | solution.py:675
  409.4 7.2 collective-permute-done.36
  425.7 4.7 add_convert_fusion.5
  435.2 43.1 %attend_back.3 = (bf16[1024,1024]{1,0:T(8,128)(2,1)}, bf16[2,256,1024]{2,1,0:T(8,128)(2,1)}, bf16[2,256,1024]{2,1,0:T(8,128)(2,1)}, f32[1,384]{1,0:T(1,128)}) custom-call(s32[2]{0:T(128)} %pad_add_fusion.place_ref, bf16[1024,1024]{1,0:T(8,128)(2,1)} %get-tuple-element.663.residual_low, bf16[1024,1024]{1,0:T(8,128)(2,1)} %get-tuple-element.664.w_out, ...), custom_call_target="tpu_custom_call" | custom-call | flops 30000001024 | bytes 20000000 | tf_op jit(solution)/shard_map/attend_back/pallas_call | solution.py:675
  481.3 4.3 add_convert_fusion.9
  497.7 17.8 %collective-permute-done.47 = bf16[128,1024]{1,0:T(8,128)(2,1)S(1)} collective-permute-done((bf16[128,1024]{1,0:T(8,128)(2,1)S(1)}, bf16[128,1024]{1,0:T(8,128)(2,1)S(1)}, u32[]{:S(2)}, u32[]{:S(2)}) %collective-permute-start.47) | collective-permute-done | bytes 262176 | tf_op jit(solution)/shard_map/ppermute | solution.py:816
  522.8 6.8 last_norm.1
  556.6 4.6 collective-permute-done.54
  561.2 15.8 %collective-permute-done.50 = bf16[384,384]{1,0:T(8,128)(2,1)} collective-permute-done((bf16[384,384]{1,0:T(8,128)(2,1)S(1)}, bf16[384,384]{1,0:T(8,128)(2,1)}, u32[]{:S(2)}, u32[]{:S(2)}) %collective-permute-start.50) | collective-permute-done | bytes 294944 | tf_op jit(solution)/shard_map/ppermute | solution.py:816
  577.0 6.3 collective-permute-done.51
  583.3 6.1 collective-permute-done.52
  608.7 21.8 %collective-permute-done.60 = bf16[32,1024]{1,0:T(8,128)(2,1)} collective-permute-done((bf16[32,1024]{1,0:T(8,128)(2,1)S(1)}, bf16[32,1024]{1,0:T(8,128)(2,1)}, u32[]{:S(2)}, u32[]{:S(2)}) %collective-permute-start.60) | collective-permute-done | bytes 65568 | tf_op jit(solution)/shard_map/ppermute | solution.py:816
  630.6 5.0 collective-permute-done.61
  650.1 33.5 %collective-permute-done.70 = f32[1,2176]{1,0:T(1,128)S(1)} collective-permute-done((f32[1,2176]{1,0:T(1,128)S(1)}, f32[1,2176]{1,0:T(1,128)S(1)}, u32[]{:S(2)}, u32[]{:S(2)}) %collective-permute-start.70) | collective-permute-done | bytes 8736 | tf_op jit(solution)/shard_map/ppermute | solution.py:816
  709.5 21.1 %collective-permute-done.76 = f32[1,2176]{1,0:T(1,128)S(1)} collective-permute-done((f32[1,2176]{1,0:T(1,128)S(1)}, f32[1,2176]{1,0:T(1,128)S(1)}, u32[]{:S(2)}, u32[]{:S(2)}) %collective-permute-start.76) | collective-permute-done | bytes 8736 | tf_op jit(solution)/shard_map/ppermute | solution.py:816
  732.4 4.7 finish.3
  751.5 4.5 finish.4
  756.0 4.5 finish.5
  (475 shorter events, 272.6 us)
Async XLA Ops:
  79.8 48.9 %collective-permute-start.18 = (bf16[256,4608]{1,0:T(8,128)(2,1)}, bf16[256,4608]{1,0:T(8,128)(2,1)}, u32[]{:S(2)}, u32[]{:S(2)}) collective-permute-start(bf16[256,4608]{1,0:T(8,128)(2,1)} %gate1.2), channel_id=1, source_target_pairs={{0,1},{1,0},{2,3},{3,2},{4,5},{5,4},{6,7},{7,6},{8,9},{9,8},{10,11... | collective-permute-start | bytes 7077896 | tf_op jit(solution)/shard_map/ppermute | solution.py:809
  79.9 48.8 %collective-permute-start.19 = (bf16[256,4608]{1,0:T(8,128)(2,1)}, bf16[256,4608]{1,0:T(8,128)(2,1)}, u32[]{:S(2)}, u32[]{:S(2)}) collective-permute-start(bf16[256,4608]{1,0:T(8,128)(2,1)} %up1.2), channel_id=1, source_target_pairs={{0,1},{1,0},{2,3},{3,2},{4,5},{5,4},{6,7},{7,6},{8,9},{9,8},{10,11... | collective-permute-start | bytes 7077896 | tf_op jit(solution)/shard_map/ppermute | solution.py:809
  80.4 48.3 %collective-permute-start.20 = (bf16[1152,1024]{1,0:T(8,128)(2,1)}, bf16[1152,1024]{1,0:T(8,128)(2,1)}, u32[]{:S(2)}, u32[]{:S(2)}) collective-permute-start(bf16[1152,1024]{1,0:T(8,128)(2,1)} %down.3), channel_id=1, source_target_pairs={{0,1},{1,0},{2,3},{3,2},{4,5},{5,4},{6,7},{7,6},{8,9},{9,8},{10,11... | collective-permute-start | bytes 7077896 | tf_op jit(solution)/shard_map/ppermute | solution.py:809
  156.1 45.2 %collective-permute-start.26 = (bf16[4,768,384]{2,1,0:T(8,128)(2,1)}, bf16[4,768,384]{2,1,0:T(8,128)(2,1)}, u32[]{:S(2)}, u32[]{:S(2)}) collective-permute-start(bf16[4,768,384]{2,1,0:T(8,128)(2,1)} %pad_maximum_fusion.1.far), channel_id=1, source_target_pairs={{0,1},{1,0},{2,3},{3,2},{4,5},{5,4},{6,7},{7,6},{8,9},{9,8},{10,11... | collective-permute-start | bytes 7077896 | tf_op jit(solution)/shard_map/ppermute | solution.py:809
  156.2 45.2 %collective-permute-start.27 = (bf16[4,768,384]{2,1,0:T(8,128)(2,1)S(1)}, bf16[4,768,384]{2,1,0:T(8,128)(2,1)}, u32[]{:S(2)}, u32[]{:S(2)}) collective-permute-start(bf16[4,768,384]{2,1,0:T(8,128)(2,1)S(1)} %pad_maximum_fusion.2.far), channel_id=1, source_target_pairs={{0,1},{1,0},{2,3},{3,2},{4,5},{5,4},{6,7},{7,6},{8,9},{9,8},{10,11... | collective-permute-start | bytes 7077896 | tf_op jit(solution)/shard_map/ppermute | solution.py:809
  201.4 45.6 %collective-permute-start.28 = (bf16[2,2,4,256,384]{4,3,2,1,0:T(8,128)(2,1)}, bf16[2,2,4,256,384]{4,3,2,1,0:T(8,128)(2,1)}, u32[]{:S(2)}, u32[]{:S(2)}) collective-permute-start(bf16[2,2,4,256,384]{4,3,2,1,0:T(8,128)(2,1)} %get-tuple-element.555), channel_id=1, source_target_pairs={{0,1},{1,0},{2,3},{3,2},{4,5},{5,4},{6,7},{7,6},{8,9},{9,8},{10,11... | collective-permute-start | bytes 9437192 | tf_op jit(solution)/shard_map/ppermute | solution.py:809
  201.5 45.4 %collective-permute-start.29 = (bf16[2,1024,384]{2,1,0:T(8,128)(2,1)}, bf16[2,1024,384]{2,1,0:T(8,128)(2,1)}, u32[]{:S(2)}, u32[]{:S(2)}) collective-permute-start(bf16[2,1024,384]{2,1,0:T(8,128)(2,1)} %get-tuple-element.556), channel_id=1, source_target_pairs={{0,1},{1,0},{2,3},{3,2},{4,5},{5,4},{6,7},{7,6},{8,9},{9,8},{10,11... | collective-permute-start | bytes 4718600 | tf_op jit(solution)/shard_map/ppermute | solution.py:809
  252.0 54.1 %collective-permute-start.31 = (bf16[2,2,4,256,384]{4,3,2,1,0:T(8,128)(2,1)}, bf16[2,2,4,256,384]{4,3,2,1,0:T(8,128)(2,1)}, u32[]{:S(2)}, u32[]{:S(2)}) collective-permute-start(bf16[2,2,4,256,384]{4,3,2,1,0:T(8,128)(2,1)} %get-tuple-element.585), channel_id=1, source_target_pairs={{0,1},{1,0},{2,3},{3,2},{4,5},{5,4},{6,7},{7,6},{8,9},{9,8},{10,11... | collective-permute-start | bytes 9437192 | tf_op jit(solution)/shard_map/ppermute | solution.py:809
  252.0 45.6 %collective-permute-start.32 = (bf16[2,1024,384]{2,1,0:T(8,128)(2,1)}, bf16[2,1024,384]{2,1,0:T(8,128)(2,1)}, u32[]{:S(2)}, u32[]{:S(2)}) collective-permute-start(bf16[2,1024,384]{2,1,0:T(8,128)(2,1)} %get-tuple-element.586), channel_id=1, source_target_pairs={{0,1},{1,0},{2,3},{3,2},{4,5},{5,4},{6,7},{7,6},{8,9},{9,8},{10,11... | collective-permute-start | bytes 4718600 | tf_op jit(solution)/shard_map/ppermute | solution.py:809
  252.5 53.5 %collective-permute-start.30 = (bf16[3072,384]{1,0:T(8,128)(2,1)}, bf16[3072,384]{1,0:T(8,128)(2,1)}, u32[]{:S(2)}, u32[]{:S(2)}) collective-permute-start(bf16[3072,384]{1,0:T(8,128)(2,1)} %pad_maximum_fusion.3), channel_id=1, source_target_pairs={{0,2},{1,3},{2,0},{3,1},{4,6},{5,7},{6,4},{7,5},{8,10},{9,11},{10,... | collective-permute-start | bytes 7077896 | tf_op jit(solution)/shard_map/ppermute | solution.py:812
  361.6 47.8 %collective-permute-start.38 = (bf16[2,256,1024]{2,1,0:T(8,128)(2,1)}, bf16[2,256,1024]{2,1,0:T(8,128)(2,1)}, u32[]{:S(2)}, u32[]{:S(2)}) collective-permute-start(bf16[2,256,1024]{2,1,0:T(8,128)(2,1)} %pad_maximum_fusion.12), channel_id=1, source_target_pairs={{0,1},{1,0},{2,3},{3,2},{4,5},{5,4},{6,7},{7,6},{8,9},{9,8},{10,11... | collective-permute-start | bytes 3145736 | tf_op jit(solution)/shard_map/ppermute | solution.py:809
  361.9 47.5 %collective-permute-start.35 = (bf16[1536,384]{1,0:T(8,128)(2,1)}, bf16[1536,384]{1,0:T(8,128)(2,1)}, u32[]{:S(2)}, u32[]{:S(2)}) collective-permute-start(bf16[1536,384]{1,0:T(8,128)(2,1)} %add_convert_fusion.6), channel_id=1, source_target_pairs={{0,4},{4,0},{8,12},{12,8},{16,20},{20,16},{24,28},{28,24},{1,5},{5... | collective-permute-start | bytes 3538952 | tf_op jit(solution)/shard_map/ppermute | solution.py:816
  363.1 53.4 %collective-permute-start.36 = (bf16[3072,384]{1,0:T(8,128)(2,1)}, bf16[3072,384]{1,0:T(8,128)(2,1)}, u32[]{:S(2)}, u32[]{:S(2)}) collective-permute-start(bf16[3072,384]{1,0:T(8,128)(2,1)} %pad_maximum_fusion.4), channel_id=1, source_target_pairs={{0,2},{1,3},{2,0},{3,1},{4,6},{5,7},{6,4},{7,5},{8,10},{9,11},{10,... | collective-permute-start | bytes 7077896 | tf_op jit(solution)/shard_map/ppermute | solution.py:812
  363.7 53.2 %collective-permute-start.37 = (bf16[2,1536,384]{2,1,0:T(8,128)(2,1)}, bf16[2,1536,384]{2,1,0:T(8,128)(2,1)}, u32[]{:S(2)}, u32[]{:S(2)}) collective-permute-start(bf16[2,1536,384]{2,1,0:T(8,128)(2,1)} %get-tuple-element.649), channel_id=1, source_target_pairs={{0,8},{4,12},{8,0},{12,4},{16,24},{20,28},{24,16},{28,20},{1,9},{5... | collective-permute-start | bytes 7077896 | tf_op jit(solution)/shard_map/ppermute | solution.py:816
  431.4 49.7 %collective-permute-start.42 = (bf16[256,1024]{1,0:T(8,128)(2,1)}, bf16[256,1024]{1,0:T(8,128)(2,1)S(1)}, u32[]{:S(2)}, u32[]{:S(2)}) collective-permute-start(bf16[256,1024]{1,0:T(8,128)(2,1)} %fusion.27), channel_id=1, source_target_pairs={{0,2},{1,3},{2,0},{3,1},{4,6},{5,7},{6,4},{7,5},{8,10},{9,11},{10,... | collective-permute-start | bytes 1572872 | tf_op jit(solution)/shard_map/ppermute | solution.py:812
  432.9 48.2 %collective-permute-start.39 = (bf16[768,384]{1,0:T(8,128)(2,1)}, bf16[768,384]{1,0:T(8,128)(2,1)}, u32[]{:S(2)}, u32[]{:S(2)}) collective-permute-start(bf16[768,384]{1,0:T(8,128)(2,1)} %add_convert_fusion.10), channel_id=1, source_target_pairs={{0,8},{4,12},{8,0},{12,4},{16,24},{20,28},{24,16},{28,20},{1,9},{5... | collective-permute-start | bytes 1769480 | tf_op jit(solution)/shard_map/ppermute | solution.py:816
  433.4 47.8 %collective-permute-start.43 = (bf16[2,256,1024]{2,1,0:T(8,128)(2,1)}, bf16[2,256,1024]{2,1,0:T(8,128)(2,1)}, u32[]{:S(2)}, u32[]{:S(2)}) collective-permute-start(bf16[2,256,1024]{2,1,0:T(8,128)(2,1)} %get-tuple-element.686), channel_id=1, source_target_pairs={{0,1},{1,0},{2,3},{3,2},{4,5},{5,4},{6,7},{7,6},{8,9},{9,8},{10,11... | collective-permute-start | bytes 3145736 | tf_op jit(solution)/shard_map/ppermute | solution.py:809
  433.4 47.8 %collective-permute-start.40 = (bf16[1536,384]{1,0:T(8,128)(2,1)}, bf16[1536,384]{1,0:T(8,128)(2,1)}, u32[]{:S(2)}, u32[]{:S(2)}) collective-permute-start(bf16[1536,384]{1,0:T(8,128)(2,1)} %add_convert_fusion.5), channel_id=1, source_target_pairs={{0,4},{4,0},{8,12},{12,8},{16,20},{20,16},{24,28},{28,24},{1,5},{5... | collective-permute-start | bytes 3538952 | tf_op jit(solution)/shard_map/ppermute | solution.py:816
  434.7 46.5 %collective-permute-start.41 = (bf16[1536,384]{1,0:T(8,128)(2,1)}, bf16[1536,384]{1,0:T(8,128)(2,1)}, u32[]{:S(2)}, u32[]{:S(2)}) collective-permute-start(bf16[1536,384]{1,0:T(8,128)(2,1)} %fusion.10), channel_id=1, source_target_pairs={{0,2},{1,3},{2,0},{3,1},{4,6},{5,7},{6,4},{7,5},{8,10},{9,11},{10,... | collective-permute-start | bytes 3538952 | tf_op jit(solution)/shard_map/ppermute | solution.py:812
  493.1 38.7 %collective-permute-start.49 = (bf16[2,256,1024]{2,1,0:T(8,128)(2,1)}, bf16[2,256,1024]{2,1,0:T(8,128)(2,1)}, u32[]{:S(2)}, u32[]{:S(2)}) collective-permute-start(bf16[2,256,1024]{2,1,0:T(8,128)(2,1)} %get-tuple-element.707), channel_id=1, source_target_pairs={{0,1},{1,0},{2,3},{3,2},{4,5},{5,4},{6,7},{7,6},{8,9},{9,8},{10,11... | collective-permute-start | bytes 3145736 | tf_op jit(solution)/shard_map/ppermute | solution.py:809
  493.1 38.6 %collective-permute-start.45 = (bf16[768,384]{1,0:T(8,128)(2,1)}, bf16[768,384]{1,0:T(8,128)(2,1)}, u32[]{:S(2)}, u32[]{:S(2)}) collective-permute-start(bf16[768,384]{1,0:T(8,128)(2,1)} %add_convert_fusion.9), channel_id=1, source_target_pairs={{0,8},{4,12},{8,0},{12,4},{16,24},{20,28},{24,16},{28,20},{1,9},{5... | collective-permute-start | bytes 1769480 | tf_op jit(solution)/shard_map/ppermute | solution.py:816
  494.1 37.7 %collective-permute-start.46 = (bf16[768,384]{1,0:T(8,128)(2,1)}, bf16[768,384]{1,0:T(8,128)(2,1)}, u32[]{:S(2)}, u32[]{:S(2)}) collective-permute-start(bf16[768,384]{1,0:T(8,128)(2,1)} %fusion.15), channel_id=1, source_target_pairs={{0,4},{4,0},{8,12},{12,8},{16,20},{20,16},{24,28},{28,24},{1,5},{5... | collective-permute-start | bytes 1769480 | tf_op jit(solution)/shard_map/ppermute | solution.py:816
  496.2 35.6 %collective-permute-start.48 = (bf16[256,1024]{1,0:T(8,128)(2,1)}, bf16[256,1024]{1,0:T(8,128)(2,1)}, u32[]{:S(2)}, u32[]{:S(2)}) collective-permute-start(bf16[256,1024]{1,0:T(8,128)(2,1)} %fusion.28), channel_id=1, source_target_pairs={{0,2},{1,3},{2,0},{3,1},{4,6},{5,7},{6,4},{7,5},{8,10},{9,11},{10,... | collective-permute-start | bytes 1572872 | tf_op jit(solution)/shard_map/ppermute | solution.py:812
  544.9 44.5 %collective-permute-start.55 = (bf16[256,1024]{1,0:T(8,128)(2,1)}, bf16[256,1024]{1,0:T(8,128)(2,1)}, u32[]{:S(2)}, u32[]{:S(2)}) collective-permute-start(bf16[256,1024]{1,0:T(8,128)(2,1)} %fusion.29), channel_id=1, source_target_pairs={{0,2},{1,3},{2,0},{3,1},{4,6},{5,7},{6,4},{7,5},{8,10},{9,11},{10,... | collective-permute-start | bytes 1572872 | tf_op jit(solution)/shard_map/ppermute | solution.py:812
  550.1 39.3 %collective-permute-start.52 = (bf16[384,384]{1,0:T(8,128)(2,1)}, bf16[384,384]{1,0:T(8,128)(2,1)}, u32[]{:S(2)}, u32[]{:S(2)}) collective-permute-start(bf16[384,384]{1,0:T(8,128)(2,1)} %fusion.26), channel_id=1, source_target_pairs={{0,16},{4,20},{8,24},{12,28},{16,0},{20,4},{24,8},{28,12},{1,17},{... | collective-permute-start | bytes 884744 | tf_op jit(solution)/shard_map/ppermute | solution.py:816
  598.5 37.0 %collective-permute-start.57 = (bf16[768,384]{1,0:T(8,128)(2,1)S(1)}, bf16[768,384]{1,0:T(8,128)(2,1)S(1)}, u32[]{:S(2)}, u32[]{:S(2)}) collective-permute-start(bf16[768,384]{1,0:T(8,128)(2,1)S(1)} %pad_maximum_fusion.13), channel_id=1, source_target_pairs={{0,8},{4,12},{8,0},{12,4},{16,24},{20,28},{24,16},{28,20},{1,9},{5... | collective-permute-start | bytes 1769480 | tf_op jit(solution)/shard_map/ppermute | solution.py:816
  598.6 36.9 %collective-permute-start.58 = (bf16[384,384]{1,0:T(8,128)(2,1)}, bf16[384,384]{1,0:T(8,128)(2,1)S(1)}, u32[]{:S(2)}, u32[]{:S(2)}) collective-permute-start(bf16[384,384]{1,0:T(8,128)(2,1)} %add_convert_fusion.14), channel_id=1, source_target_pairs={{0,16},{4,20},{8,24},{12,28},{16,0},{20,4},{24,8},{28,12},{1,17},{... | collective-permute-start | bytes 884744 | tf_op jit(solution)/shard_map/ppermute | solution.py:816
  644.8 45.6 %collective-permute-start.64 = (bf16[1536,384]{1,0:T(8,128)(2,1)}, bf16[1536,384]{1,0:T(8,128)(2,1)S(1)}, u32[]{:S(2)}, u32[]{:S(2)}) collective-permute-start(bf16[1536,384]{1,0:T(8,128)(2,1)} %pad_maximum_fusion.9), channel_id=1, source_target_pairs={{0,4},{4,0},{8,12},{12,8},{16,20},{20,16},{24,28},{28,24},{1,5},{5... | collective-permute-start | bytes 3538952 | tf_op jit(solution)/shard_map/ppermute | solution.py:816
  645.7 44.6 %collective-permute-start.65 = (bf16[768,384]{1,0:T(8,128)(2,1)}, bf16[768,384]{1,0:T(8,128)(2,1)}, u32[]{:S(2)}, u32[]{:S(2)}) collective-permute-start(bf16[768,384]{1,0:T(8,128)(2,1)} %pad_maximum_fusion.14), channel_id=1, source_target_pairs={{0,8},{4,12},{8,0},{12,4},{16,24},{20,28},{24,16},{28,20},{1,9},{5... | collective-permute-start | bytes 1769480 | tf_op jit(solution)/shard_map/ppermute | solution.py:816
  645.7 44.6 %collective-permute-start.66 = (bf16[768,384]{1,0:T(8,128)(2,1)}, bf16[768,384]{1,0:T(8,128)(2,1)S(1)}, u32[]{:S(2)}, u32[]{:S(2)}) collective-permute-start(bf16[768,384]{1,0:T(8,128)(2,1)} %pad_maximum_fusion.15), channel_id=1, source_target_pairs={{0,4},{4,0},{8,12},{12,8},{16,20},{20,16},{24,28},{28,24},{1,5},{5... | collective-permute-start | bytes 1769480 | tf_op jit(solution)/shard_map/ppermute | solution.py:816
  646.9 36.7 %collective-permute-start.70 = (f32[1,2176]{1,0:T(1,128)S(1)}, f32[1,2176]{1,0:T(1,128)S(1)}, u32[]{:S(2)}, u32[]{:S(2)}) collective-permute-start(f32[1,2176]{1,0:T(1,128)S(1)} %add.830), channel_id=1, source_target_pairs={{0,4},{4,0},{8,12},{12,8},{16,20},{20,16},{24,28},{28,24},{1,5},{5... | collective-permute-start | bytes 26120 | tf_op jit(solution)/shard_map/ppermute | solution.py:816
  647.7 36.2 %collective-permute-start.67 = (bf16[32,1024]{1,0:T(8,128)(2,1)S(1)}, bf16[32,1024]{1,0:T(8,128)(2,1)S(1)}, u32[]{:S(2)}, u32[]{:S(2)}) collective-permute-start(bf16[32,1024]{1,0:T(8,128)(2,1)S(1)} %fusion.65), channel_id=1, source_target_pairs={{0,16},{4,20},{8,24},{12,28},{16,0},{20,4},{24,8},{28,12},{1,17},{... | collective-permute-start | bytes 196616 | tf_op jit(solution)/shard_map/ppermute | solution.py:816
  (139 other events, 1728.0 us)

commit v2 on v1

--- a/solution.py
+++ b/solution.py
@@ -1,3 +1,5 @@
+import functools
+
 import jax
 import jax.numpy as jnp
 from jax import lax
@@ -396,13 +398,15 @@
     residual_low[...] = back.astype(bf16)
 
 
-def last_kernel(tokens, residual_grad, gain, fg0, fg1, input_grad, gain_grad):
+def last_kernel(tokens, residual_grad, gain, *refs):
+    *parts, input_grad, gain_grad = refs
+
     @pl.when(pl.program_id(0) == 0)
     def _():
         gain_grad[...] = jnp.zeros_like(gain_grad)
 
     inputs = tokens[...].astype(f32)
-    first_grad = fg0[...].astype(f32) + fg1[...].astype(f32)
+    first_grad = sum(part[...].astype(f32) for part in parts)
     inverse = rms_scale(inputs)
     unit = inputs * inverse
     gain_grad[...] += jnp.sum(first_grad * unit, axis=0, keepdims=True)
@@ -665,12 +669,12 @@
 
 
 def attend_back(
-    part, place, residual_low, w_out, weights, first_t, proj, qk_low, v_low, mixed, lse, cos, sin,
+    skip, steps, place, residual_low, w_out, weights, first_t, proj, qk_low, v_low, mixed, lse, cos, sin,
     gain, seg_col, seg_row, spread,
 ):
     count = residual_low.shape[0]
-    steps = GRP // 2
-    step_cols = lambda width, rows=count: pl.BlockSpec((rows, width), lambda t, p: (0, t))
+    held = skip % (GRP // 2)
+    step_cols = lambda width, rows=count: pl.BlockSpec((rows, width), lambda t, p: (0, held + t))
     grad_spec = pl.BlockSpec((2, ROWS, GROUP_ALL), lambda t, p: (0, 0, t))
     return pl.pallas_call(
         attend_back_kernel,
@@ -679,7 +683,7 @@
             grid=(steps,),
             in_specs=[
                 whole((count, D)),
-                pl.BlockSpec((ROWS, D), lambda t, p: (part * steps + t, 0)),
+                pl.BlockSpec((ROWS, D), lambda t, p: (skip + t, 0)),
                 step_cols(GROUP_ALL, D),
                 whole((D, count)),
                 step_cols(GROUP_QK),
@@ -728,7 +732,7 @@
     return pl.pallas_call(
         last_kernel,
         grid=(count // BLOCK,),
-        in_specs=[rows_spec(D), rows_spec(D), whole((1, D)), rows_spec(D), rows_spec(D)],
+        in_specs=[rows_spec(D), rows_spec(D), whole((1, D))] + [rows_spec(D)] * len(first_grads),
         out_specs=[rows_spec(D), whole((1, D))],
         out_shape=[struct((count, D), bf16), struct((1, D), f32)],
         compiler_params=params(60),
@@ -762,27 +766,25 @@
     )(total, total, total, *held)
 
 
-def split_sums(halves):
-    def one(half, held):
-        at = lambda width: pl.BlockSpec((ROWS, width), lambda t: (0, GRP // 2 * half + t))
-        return pl.pallas_call(
-            lambda block, *refs: split_kernel(block, *refs[-3:]),
-            grid=(GRP // 2,),
-            in_specs=[lanes_spec(ROWS, GROUP_ALL)]
-            + [pl.BlockSpec(memory_space=pl.ANY)] * len(held),
-            out_specs=[at(GROUP_Q), at(GROUP_K), at(GROUP_K)],
-            out_shape=[
-                struct((ROWS, H * HD), f32),
-                struct((ROWS, KV * HD), f32),
-                struct((ROWS, KV * HD), f32),
-            ],
-            input_output_aliases={1 + k: k for k in range(len(held))},
-            compiler_params=params(60),
-            cost_estimate=cost(1e6, 4e6),
-            name="split_sums",
-        )(halves[half], *held)
-
-    return one(1, one(0, ()))
+def split_sums(total):
+    return pl.pallas_call(
+        split_kernel,
+        grid=(GRP,),
+        in_specs=[pl.BlockSpec((ROWS, GROUP_ALL), lambda t: (t, 0))],
+        out_specs=[
+            lanes_spec(ROWS, GROUP_Q),
+            lanes_spec(ROWS, GROUP_K),
+            lanes_spec(ROWS, GROUP_K),
+        ],
+        out_shape=[
+            struct((ROWS, H * HD), f32),
+            struct((ROWS, KV * HD), f32),
+            struct((ROWS, KV * HD), f32),
+        ],
+        compiler_params=params(60),
+        cost_estimate=cost(1e6, 4e6),
+        name="split_sums",
+    )(total)
 
 
 class Job:
@@ -828,18 +830,22 @@
         half = values.shape[axis] // 2
         return lax.dynamic_slice_in_dim(values, upper * half, half, axis)
 
-    def reduce_stages(kept, sent, early=()):
+    def core_stages(sent):
+        came = yield [(values, to_core) for values in sent]
+        return came
+
+    def reduce_stages(kept, came, sent, early=(), stepwise=False):
         rep = lax.axis_index("rep")
         upper_of = lambda bit: (rep >> bit) & 1
         flat = lambda values: values.reshape(-1, values.shape[-1])
         wide = lambda values: values.reshape(2, -1, values.shape[-1])
         join = lambda parts, axis=0: jnp.concatenate(parts, axis=axis) if len(parts) > 1 else parts[0]
-        came = yield [(values, to_core) for values in sent]
+        more = yield [(values, to_core) for values in sent]
+        came = list(came) + list(more)
         if early:
-            both = join(
-                [low_sum([wide(mine), wide(other)]) for mine, other in zip(kept, came)], axis=1
-            )
-            terms = [both]
+            terms = [
+                join([low_sum([wide(mine), wide(other)]) for mine, other in zip(kept, came)], axis=1)
+            ]
             for bit in early:
                 upper = upper_of(bit)
                 away = low_sum([half_of(term, 1 - upper, 1) for term in terms])
@@ -856,17 +862,29 @@
                 join([flat(values[0]) for values in came]),
             ]
         terms += yield [(away, to_far)]
-        late = [bit for bit in range(rep_bits) if bit not in early]
-        for bit in late:
-            upper = upper_of(bit)
-            away = low_sum([half_of(term, 1 - upper) for term in terms])
-            terms = [half_of(term, upper) for term in terms]
-            terms += yield [(away, to_rep(bit))]
+        for bit in range(rep_bits):
+            if bit not in early:
+                upper = upper_of(bit)
+                away = low_sum([half_of(term, 1 - upper) for term in terms])
+                terms = [half_of(term, upper) for term in terms]
+                terms += yield [(away, to_rep(bit))]
         total = low_sum(terms)
-        for bit in reversed(list(early) + late):
-            (got,) = yield [(total, to_rep(bit))]
-            total = ordered(upper_of(bit) == 1, total, got)
+        if stepwise:
+            for bit in reversed(range(rep_bits)):
+                (got,) = yield [(total, to_rep(bit))]
+                total = ordered(upper_of(bit) == 1, total, got)
+            return total
+        (total,) = yield [(total, functools.partial(replica_gather, early=early))]
         return total
+
+    def replica_gather(values, early):
+        bits = list(early) + [bit for bit in range(rep_bits) if bit not in early]
+        whole = lax.all_gather(values, "rep", axis=0, tiled=False)
+        size = values.shape
+        whole = whole.reshape((2,) * rep_bits + size)
+        order = [rep_bits - 1 - bit for bit in bits]
+        whole = whole.transpose(order + [rep_bits, rep_bits + 1])
+        return whole.reshape(-1, size[-1])
 
     def small_stages(values):
         for send in [to_core, to_far] + [to_rep(bit) for bit in range(rep_bits)]:
@@ -888,13 +906,20 @@
         return outs
 
     def finish_jobs(jobs):
+        running, turn = [], 0
         while not all(job.done for job in jobs):
-            left = [job for job in jobs if not job.done]
+            left = [job for job in jobs if not job.done and job not in [one for one, _ in running]]
             payloads = tie(*[[values for values, _ in job.wanted] for job in left])
             for job, group in zip(left, payloads):
                 job.start(group)
-            for job, group in zip(left, tie(*[job.flight for job in left])):
+            slow = [job for job in left if isinstance(job.wanted[0][1], functools.partial)]
+            running += [(job, turn + 3 + 2 * k) for k, job in enumerate(slow)]
+            ending = [job for job in left if job not in slow]
+            ending += [job for job, due in running if due <= turn or not ending]
+            running = [(job, due) for job, due in running if job not in ending]
+            for job, group in zip(ending, tie(*[job.flight for job in ending])):
                 job.advance(group)
+            turn += 1
         return [job.result for job in jobs]
 
     def body(
@@ -939,6 +964,7 @@
         yz_attn, x0, core_attn, first, segments = tie(yz_attn, x0, core_attn, first, segments)
 
         two_attn, x1 = spread_two(*yz_attn), to_far(q_ffn[1])
+        core_gate, core_up = to_core(w_gate), to_core(w_up)
         places = jnp.arange(count, dtype=jnp.int32)
         seg_col = segments.reshape(count, 1)
         seg_row = segments.reshape(1, count)
@@ -953,34 +979,30 @@
         spread = jnp.where(lane[:, None] == lane[None, :], 1.0 / HD, 0.0).astype(bf16)
         head_gain = jnp.concatenate([query_full] * (H // GRP) + [key_full] * (KV // GRP), axis=1)
         fold = jnp.where(jnp.arange(GROUP_QK) < GROUP_Q, score_scale * log2_e, 1.0)[None, :]
-        two_attn, x1, cos, sin, spread, head_gain = tie(two_attn, x1, cos, sin, spread, head_gain)
+        two_attn, x1, cos, sin, spread, head_gain, core_gate, core_up = tie(
+            two_attn, x1, cos, sin, spread, head_gain, core_gate, core_up
+        )
 
         far_attn = far_of(x_attn, *yz_attn, *two_attn)
         far_core_attn = to_core(far_attn)
         attn_pieces = (own_attn, core_attn, far_attn, far_core_attn)
         inputs = (place, first, attn_pieces, cos, sin, head_gain * fold, seg_col, seg_row, spread)
         inputs, x0, x1, q2 = tie(inputs, x0, x1, q_ffn[2])
-        yz0, x2 = spread_one(x0), to_far(q2)
-        saved0, inputs, yz0, x1, x2, owns = tie(
-            attend(0, *inputs), inputs, yz0, x1, x2, [w_gate, w_up, w_down]
-        )
-        two0, yz1, yz2 = spread_two(*yz0), spread_one(x1), spread_one(x2)
-        cores = [to_core(values) for values in owns]
-        saved1, two0, yz1, yz2, cores = tie(attend(1, *inputs), two0, yz1, yz2, cores)
+        yz0, yz1, x2 = spread_one(x0), spread_one(x1), to_far(q2)
+        saved0, inputs, yz0, yz1, x2, w_down = tie(attend(0, *inputs), inputs, yz0, yz1, x2, w_down)
+        two0, two1, core_down = spread_two(*yz0), spread_two(*yz1), to_core(w_down)
+        saved1, two0, two1, core_down, x2 = tie(attend(1, *inputs), two0, two1, core_down, x2)
         far0 = far_of(x0, *yz0, *two0)
+        far1 = far_of(x1, *yz1, *two1)
         mixed = (saved0[3], saved1[3])
-        far0, yz1, yz2, mixed = tie(far0, yz1, yz2, mixed)
-        two1, two2 = spread_two(*yz1), spread_two(*yz2)
-        far_core0 = to_core(far0)
-        middle_out, far_core0, two1, two2 = tie(
-            middle(place, mixed, tokens, ffn_full, attn_pieces), far_core0, two1, two2
+        far0, far1, mixed, x2 = tie(far0, far1, mixed, x2)
+        far_core0, far_core1, yz2 = to_core(far0), to_core(far1), spread_one(x2)
+        middle_out, far_core0, far_core1, yz2 = tie(
+            middle(place, mixed, tokens, ffn_full, attn_pieces), far_core0, far_core1, yz2
         )
         residual, second, second_t, out_weights = middle_out
-        far1, far2 = far_of(x1, *yz1, *two1), far_of(x2, *yz2, *two2)
-        second, far1, far2 = tie(second, far1, far2)
-        core_gate, core_up, core_down = cores
         near = (w_gate, w_up, core_gate, core_up, w_down, core_down)
-        fars = [(far0, far_core0), None, None]
+        fars = [(far0, far_core0), (far1, far_core1), None]
 
         outs, second_grads, jobs = [], [], []
         for i in range(CHUNKS):
@@ -991,45 +1013,69 @@
                 jobs,
             )
             if i == 0:
-                out, *far_cores = tie(out, to_core(far1), to_core(far2))
-                fars[1:] = [(far1, far_cores[0]), (far2, far_cores[1])]
+                out, two2 = tie(out, spread_two(*yz2))
+                far2 = far_of(x2, *yz2, *two2)
+                second, far2 = tie(second, far2)
+            if i == 1:
+                out, far_core2 = tie(out, to_core(far2))
+                fars[2] = (far2, far_core2)
             outs.append(out)
             second_grads.append(second_grad)
-            early = (1,) if i == CHUNKS - 1 else ()
-            jobs.append(Job(reduce_stages([gu_kept, dn_kept], [gu_sent, dn_sent], early)))
-
-        outputs, residual_grad, residual_low, ffn_gain_grad = beside(
-            after_ffn, (residual, out_grad, ffn_full, outs, second_grads), jobs[2:], jobs[2:]
-        )
-
-        def out_back(mixed, residual_low):
-            wgrad = dot_tn(jnp.concatenate(mixed, axis=1), residual_low)
+            early = (0,) if i == CHUNKS - 1 else ()
+            jobs.append(Job(reduce_stages([gu_kept, dn_kept], [], [gu_sent, dn_sent], early)))
+
+        def after_and_out(*given):
+            outputs, residual_grad, residual_low, ffn_gain_grad = after_ffn(*given[:-1])
+            wgrad = dot_tn(jnp.concatenate(given[-1], axis=1), residual_low)
             wgrad = wgrad.astype(bf16).reshape(GRP, ROWS, D)
             at = lambda q: lax.dynamic_slice_in_dim(wgrad, g ^ q, 1, 0)
-            return jnp.concatenate([at(0), at(2)], axis=0), jnp.concatenate([at(1), at(3)], axis=0)
-
-        out_kept, out_sent = out_back(mixed, residual_low)
-        jobs.append(Job(reduce_stages([out_kept], [out_sent])))
-
-        first_grads, head_grads = [], []
-        for part, saved in enumerate((saved0, saved1)):
+            out_kept = jnp.concatenate([at(0), at(2)], axis=0)
+            out_sent = jnp.concatenate([at(1), at(3)], axis=0)
+            return outputs, residual_grad, residual_low, ffn_gain_grad, out_kept, out_sent
+
+        outputs, residual_grad, residual_low, ffn_gain_grad, out_kept, out_sent = beside(
+            after_and_out,
+            (residual, out_grad, ffn_full, outs, second_grads, mixed),
+            [jobs[0], jobs[2]],
+            [jobs[0], jobs[2]],
+        )
+
+        first_grads, head_grads, kepts, cores = [], [], [], []
+        to_send = [out_sent]
+        for skip, steps in ((0, 2), (2, 1), (3, 1)):
+            core_job = Job(core_stages(to_send))
+            saved = (saved0, saved1)[skip // 2]
+            last = skip == GRP - 1
             first_grad, kept, sent, head_grad = beside(
-                lambda *given, part=part: attend_back(part, *given),
+                lambda *given, skip=skip, steps=steps: attend_back(skip, steps, *given),
                 (
                     place, residual_low, out_weights, saved[5], first_t, *saved[:5],
                     cos, sin, head_gain, seg_col, seg_row, spread,
                 ),
-                jobs,
-                jobs,
+                jobs + [core_job],
+                (jobs[1:] if last else jobs) + [core_job],
             )
             first_grads.append(first_grad)
             head_grads.append(head_grad)
-            jobs.append(Job(reduce_stages([kept], [sent])))
+            cores.append(core_job.result[0])
+            by_group = [(kept[:, :, :GROUP_ALL], sent[:, :, :GROUP_ALL])]
+            if steps == 2:
+                by_group.append((kept[:, :, GROUP_ALL:], sent[:, :, GROUP_ALL:]))
+            kepts += [pair[0] for pair in by_group]
+            to_send = [sent]
+        out_came, two_came, one_came = cores
+        came = [two_came[:, :, :GROUP_ALL], two_came[:, :, GROUP_ALL:], one_came]
+        attn_job = Job(reduce_stages(kepts, came, to_send, stepwise=True))
+        out_job = Job(reduce_stages([out_kept], [out_came], [], stepwise=True))
         input_grad, attn_gain_grad = beside(
-            last_norm, (tokens, residual_grad, attn_full, first_grads), jobs, jobs
+            last_norm,
+            (tokens, residual_grad, attn_full, first_grads),
+            jobs[1:] + [attn_job, out_job],
+            jobs + [attn_job, out_job],
         )
-
-        head_grad = (head_grads[0] + head_grads[1]).reshape(GROUP_QK // HD, HD)
+        jobs += [attn_job, out_job]
+
+        head_grad = sum(head_grads).reshape(GROUP_QK // HD, HD)
         small = jnp.concatenate(
             [
                 attn_gain_grad[0],
@@ -1039,13 +1085,13 @@
             ]
         )
         jobs.append(Job(small_stages(small.reshape(1, -1))))
-        sum0, sum1, sum2, out_sum, attn0, attn1, small = finish_jobs(jobs)
+        sum0, sum1, sum2, attn_sum, out_sum, small = finish_jobs(jobs)
         mine = lambda start, size: lax.dynamic_slice_in_dim(small[0], start + g * size, size, 0)
         held = ()
         for i, total in enumerate((sum0, sum1, sum2)):
             held = finish(i, total, held)
         gate_grad, up_grad, down_grad = held
-        query_grad, key_grad, value_grad = split_sums((attn0, attn1))
+        query_grad, key_grad, value_grad = split_sums(attn_sum)
         return (
             outputs,
             input_grad,

time: 790 us -> 745 us (0.943)
  waiting for transfers between devices: 198 us -> 167 us
  other arithmetic: 128 us -> 106 us
  starting transfers between devices: 79.9 us -> 62.2 us
  between operations: 2.35 us -> 14.9 us
    ppermute x55 -> x40, waiting for transfers between devices: 170 us -> 111 us  [by_xor(): return lambda values: lax.ppermute(values, 'rep', pairs)]
    ppermute x11 -> x10, waiting for transfers between devices: 25.2 us -> 53.5 us  [to_far(): return lax.ppermute(values, 'grp', far_pairs)]
    ppermute x55 -> x40, starting transfers between devices: 63.3 us -> 45.8 us  [by_xor(): return lambda values: lax.ppermute(values, 'rep', pairs)]
    concatenate x17 -> x5, other arithmetic: 12.9 us -> 1.13 us  [ordered(): jnp.concatenate([jnp.where(upper, other, own), jnp.where(upper, own, othe...]
    select_n x18 -> x6, other arithmetic: 11.7 us -> 0.48 us  [ordered(): jnp.where(upper, other, own)]
    transpose x0 -> x3, local copies, waits for them, and re-layouts: none -> 9.93 us  [replica_gather(): whole = whole.transpose(order + [rep_bits, rep_bits + 1])]
    pallas_call x2 -> x3, Pallas kernels: 85.8 us -> 92.5 us  [attend_back(): pl.pallas_call(attend_back_kernel, grid_spec=pltpu.PrefetchScalarGridSpec...]
    convert_element_type x33 -> x30, other arithmetic: 72.1 us -> 67.1 us  [low_sum(): return sum((term.astype(f32) for term in terms)).astype(bf16)]
  transfers between devices with their start and end apart: 84 -> 72, of which waited for: 29 -> 26; matrix products, arithmetic and copies ran while one was open for 8% -> 12% of each run, Pallas kernels for 40% -> 43%
where the time goes in v2:
time: 745 us; the launch traced here: 735 us
  Pallas kernels  325 us (44%)
  waiting for transfers between devices  167 us (22%)
  other arithmetic  106 us (14%)
  starting transfers between devices  62.2 us (8%)
  local copies, waits for them, and re-layouts  47.3 us (6%)
  between operations  14.9 us (2%)
    pallas_call x3, Pallas kernels, ffn(): pl.pallas_call(ffn_kernel, grid_spec=pltpu.PrefetchScalarGridSpec(num_sca...  134 us
    ppermute x40, waiting for transfers between devices, by_xor(): return lambda values: lax.ppermute(values, 'rep', pairs)  111 us
    pallas_call x3, Pallas kernels, attend_back(): pl.pallas_call(attend_back_kernel, grid_spec=pltpu.PrefetchScalarGridSpec...  92.5 us
    convert_element_type x30, other arithmetic, low_sum(): return sum((term.astype(f32) for term in terms)).astype(bf16)  67.1 us
    ppermute x10, waiting for transfers between devices, to_far(): return lax.ppermute(values, 'grp', far_pairs)  53.5 us
    ppermute x40, starting transfers between devices, by_xor(): return lambda values: lax.ppermute(values, 'rep', pairs)  45.8 us
    pallas_call x2, Pallas kernels, attend(): pl.pallas_call(attend_kernel, grid_spec=pltpu.PrefetchScalarGridSpec(num_...  40.5 us
    concatenate x6, other arithmetic, reduce_stages(): jnp.concatenate(parts, axis=axis)  16.6 us
  transfers between devices with their start and end apart: 72, of which 26 were waited for; matrix products, arithmetic and copies ran while one was open for 12% of the time, Pallas kernels for 43%

profile of v2, /device:TPU:0, one launch (start us, length us, event | category | flops | bytes accessed | tf_op | source)
XLA Modules:
  0.0 734.7 jit_solution(16922137983751501825)
XLA Ops:
  18.4 7.3 all-gather.4
  29.8 8.0 %collective-permute-done.2 = bf16[64,3072]{1,0:T(8,128)(2,1)S(1)} collective-permute-done((bf16[64,3072]{1,0:T(8,128)(2,1)S(1)}, bf16[64,3072]{1,0:T(8,128)(2,1)S(1)}, u32[]{:S(2)}, u32[]{:S(2)}) %collective-permute-start.2) | collective-permute-done | bytes 393248 | tf_op jit(solution)/shard_map/ppermute | solution.py:818
  40.6 5.6 first_norm.1
  57.6 5.2 collective-permute-done.7
  74.2 20.0 %attend.2 = (f32[1024,768]{1,0:T(8,128)}, bf16[1024,768]{1,0:T(8,128)(2,1)}, bf16[1024,256]{1,0:T(8,128)(2,1)}, bf16[1024,512]{1,0:T(8,128)(2,1)}, f32[1024,512]{1,0:T(8,128)}, /*index=5*/bf16[1024,1024]{1,0:T(8,128)(2,1)}) custom-call(s32[2]{0:T(128)} %pad_add_fusion.place_ref, bf16[1024,1024]{1,0:T(8,128)(2,1)} %get-tuple-element.462.first, ...), custom_call_target="tpu_custom_call" | custom-call | flops 10000000000 | bytes 12000000 | tf_op jit(solution)/shard_map/attend/pallas_call | solution.py:519
  106.3 20.5 %attend.3 = (f32[1024,768]{1,0:T(8,128)}, bf16[1024,768]{1,0:T(8,128)(2,1)}, bf16[1024,256]{1,0:T(8,128)(2,1)}, bf16[1024,512]{1,0:T(8,128)(2,1)}, f32[1024,512]{1,0:T(8,128)}, /*index=5*/bf16[1024,1024]{1,0:T(8,128)(2,1)}) custom-call(s32[2]{0:T(128)} %pad_add_fusion.place_ref, bf16[1024,1024]{1,0:T(8,128)(2,1)} %get-tuple-element.462.first, ...), custom_call_target="tpu_custom_call" | custom-call | flops 10000000000 | bytes 12000000 | tf_op jit(solution)/shard_map/attend/pallas_call | solution.py:519
  135.1 9.6 %middle.1 = (f32[1024,1024]{1,0:T(8,128)}, bf16[1024,1024]{1,0:T(8,128)(2,1)}, bf16[1024,1024]{1,0:T(8,128)(2,1)}, bf16[1024,1024]{1,0:T(8,128)(2,1)}) custom-call(s32[2]{0:T(128)} %pad_add_fusion.place_ref, bf16[1024,512]{1,0:T(8,128)(2,1)} %get-tuple-element.636.mixed0.mixed, bf16[1024,512]{1,0:T(8,128)(2,1)} %get-tuple-element.699.mixed1.mixed, ...), custom_call_target="tpu_custom_call" | custom-call | flops 2000000000 | bytes 16000000 | tf_op jit(solution)/shard_map/middle/pallas_call | solution.py:570
  151.5 44.6 %ffn.3 = (bf16[1024,1024]{1,0:T(8,128)(2,1)}, bf16[1024,1024]{1,0:T(8,128)(2,1)}, bf16[2,2,4,256,384]{4,3,2,1,0:T(8,128)(2,1)}, bf16[2,2,4,256,384]{4,3,2,1,0:T(...) custom-call(s32[2]{0:T(128)} %pad_add_fusion.place_ref, ...), custom_call_target="tpu_custom_call" | custom-call | flops 28999999488 | bytes 36000000 | tf_op jit(solution)/shard_map/ffn/pallas_call | solution.py:610
  201.3 44.7 %ffn.4 = (bf16[1024,1024]{1,0:T(8,128)(2,1)}, bf16[1024,1024]{1,0:T(8,128)(2,1)}, bf16[2,2,4,256,384]{4,3,2,1,0:T(8,128)(2,1)}, bf16[2,2,4,256,384]{4,3,2,1,0:T(...) custom-call(s32[2]{0:T(128)} %pad_add_fusion.place_ref, ...), custom_call_target="tpu_custom_call" | custom-call | flops 28999999488 | bytes 36000000 | tf_op jit(solution)/shard_map/ffn/pallas_call | solution.py:610
  256.4 44.8 %ffn.5 = (bf16[1024,1024]{1,0:T(8,128)(2,1)}, bf16[1024,1024]{1,0:T(8,128)(2,1)}, bf16[2,2,4,256,384]{4,3,2,1,0:T(8,128)(2,1)}, bf16[2,2,4,256,384]{4,3,2,1,0:T(...) custom-call(s32[2]{0:T(128)} %pad_add_fusion.place_ref, ...), custom_call_target="tpu_custom_call" | custom-call | flops 28999999488 | bytes 36000000 | tf_op jit(solution)/shard_map/ffn/pallas_call | solution.py:610
  301.2 6.7 collective-permute-done.30
  316.6 10.7 %after_ffn.1 = (bf16[1024,1024]{1,0:T(8,128)(2,1)}, f32[1024,1024]{1,0:T(8,128)}, bf16[1024,1024]{1,0:T(8,128)(2,1)}, f32[1,1024]{1,0:T(1,128)}) custom-call(f32[1024,1024]{1,0:T(8,128)} %get-tuple-element.590.residual, bf16[1024,1024]{1,0:T(8,128)(2,1)} %grad.5, f32[1,1024]{1,0:T(1,128)} %bitcast.200, bf16[1024,1024]{1,0:T(8,128)(2,1)} %get-tuple-element.593.out0, ...), custom_call_target="tpu_custom_call" | custom-call | flops 20000000 | bytes 24000000 | tf_op jit(solution)/shard_map/after_ffn/pallas_call | solution.py:654
  327.4 4.6 fusion.7
  350.1 9.9 %fusion.1 = (bf16[2,1536,384]{2,1,0:T(8,128)(2,1)}, bf16[2,1536,384]{2,1,0:T(8,128)(2,1)}) fusion(s32[]{:T(128)S(6)} %select_n.312, bf16[2,2048,384]{2,1,0:T(8,128)(2,1)S(1)} %bitcast.175, bf16[2,1024,384]{2,1,0:T(8,128)(2,1)S(1)} %add_convert_fusion.1, s32[]{:T(128)S(6)} %select_n.305), kind=kLoop, calls=%fused_computation.43 | loop fusion | flops 9437184 | bytes 9437192 | tf_op jit(solution)/shard_map/concatenate | solution.py:842
  368.2 43.1 %attend_back.3 = (bf16[1024,1024]{1,0:T(8,128)(2,1)}, bf16[2,256,1024]{2,1,0:T(8,128)(2,1)}, bf16[2,256,1024]{2,1,0:T(8,128)(2,1)}, f32[1,384]{1,0:T(1,128)}) custom-call(s32[2]{0:T(128)} %pad_add_fusion.place_ref, bf16[1024,1024]{1,0:T(8,128)(2,1)} %get-tuple-element.692.residual_low, bf16[1024,1024]{1,0:T(8,128)(2,1)} %get-tuple-element.693.w_out, ...), custom_call_target="tpu_custom_call" | custom-call | flops 30000001024 | bytes 20000000 | tf_op jit(solution)/shard_map/attend_back/pallas_call | solution.py:679
  413.9 5.3 collective-permute-done.37
  425.6 4.7 add_convert_fusion.5
  436.0 24.4 %attend_back.4 = (bf16[1024,1024]{1,0:T(8,128)(2,1)}, bf16[2,256,512]{2,1,0:T(8,128)(2,1)}, bf16[2,256,512]{2,1,0:T(8,128)(2,1)}, f32[1,384]{1,0:T(1,128)}) custom-call(s32[2]{0:T(128)} %pad_add_fusion.place_ref, bf16[1024,1024]{1,0:T(8,128)(2,1)} %get-tuple-element.692.residual_low, bf16[1024,1024]{1,0:T(8,128)(2,1)} %get-tuple-element.693.w_out, ...), custom_call_target="tpu_custom_call" | custom-call | flops 30000001024 | bytes 20000000 | tf_op jit(solution)/shard_map/attend_back/pallas_call | solution.py:679
  478.5 25.0 %attend_back.5 = (bf16[1024,1024]{1,0:T(8,128)(2,1)}, bf16[2,256,512]{2,1,0:T(8,128)(2,1)}, bf16[2,256,512]{2,1,0:T(8,128)(2,1)}, f32[1,384]{1,0:T(1,128)}) custom-call(s32[2]{0:T(128)} %pad_add_fusion.place_ref, bf16[1024,1024]{1,0:T(8,128)(2,1)} %get-tuple-element.692.residual_low, bf16[1024,1024]{1,0:T(8,128)(2,1)} %get-tuple-element.693.w_out, ...), custom_call_target="tpu_custom_call" | custom-call | flops 30000001024 | bytes 20000000 | tf_op jit(solution)/shard_map/attend_back/pallas_call | solution.py:679
  505.7 22.3 %collective-permute-done.45 = bf16[768,384]{1,0:T(8,128)(2,1)} collective-permute-done((bf16[768,384]{1,0:T(8,128)(2,1)}, bf16[768,384]{1,0:T(8,128)(2,1)}, u32[]{:S(2)}, u32[]{:S(2)}) %collective-permute-start.45) | collective-permute-done | bytes 589856 | tf_op jit(solution)/shard_map/ppermute | solution.py:818
  536.1 7.8 %last_norm.1 = (bf16[1024,1024]{1,0:T(8,128)(2,1)}, f32[1,1024]{1,0:T(1,128)}) custom-call(bf16[1024,1024]{1,0:T(8,128)(2,1)} %tokens.4, f32[1024,1024]{1,0:T(8,128)} %get-tuple-element.719.residual_grad, f32[1,1024]{1,0:T(1,128)} %bitcast.202, bf16[1024,1024]{1,0:T(8,128)(2,1)} %get-tuple-element.721.refs_0_, ...), custom_call_target="tpu_custom_call" | custom-call | flops 20000000 | bytes 12000000 | tf_op jit(solution)/shard_map/last_norm/pallas_call | solution.py:732
  552.4 6.2 collective-permute-done.48
  574.8 32.1 %collective-permute-done.51 = bf16[256,1024]{1,0:T(8,128)(2,1)} collective-permute-done((bf16[256,1024]{1,0:T(8,128)(2,1)}, bf16[256,1024]{1,0:T(8,128)(2,1)}, u32[]{:S(2)}, u32[]{:S(2)}) %collective-permute-start.51) | collective-permute-done | bytes 524320 | tf_op jit(solution)/shard_map/ppermute | solution.py:814
  616.5 13.7 %collective-permute-done.54 = bf16[128,1024]{1,0:T(8,128)(2,1)S(1)} collective-permute-done((bf16[128,1024]{1,0:T(8,128)(2,1)}, bf16[128,1024]{1,0:T(8,128)(2,1)S(1)}, u32[]{:S(2)}, u32[]{:S(2)}) %collective-permute-start.54) | collective-permute-done | bytes 262176 | tf_op jit(solution)/shard_map/ppermute | solution.py:818
  639.0 9.4 %collective-permute-done.57 = bf16[64,1024]{1,0:T(8,128)(2,1)} collective-permute-done((bf16[64,1024]{1,0:T(8,128)(2,1)S(1)}, bf16[64,1024]{1,0:T(8,128)(2,1)}, u32[]{:S(2)}, u32[]{:S(2)}) %collective-permute-start.57) | collective-permute-done | bytes 131104 | tf_op jit(solution)/shard_map/ppermute | solution.py:818
  659.7 4.5 collective-permute-done.61
  664.2 11.4 %collective-permute-done.60 = bf16[32,1024]{1,0:T(8,128)(2,1)} collective-permute-done((bf16[32,1024]{1,0:T(8,128)(2,1)}, bf16[32,1024]{1,0:T(8,128)(2,1)}, u32[]{:S(2)}, u32[]{:S(2)}) %collective-permute-start.60) | collective-permute-done | bytes 65568 | tf_op jit(solution)/shard_map/ppermute | solution.py:818
  682.4 9.4 %collective-permute-done.64 = f32[1,2176]{1,0:T(1,128)S(1)} collective-permute-done((f32[1,2176]{1,0:T(1,128)S(1)}, f32[1,2176]{1,0:T(1,128)S(1)}, u32[]{:S(2)}, u32[]{:S(2)}) %collective-permute-start.64) | collective-permute-done | bytes 8736 | tf_op jit(solution)/shard_map/ppermute | solution.py:818
  697.4 5.7 collective-permute-done.66
  705.4 4.5 finish.3
  709.9 4.5 finish.4
  715.6 4.5 finish.5
  (378 shorter events, 238.9 us)
Async XLA Ops:
  7.2 537.7 %all-gather.9.cloned.1.call-start = ((), (), s32[]{:S(2)}) async-start(), calls=%async_computation | async-start | bytes 2654208 | tf_op jit(solution)/shard_map/all_gather | solution.py:882
  11.3 38.8 %collective-permute-start.4 = (bf16[256,3072]{1,0:T(8,128)(2,1)}, bf16[256,3072]{1,0:T(8,128)(2,1)S(1)}, u32[]{:S(2)}, u32[]{:S(2)}) collective-permute-start(bf16[256,3072]{1,0:T(8,128)(2,1)} %get-tuple-element.463.own), channel_id=1, source_target_pairs={{0,1},{1,0},{2,3},{3,2},{4,5},{5,4},{6,7},{7,6},{8,9},{9,8},{10,11... | collective-permute-start | bytes 4718600 | tf_op jit(solution)/shard_map/ppermute | solution.py:811
  11.7 51.1 %collective-permute-start.8 = (bf16[256,4608]{1,0:T(8,128)(2,1)}, bf16[256,4608]{1,0:T(8,128)(2,1)}, u32[]{:S(2)}, u32[]{:S(2)}) collective-permute-start(bf16[256,4608]{1,0:T(8,128)(2,1)} %gate1.2), channel_id=1, source_target_pairs={{0,1},{1,0},{2,3},{3,2},{4,5},{5,4},{6,7},{7,6},{8,9},{9,8},{10,11... | collective-permute-start | bytes 7077896 | tf_op jit(solution)/shard_map/ppermute | solution.py:811
  11.8 51.1 %collective-permute-start.9 = (bf16[256,4608]{1,0:T(8,128)(2,1)}, bf16[256,4608]{1,0:T(8,128)(2,1)}, u32[]{:S(2)}, u32[]{:S(2)}) collective-permute-start(bf16[256,4608]{1,0:T(8,128)(2,1)} %up1.2), channel_id=1, source_target_pairs={{0,1},{1,0},{2,3},{3,2},{4,5},{5,4},{6,7},{7,6},{8,9},{9,8},{10,11... | collective-permute-start | bytes 7077896 | tf_op jit(solution)/shard_map/ppermute | solution.py:811
  67.6 26.6 %collective-permute-start.12 = (bf16[768,384]{1,0:T(8,128)(2,1)}, bf16[768,384]{1,0:T(8,128)(2,1)}, u32[]{:S(2)}, u32[]{:S(2)}) collective-permute-start(bf16[768,384]{1,0:T(8,128)(2,1)} %collective-permute-done.3), channel_id=1, source_target_pairs={{0,8},{4,12},{8,0},{12,4},{16,24},{20,28},{24,16},{28,20},{1,9},{5... | collective-permute-start | bytes 1769480 | tf_op jit(solution)/shard_map/ppermute | solution.py:818
  97.2 29.7 %collective-permute-start.20 = (bf16[1152,1024]{1,0:T(8,128)(2,1)}, bf16[1152,1024]{1,0:T(8,128)(2,1)}, u32[]{:S(2)}, u32[]{:S(2)}) collective-permute-start(bf16[1152,1024]{1,0:T(8,128)(2,1)} %down.3), channel_id=1, source_target_pairs={{0,1},{1,0},{2,3},{3,2},{4,5},{5,4},{6,7},{7,6},{8,9},{9,8},{10,11... | collective-permute-start | bytes 7077896 | tf_op jit(solution)/shard_map/ppermute | solution.py:811
  148.4 47.7 %collective-permute-start.26 = (bf16[384,384]{1,0:T(8,128)(2,1)S(1)}, bf16[384,384]{1,0:T(8,128)(2,1)S(1)}, u32[]{:S(2)}, u32[]{:S(2)}) collective-permute-start(bf16[384,384]{1,0:T(8,128)(2,1)S(1)} %slice.191), channel_id=1, source_target_pairs={{0,4},{4,0},{8,12},{12,8},{16,20},{20,16},{24,28},{28,24},{1,5},{5... | collective-permute-start | bytes 884744 | tf_op jit(solution)/shard_map/ppermute | solution.py:818
  149.9 46.2 %collective-permute-start.25 = (bf16[384,384]{1,0:T(8,128)(2,1)S(1)}, bf16[384,384]{1,0:T(8,128)(2,1)S(1)}, u32[]{:S(2)}, u32[]{:S(2)}) collective-permute-start(bf16[384,384]{1,0:T(8,128)(2,1)S(1)} %slice.190), channel_id=1, source_target_pairs={{0,8},{4,12},{8,0},{12,4},{16,24},{20,28},{24,16},{28,20},{1,9},{5... | collective-permute-start | bytes 884744 | tf_op jit(solution)/shard_map/ppermute | solution.py:818
  199.1 47.0 %collective-permute-start.27 = (bf16[2,2,4,256,384]{4,3,2,1,0:T(8,128)(2,1)}, bf16[2,2,4,256,384]{4,3,2,1,0:T(8,128)(2,1)}, u32[]{:S(2)}, u32[]{:S(2)}) collective-permute-start(bf16[2,2,4,256,384]{4,3,2,1,0:T(8,128)(2,1)} %get-tuple-element.549), channel_id=1, source_target_pairs={{0,1},{1,0},{2,3},{3,2},{4,5},{5,4},{6,7},{7,6},{8,9},{9,8},{10,11... | collective-permute-start | bytes 9437192 | tf_op jit(solution)/shard_map/ppermute | solution.py:811
  200.6 45.4 %collective-permute-start.28 = (bf16[2,1024,384]{2,1,0:T(8,128)(2,1)}, bf16[2,1024,384]{2,1,0:T(8,128)(2,1)S(1)}, u32[]{:S(2)}, u32[]{:S(2)}) collective-permute-start(bf16[2,1024,384]{2,1,0:T(8,128)(2,1)} %get-tuple-element.550), channel_id=1, source_target_pairs={{0,1},{1,0},{2,3},{3,2},{4,5},{5,4},{6,7},{7,6},{8,9},{9,8},{10,11... | collective-permute-start | bytes 4718600 | tf_op jit(solution)/shard_map/ppermute | solution.py:811
  201.2 47.7 %collective-permute-start.29 = (bf16[4,768,384]{2,1,0:T(8,128)(2,1)}, bf16[4,768,384]{2,1,0:T(8,128)(2,1)}, u32[]{:S(2)}, u32[]{:S(2)}) collective-permute-start(bf16[4,768,384]{2,1,0:T(8,128)(2,1)} %pad_maximum_fusion.2.far), channel_id=1, source_target_pairs={{0,1},{1,0},{2,3},{3,2},{4,5},{5,4},{6,7},{7,6},{8,9},{9,8},{10,11... | collective-permute-start | bytes 7077896 | tf_op jit(solution)/shard_map/ppermute | solution.py:811
  250.8 57.1 %collective-permute-start.31 = (bf16[2,2,4,256,384]{4,3,2,1,0:T(8,128)(2,1)}, bf16[2,2,4,256,384]{4,3,2,1,0:T(8,128)(2,1)}, u32[]{:S(2)}, u32[]{:S(2)}) collective-permute-start(bf16[2,2,4,256,384]{4,3,2,1,0:T(8,128)(2,1)} %get-tuple-element.581), channel_id=1, source_target_pairs={{0,1},{1,0},{2,3},{3,2},{4,5},{5,4},{6,7},{7,6},{8,9},{9,8},{10,11... | collective-permute-start | bytes 9437192 | tf_op jit(solution)/shard_map/ppermute | solution.py:811
  253.8 47.4 %collective-permute-start.32 = (bf16[2,1024,384]{2,1,0:T(8,128)(2,1)}, bf16[2,1024,384]{2,1,0:T(8,128)(2,1)}, u32[]{:S(2)}, u32[]{:S(2)}) collective-permute-start(bf16[2,1024,384]{2,1,0:T(8,128)(2,1)} %get-tuple-element.582), channel_id=1, source_target_pairs={{0,1},{1,0},{2,3},{3,2},{4,5},{5,4},{6,7},{7,6},{8,9},{9,8},{10,11... | collective-permute-start | bytes 4718600 | tf_op jit(solution)/shard_map/ppermute | solution.py:811
  254.0 53.9 %collective-permute-start.30 = (bf16[3072,384]{1,0:T(8,128)(2,1)}, bf16[3072,384]{1,0:T(8,128)(2,1)}, u32[]{:S(2)}, u32[]{:S(2)}) collective-permute-start(bf16[3072,384]{1,0:T(8,128)(2,1)} %pad_maximum_fusion.3), channel_id=1, source_target_pairs={{0,2},{1,3},{2,0},{3,1},{4,6},{5,7},{6,4},{7,5},{8,10},{9,11},{10,... | collective-permute-start | bytes 7077896 | tf_op jit(solution)/shard_map/ppermute | solution.py:814
  312.3 32.6 %collective-permute-start.34 = (bf16[2,2,4,256,384]{4,3,2,1,0:T(8,128)(2,1)}, bf16[2,2,4,256,384]{4,3,2,1,0:T(8,128)(2,1)}, u32[]{:S(2)}, u32[]{:S(2)}) collective-permute-start(bf16[2,2,4,256,384]{4,3,2,1,0:T(8,128)(2,1)} %get-tuple-element.606), channel_id=1, source_target_pairs={{0,1},{1,0},{2,3},{3,2},{4,5},{5,4},{6,7},{7,6},{8,9},{9,8},{10,11... | collective-permute-start | bytes 9437192 | tf_op jit(solution)/shard_map/ppermute | solution.py:811
  316.1 28.7 %collective-permute-start.33 = (bf16[1536,384]{1,0:T(8,128)(2,1)}, bf16[1536,384]{1,0:T(8,128)(2,1)}, u32[]{:S(2)}, u32[]{:S(2)}) collective-permute-start(bf16[1536,384]{1,0:T(8,128)(2,1)} %add_convert_fusion.6), channel_id=1, source_target_pairs={{0,4},{4,0},{8,12},{12,8},{16,20},{20,16},{24,28},{28,24},{1,5},{5... | collective-permute-start | bytes 3538952 | tf_op jit(solution)/shard_map/ppermute | solution.py:818
  316.2 28.7 %collective-permute-start.35 = (bf16[2,1024,384]{2,1,0:T(8,128)(2,1)}, bf16[2,1024,384]{2,1,0:T(8,128)(2,1)}, u32[]{:S(2)}, u32[]{:S(2)}) collective-permute-start(bf16[2,1024,384]{2,1,0:T(8,128)(2,1)} %get-tuple-element.607), channel_id=1, source_target_pairs={{0,1},{1,0},{2,3},{3,2},{4,5},{5,4},{6,7},{7,6},{8,9},{9,8},{10,11... | collective-permute-start | bytes 4718600 | tf_op jit(solution)/shard_map/ppermute | solution.py:811
  364.7 49.2 %collective-permute-start.36 = (bf16[768,384]{1,0:T(8,128)(2,1)}, bf16[768,384]{1,0:T(8,128)(2,1)}, u32[]{:S(2)}, u32[]{:S(2)}) collective-permute-start(bf16[768,384]{1,0:T(8,128)(2,1)} %add_convert_fusion.10), channel_id=1, source_target_pairs={{0,8},{4,12},{8,0},{12,4},{16,24},{20,28},{24,16},{28,20},{1,9},{5... | collective-permute-start | bytes 1769480 | tf_op jit(solution)/shard_map/ppermute | solution.py:818
  365.2 48.7 %collective-permute-start.39 = (bf16[2,256,1024]{2,1,0:T(8,128)(2,1)}, bf16[2,256,1024]{2,1,0:T(8,128)(2,1)}, u32[]{:S(2)}, u32[]{:S(2)}) collective-permute-start(bf16[2,256,1024]{2,1,0:T(8,128)(2,1)} %pad_maximum_fusion.7), channel_id=1, source_target_pairs={{0,1},{1,0},{2,3},{3,2},{4,5},{5,4},{6,7},{7,6},{8,9},{9,8},{10,11... | collective-permute-start | bytes 3145736 | tf_op jit(solution)/shard_map/ppermute | solution.py:811
  365.2 54.0 %collective-permute-start.37 = (bf16[3072,384]{1,0:T(8,128)(2,1)}, bf16[3072,384]{1,0:T(8,128)(2,1)}, u32[]{:S(2)}, u32[]{:S(2)}) collective-permute-start(bf16[3072,384]{1,0:T(8,128)(2,1)} %pad_maximum_fusion.4), channel_id=1, source_target_pairs={{0,2},{1,3},{2,0},{3,1},{4,6},{5,7},{6,4},{7,5},{8,10},{9,11},{10,... | collective-permute-start | bytes 7077896 | tf_op jit(solution)/shard_map/ppermute | solution.py:814
  366.7 53.7 %collective-permute-start.38 = (bf16[2,1536,384]{2,1,0:T(8,128)(2,1)}, bf16[2,1536,384]{2,1,0:T(8,128)(2,1)}, u32[]{:S(2)}, u32[]{:S(2)}) collective-permute-start(bf16[2,1536,384]{2,1,0:T(8,128)(2,1)} %get-tuple-element.650), channel_id=1, source_target_pairs={{0,4},{4,0},{8,12},{12,8},{16,20},{20,16},{24,28},{28,24},{1,5},{5... | collective-permute-start | bytes 7077896 | tf_op jit(solution)/shard_map/ppermute | solution.py:818
  430.3 32.7 %collective-permute-start.40 = (bf16[384,384]{1,0:T(8,128)(2,1)S(1)}, bf16[384,384]{1,0:T(8,128)(2,1)}, u32[]{:S(2)}, u32[]{:S(2)}) collective-permute-start(bf16[384,384]{1,0:T(8,128)(2,1)S(1)} %add_convert_fusion.16), channel_id=1, source_target_pairs={{0,16},{4,20},{8,24},{12,28},{16,0},{20,4},{24,8},{28,12},{1,17},{... | collective-permute-start | bytes 884744 | tf_op jit(solution)/shard_map/ppermute | solution.py:818
  433.9 29.1 %collective-permute-start.43 = (bf16[2,256,1024]{2,1,0:T(8,128)(2,1)}, bf16[2,256,1024]{2,1,0:T(8,128)(2,1)}, u32[]{:S(2)}, u32[]{:S(2)}) collective-permute-start(bf16[2,256,1024]{2,1,0:T(8,128)(2,1)} %get-tuple-element.685), channel_id=1, source_target_pairs={{0,1},{1,0},{2,3},{3,2},{4,5},{5,4},{6,7},{7,6},{8,9},{9,8},{10,11... | collective-permute-start | bytes 3145736 | tf_op jit(solution)/shard_map/ppermute | solution.py:811
  433.9 29.1 %collective-permute-start.41 = (bf16[1536,384]{1,0:T(8,128)(2,1)}, bf16[1536,384]{1,0:T(8,128)(2,1)}, u32[]{:S(2)}, u32[]{:S(2)}) collective-permute-start(bf16[1536,384]{1,0:T(8,128)(2,1)} %add_convert_fusion.5), channel_id=1, source_target_pairs={{0,4},{4,0},{8,12},{12,8},{16,20},{20,16},{24,28},{28,24},{1,5},{5... | collective-permute-start | bytes 3538952 | tf_op jit(solution)/shard_map/ppermute | solution.py:818
  435.4 28.4 %collective-permute-start.42 = (bf16[1536,384]{1,0:T(8,128)(2,1)}, bf16[1536,384]{1,0:T(8,128)(2,1)}, u32[]{:S(2)}, u32[]{:S(2)}) collective-permute-start(bf16[1536,384]{1,0:T(8,128)(2,1)} %fusion.10), channel_id=1, source_target_pairs={{0,2},{1,3},{2,0},{3,1},{4,6},{5,7},{6,4},{7,5},{8,10},{9,11},{10,... | collective-permute-start | bytes 3538952 | tf_op jit(solution)/shard_map/ppermute | solution.py:814
  473.3 183.1 %all-gather.11.cloned.1.call-start = ((), (), s32[]{:S(2)}) async-start(), calls=%async_computation.1 | async-start | bytes 2654208 | tf_op jit(solution)/shard_map/all_gather | solution.py:882
  476.4 29.3 %collective-permute-start.46 = (bf16[2,256,512]{2,1,0:T(8,128)(2,1)}, bf16[2,256,512]{2,1,0:T(8,128)(2,1)S(1)}, u32[]{:S(2)}, u32[]{:S(2)}) collective-permute-start(bf16[2,256,512]{2,1,0:T(8,128)(2,1)} %get-tuple-element.713), channel_id=1, source_target_pairs={{0,1},{1,0},{2,3},{3,2},{4,5},{5,4},{6,7},{7,6},{8,9},{9,8},{10,11... | collective-permute-start | bytes 1572872 | tf_op jit(solution)/shard_map/ppermute | solution.py:811
  476.4 29.3 %collective-permute-start.44 = (bf16[768,384]{1,0:T(8,128)(2,1)}, bf16[768,384]{1,0:T(8,128)(2,1)}, u32[]{:S(2)}, u32[]{:S(2)}) collective-permute-start(bf16[768,384]{1,0:T(8,128)(2,1)} %add_convert_fusion.9), channel_id=1, source_target_pairs={{0,8},{4,12},{8,0},{12,4},{16,24},{20,28},{24,16},{28,20},{1,9},{5... | collective-permute-start | bytes 1769480 | tf_op jit(solution)/shard_map/ppermute | solution.py:818
  478.0 50.0 %collective-permute-start.45 = (bf16[768,384]{1,0:T(8,128)(2,1)}, bf16[768,384]{1,0:T(8,128)(2,1)}, u32[]{:S(2)}, u32[]{:S(2)}) collective-permute-start(bf16[768,384]{1,0:T(8,128)(2,1)} %fusion.15), channel_id=1, source_target_pairs={{0,8},{4,12},{8,0},{12,4},{16,24},{20,28},{24,16},{28,20},{1,9},{5... | collective-permute-start | bytes 1769480 | tf_op jit(solution)/shard_map/ppermute | solution.py:818
  567.1 126.9 %all-gather.13.cloned.1.call-start = ((), (), s32[]{:S(2)}) async-start(), calls=%async_computation.2 | async-start | bytes 2654208 | tf_op jit(solution)/shard_map/all_gather | solution.py:882
  570.3 36.6 %collective-permute-start.50 = (bf16[1024,512]{1,0:T(8,128)(2,1)}, bf16[1024,512]{1,0:T(8,128)(2,1)}, u32[]{:S(2)}, u32[]{:S(2)}) collective-permute-start(bf16[1024,512]{1,0:T(8,128)(2,1)} %pad_maximum_fusion.8), channel_id=1, source_target_pairs={{0,2},{1,3},{2,0},{3,1},{4,6},{5,7},{6,4},{7,5},{8,10},{9,11},{10,... | collective-permute-start | bytes 3145736 | tf_op jit(solution)/shard_map/ppermute | solution.py:814
  570.8 36.2 %collective-permute-start.51 = (bf16[256,1024]{1,0:T(8,128)(2,1)}, bf16[256,1024]{1,0:T(8,128)(2,1)}, u32[]{:S(2)}, u32[]{:S(2)}) collective-permute-start(bf16[256,1024]{1,0:T(8,128)(2,1)} %fusion.27), channel_id=1, source_target_pairs={{0,2},{1,3},{2,0},{3,1},{4,6},{5,7},{6,4},{7,5},{8,10},{9,11},{10,... | collective-permute-start | bytes 1572872 | tf_op jit(solution)/shard_map/ppermute | solution.py:814
  (97 other events, 1095.2 us)
Sparse Core Ops, SparseCore 0:
  473.4 60.5 all-gather.8
  567.2 50.1 all-gather.10
  620.2 69.2 all-gather.12

commit v3 on v2

--- a/solution.py
+++ b/solution.py
@@ -396,6 +396,17 @@
     back = grad[...].astype(f32) + norm_back(second_grad * gain[...], unit, inverse)
     residual_grad[...] = back
     residual_low[...] = back.astype(bf16)
+
+
+def out_kernel(place_ref, mixed0, mixed1, residual_low, kept, sent, mixed):
+    for a in range(GRP):
+        half = (mixed0, mixed1)[a // 2]
+        first = a % 2 * GROUP_Q
+        mixed[a] = half[:, first : first + GROUP_Q]
+    for x in range(2):
+        for c, target in enumerate((kept, sent)):
+            part = dot_tn(mixed[place_ref[0] ^ (2 * x + c)], residual_low[...])
+            target[x] = part.astype(bf16)
 
 
 def last_kernel(tokens, residual_grad, gain, *refs):
@@ -727,6 +738,24 @@
     )
 
 
+def out_back(place, mixed0, mixed1, residual_low):
+    count = residual_low.shape[0]
+    return pl.pallas_call(
+        out_kernel,
+        grid_spec=pltpu.PrefetchScalarGridSpec(
+            num_scalar_prefetch=1,
+            grid=(1,),
+            in_specs=[whole((count, D // 2)), whole((count, D // 2)), whole((count, D))],
+            out_specs=[whole((2, ROWS, D)), whole((2, ROWS, D))],
+            scratch_shapes=[pltpu.VMEM((GRP, count, GROUP_Q), bf16)],
+        ),
+        out_shape=[struct((2, ROWS, D), bf16), struct((2, ROWS, D), bf16)],
+        compiler_params=params(60),
+        cost_estimate=cost(2e9, 6e6),
+        name="out_back",
+    )(place, mixed0, mixed1, residual_low)
+
+
 def last_norm(tokens, residual_grad, gain, first_grads):
     count = tokens.shape[0]
     return pl.pallas_call(
@@ -905,11 +934,11 @@
             job.advance(group)
         return outs
 
-    def finish_jobs(jobs):
+    def finish_jobs(jobs, after, made):
         running, turn = [], 0
         while not all(job.done for job in jobs):
             left = [job for job in jobs if not job.done and job not in [one for one, _ in running]]
-            payloads = tie(*[[values for values, _ in job.wanted] for job in left])
+            payloads, made = tie([[values for values, _ in job.wanted] for job in left], made)
             for job, group in zip(left, payloads):
                 job.start(group)
             slow = [job for job in left if isinstance(job.wanted[0][1], functools.partial)]
@@ -919,8 +948,10 @@
             running = [(job, due) for job, due in running if job not in ending]
             for job, group in zip(ending, tie(*[job.flight for job in ending])):
                 job.advance(group)
+                if job.done and job in after:
+                    made = after[job](job.result, made)
             turn += 1
-        return [job.result for job in jobs]
+        return [job.result for job in jobs], made
 
     def body(
         tokens, segments, attn_gain, w_query, w_key, w_value, query_gain, key_gain, w_out, ffn_gain,
@@ -1022,15 +1053,13 @@
             outs.append(out)
             second_grads.append(second_grad)
             early = (0,) if i == CHUNKS - 1 else ()
-            jobs.append(Job(reduce_stages([gu_kept, dn_kept], [], [gu_sent, dn_sent], early)))
+            jobs.append(
+                Job(reduce_stages([gu_kept, dn_kept], [], [gu_sent, dn_sent], early, early != ()))
+            )
 
         def after_and_out(*given):
             outputs, residual_grad, residual_low, ffn_gain_grad = after_ffn(*given[:-1])
-            wgrad = dot_tn(jnp.concatenate(given[-1], axis=1), residual_low)
-            wgrad = wgrad.astype(bf16).reshape(GRP, ROWS, D)
-            at = lambda q: lax.dynamic_slice_in_dim(wgrad, g ^ q, 1, 0)
-            out_kept = jnp.concatenate([at(0), at(2)], axis=0)
-            out_sent = jnp.concatenate([at(1), at(3)], axis=0)
+            out_kept, out_sent = out_back(place, *given[-1], residual_low)
             return outputs, residual_grad, residual_low, ffn_gain_grad, out_kept, out_sent
 
         outputs, residual_grad, residual_low, ffn_gain_grad, out_kept, out_sent = beside(
@@ -1058,22 +1087,19 @@
             first_grads.append(first_grad)
             head_grads.append(head_grad)
             cores.append(core_job.result[0])
-            by_group = [(kept[:, :, :GROUP_ALL], sent[:, :, :GROUP_ALL])]
-            if steps == 2:
-                by_group.append((kept[:, :, GROUP_ALL:], sent[:, :, GROUP_ALL:]))
-            kepts += [pair[0] for pair in by_group]
+            kepts.append(kept)
             to_send = [sent]
-        out_came, two_came, one_came = cores
-        came = [two_came[:, :, :GROUP_ALL], two_came[:, :, GROUP_ALL:], one_came]
-        attn_job = Job(reduce_stages(kepts, came, to_send, stepwise=True))
-        out_job = Job(reduce_stages([out_kept], [out_came], [], stepwise=True))
+            if steps == 1 and not last:
+                out_came, two_came = cores
+                halves = lambda values, size: [values[:, :, :size], values[:, :, size:]]
+                kept_a = halves(kepts[0], GROUP_ALL) + halves(out_kept, D // 2)
+                came_a = halves(two_came, GROUP_ALL) + halves(out_came, D // 2)
+                jobs.append(Job(reduce_stages(kept_a, came_a, [], stepwise=True)))
+                jobs[-1].advance([])
+        jobs.append(Job(reduce_stages(kepts[1:], cores[2:], to_send, stepwise=True)))
         input_grad, attn_gain_grad = beside(
-            last_norm,
-            (tokens, residual_grad, attn_full, first_grads),
-            jobs[1:] + [attn_job, out_job],
-            jobs + [attn_job, out_job],
+            last_norm, (tokens, residual_grad, attn_full, first_grads), jobs[1:], jobs
         )
-        jobs += [attn_job, out_job]
 
         head_grad = sum(head_grads).reshape(GROUP_QK // HD, HD)
         small = jnp.concatenate(
@@ -1085,12 +1111,16 @@
             ]
         )
         jobs.append(Job(small_stages(small.reshape(1, -1))))
-        sum0, sum1, sum2, attn_sum, out_sum, small = finish_jobs(jobs)
+        after = {
+            job: lambda total, held, i=i: finish(i, total, held)
+            for i, job in enumerate(jobs[:CHUNKS])
+        }
+        held = after[jobs[0]](jobs[0].result, ()) if jobs[0].done else ()
+        results, (gate_grad, up_grad, down_grad) = finish_jobs(jobs, after, held)
+        sums_a, sums_b, small = results[CHUNKS:]
+        out_sum = jnp.concatenate([sums_a[2 * ROWS : 3 * ROWS], sums_a[3 * ROWS :]], axis=1)
+        attn_sum = jnp.concatenate([sums_a[: 2 * ROWS], sums_b], axis=0)
         mine = lambda start, size: lax.dynamic_slice_in_dim(small[0], start + g * size, size, 0)
-        held = ()
-        for i, total in enumerate((sum0, sum1, sum2)):
-            held = finish(i, total, held)
-        gate_grad, up_grad, down_grad = held
         query_grad, key_grad, value_grad = split_sums(attn_sum)
         return (
             outputs,

time: 745 us -> 744 us (level)
  waiting for transfers between devices: 167 us -> 153 us
    ppermute x10, waiting for transfers between devices: 53.5 us -> 18.2 us  [to_far(): return lax.ppermute(values, 'grp', far_pairs)]
    ppermute x40 -> x43, waiting for transfers between devices: 111 us -> 125 us  [by_xor(): return lambda values: lax.ppermute(values, 'rep', pairs)]
    squeeze x10 -> x12, local copies, waits for them, and re-layouts: 8.03 us -> 15.2 us  [reduce_stages(): values[0]]
    ppermute x40 -> x43, starting transfers between devices: 45.8 us -> 47.2 us  [by_xor(): return lambda values: lax.ppermute(values, 'rep', pairs)]
    concatenate x6 -> x7, other arithmetic: 16.6 us -> 16.5 us  [reduce_stages(): jnp.concatenate(parts, axis=axis)]
  transfers between devices with their start and end apart: 72 -> 74, of which waited for: 26 -> 28; matrix products, arithmetic and copies ran while one was open for 12% -> 12% of each run, Pallas kernels for 43% -> 43%
where the time goes in v3:
time: 744 us; the launch traced here: 733 us
  Pallas kernels  332 us (45%)
  waiting for transfers between devices  153 us (21%)
  other arithmetic  110 us (15%)
  starting transfers between devices  64.7 us (9%)
  local copies, waits for them, and re-layouts  51.4 us (7%)
  between operations  15.3 us (2%)
    pallas_call x3, Pallas kernels, ffn(): pl.pallas_call(ffn_kernel, grid_spec=pltpu.PrefetchScalarGridSpec(num_sca...  134 us
    ppermute x43, waiting for transfers between devices, by_xor(): return lambda values: lax.ppermute(values, 'rep', pairs)  125 us
    pallas_call x3, Pallas kernels, attend_back(): pl.pallas_call(attend_back_kernel, grid_spec=pltpu.PrefetchScalarGridSpec...  92.8 us
    convert_element_type x30, other arithmetic, low_sum(): return sum((term.astype(f32) for term in terms)).astype(bf16)  67.2 us
    ppermute x43, starting transfers between devices, by_xor(): return lambda values: lax.ppermute(values, 'rep', pairs)  47.2 us
    pallas_call x2, Pallas kernels, attend(): pl.pallas_call(attend_kernel, grid_spec=pltpu.PrefetchScalarGridSpec(num_...  40.5 us
    ppermute x10, waiting for transfers between devices, to_far(): return lax.ppermute(values, 'grp', far_pairs)  18.2 us
    concatenate x7, other arithmetic, reduce_stages(): jnp.concatenate(parts, axis=axis)  16.5 us
  transfers between devices with their start and end apart: 74, of which 28 were waited for; matrix products, arithmetic and copies ran while one was open for 12% of the time, Pallas kernels for 43%

profile of v3, /device:TPU:0, one launch (start us, length us, event | category | flops | bytes accessed | tf_op | source)
XLA Modules:
  0.0 733.1 jit_solution(11127403173990653470)
XLA Ops:
  18.4 7.3 %all-gather.3 = bf16[4,1,640]{2,1,0:T(2,128)(2,1)S(1)} all-gather(bf16[1,1,640]{2,1,0:T(2,128)(2,1)S(1)} %reshape.199), channel_id=2, replica_groups=mesh['rep'=8,'grp'=4] {'grp'}, dimensions={0}, use_global_device_ids=true | all-gather | bytes 6400 | tf_op jit(solution)/shard_map/all_gather | solution.py:985
  29.8 8.0 %collective-permute-done.2 = bf16[64,3072]{1,0:T(8,128)(2,1)S(1)} collective-permute-done((bf16[64,3072]{1,0:T(8,128)(2,1)S(1)}, bf16[64,3072]{1,0:T(8,128)(2,1)S(1)}, u32[]{:S(2)}, u32[]{:S(2)}) %collective-permute-start.2) | collective-permute-done | bytes 393248 | tf_op jit(solution)/shard_map/ppermute | solution.py:847
  40.6 5.6 first_norm.1
  57.6 5.2 collective-permute-done.7
  73.2 20.0 %attend.2 = (f32[1024,768]{1,0:T(8,128)}, bf16[1024,768]{1,0:T(8,128)(2,1)}, bf16[1024,256]{1,0:T(8,128)(2,1)}, bf16[1024,512]{1,0:T(8,128)(2,1)}, f32[1024,512]{1,0:T(8,128)}, /*index=5*/bf16[1024,1024]{1,0:T(8,128)(2,1)}) custom-call(s32[2]{0:T(128)} %pad_add_fusion.place_ref, bf16[1024,1024]{1,0:T(8,128)(2,1)} %get-tuple-element.487.first, ...), custom_call_target="tpu_custom_call" | custom-call | flops 10000000000 | bytes 12000000 | tf_op jit(solution)/shard_map/attend/pallas_call | solution.py:530
  105.3 20.5 %attend.3 = (f32[1024,768]{1,0:T(8,128)}, bf16[1024,768]{1,0:T(8,128)(2,1)}, bf16[1024,256]{1,0:T(8,128)(2,1)}, bf16[1024,512]{1,0:T(8,128)(2,1)}, f32[1024,512]{1,0:T(8,128)}, /*index=5*/bf16[1024,1024]{1,0:T(8,128)(2,1)}) custom-call(s32[2]{0:T(128)} %pad_add_fusion.place_ref, bf16[1024,1024]{1,0:T(8,128)(2,1)} %get-tuple-element.487.first, ...), custom_call_target="tpu_custom_call" | custom-call | flops 10000000000 | bytes 12000000 | tf_op jit(solution)/shard_map/attend/pallas_call | solution.py:530
  134.1 9.6 %middle.1 = (f32[1024,1024]{1,0:T(8,128)}, bf16[1024,1024]{1,0:T(8,128)(2,1)}, bf16[1024,1024]{1,0:T(8,128)(2,1)}, bf16[1024,1024]{1,0:T(8,128)(2,1)}) custom-call(s32[2]{0:T(128)} %pad_add_fusion.place_ref, bf16[1024,512]{1,0:T(8,128)(2,1)} %get-tuple-element.663.mixed0.mixed, bf16[1024,512]{1,0:T(8,128)(2,1)} %get-tuple-element.730.mixed1.mixed, ...), custom_call_target="tpu_custom_call" | custom-call | flops 2000000000 | bytes 16000000 | tf_op jit(solution)/shard_map/middle/pallas_call | solution.py:581
  150.5 44.6 %ffn.3 = (bf16[1024,1024]{1,0:T(8,128)(2,1)}, bf16[1024,1024]{1,0:T(8,128)(2,1)}, bf16[2,2,4,256,384]{4,3,2,1,0:T(8,128)(2,1)}, bf16[2,2,4,256,384]{4,3,2,1,0:T(...) custom-call(s32[2]{0:T(128)} %pad_add_fusion.place_ref, ...), custom_call_target="tpu_custom_call" | custom-call | flops 28999999488 | bytes 36000000 | tf_op jit(solution)/shard_map/ffn/pallas_call | solution.py:621
  200.4 44.7 %ffn.4 = (bf16[1024,1024]{1,0:T(8,128)(2,1)}, bf16[1024,1024]{1,0:T(8,128)(2,1)}, bf16[2,2,4,256,384]{4,3,2,1,0:T(8,128)(2,1)}, bf16[2,2,4,256,384]{4,3,2,1,0:T(...) custom-call(s32[2]{0:T(128)} %pad_add_fusion.place_ref, ...), custom_call_target="tpu_custom_call" | custom-call | flops 28999999488 | bytes 36000000 | tf_op jit(solution)/shard_map/ffn/pallas_call | solution.py:621
  256.0 44.8 %ffn.5 = (bf16[1024,1024]{1,0:T(8,128)(2,1)}, bf16[1024,1024]{1,0:T(8,128)(2,1)}, bf16[2,2,4,256,384]{4,3,2,1,0:T(8,128)(2,1)}, bf16[2,2,4,256,384]{4,3,2,1,0:T(...) custom-call(s32[2]{0:T(128)} %pad_add_fusion.place_ref, ...), custom_call_target="tpu_custom_call" | custom-call | flops 28999999488 | bytes 36000000 | tf_op jit(solution)/shard_map/ffn/pallas_call | solution.py:621
  300.9 6.6 collective-permute-done.30
  307.4 4.9 add_convert_fusion.6
  320.7 10.7 %after_ffn.1 = (bf16[1024,1024]{1,0:T(8,128)(2,1)}, f32[1024,1024]{1,0:T(8,128)}, bf16[1024,1024]{1,0:T(8,128)(2,1)}, f32[1,1024]{1,0:T(1,128)}) custom-call(f32[1024,1024]{1,0:T(8,128)} %get-tuple-element.615.residual, bf16[1024,1024]{1,0:T(8,128)(2,1)} %grad.5, f32[1,1024]{1,0:T(1,128)} %bitcast.171, bf16[1024,1024]{1,0:T(8,128)(2,1)} %get-tuple-element.618.out0, ...), custom_call_target="tpu_custom_call" | custom-call | flops 20000000 | bytes 24000000 | tf_op jit(solution)/shard_map/after_ffn/pallas_call | solution.py:665
  333.6 6.5 out_back.1
  351.1 10.0 %fusion.1 = (bf16[2,1536,384]{2,1,0:T(8,128)(2,1)}, bf16[2,1536,384]{2,1,0:T(8,128)(2,1)}) fusion(s32[]{:T(128)S(6)} %select_n.328, bf16[2,2048,384]{2,1,0:T(8,128)(2,1)S(1)} %bitcast.148, bf16[2,1024,384]{2,1,0:T(8,128)(2,1)S(1)} %add_convert_fusion.1, s32[]{:T(128)S(6)} %select_n.325), kind=kLoop, calls=%fused_computation.43 | loop fusion | flops 9437184 | bytes 9437192 | tf_op jit(solution)/shard_map/concatenate | solution.py:871
  369.5 43.2 %attend_back.3 = (bf16[1024,1024]{1,0:T(8,128)(2,1)}, bf16[2,256,1024]{2,1,0:T(8,128)(2,1)}, bf16[2,256,1024]{2,1,0:T(8,128)(2,1)}, f32[1,384]{1,0:T(1,128)}) custom-call(s32[2]{0:T(128)} %pad_add_fusion.place_ref, bf16[1024,1024]{1,0:T(8,128)(2,1)} %get-tuple-element.723.residual_low, bf16[1024,1024]{1,0:T(8,128)(2,1)} %get-tuple-element.724.w_out, ...), custom_call_target="tpu_custom_call" | custom-call | flops 30000001024 | bytes 20000000 | tf_op jit(solution)/shard_map/attend_back/pallas_call | solution.py:690
  427.1 4.6 add_convert_fusion.5
  437.5 24.5 %attend_back.4 = (bf16[1024,1024]{1,0:T(8,128)(2,1)}, bf16[2,256,512]{2,1,0:T(8,128)(2,1)}, bf16[2,256,512]{2,1,0:T(8,128)(2,1)}, f32[1,384]{1,0:T(1,128)}) custom-call(s32[2]{0:T(128)} %pad_add_fusion.place_ref, bf16[1024,1024]{1,0:T(8,128)(2,1)} %get-tuple-element.723.residual_low, bf16[1024,1024]{1,0:T(8,128)(2,1)} %get-tuple-element.724.w_out, ...), custom_call_target="tpu_custom_call" | custom-call | flops 30000001024 | bytes 20000000 | tf_op jit(solution)/shard_map/attend_back/pallas_call | solution.py:690
  472.7 3.9 add_convert_fusion.9
  487.6 25.1 %attend_back.5 = (bf16[1024,1024]{1,0:T(8,128)(2,1)}, bf16[2,256,512]{2,1,0:T(8,128)(2,1)}, bf16[2,256,512]{2,1,0:T(8,128)(2,1)}, f32[1,384]{1,0:T(1,128)}) custom-call(s32[2]{0:T(128)} %pad_add_fusion.place_ref, bf16[1024,1024]{1,0:T(8,128)(2,1)} %get-tuple-element.723.residual_low, bf16[1024,1024]{1,0:T(8,128)(2,1)} %get-tuple-element.724.w_out, ...), custom_call_target="tpu_custom_call" | custom-call | flops 30000001024 | bytes 20000000 | tf_op jit(solution)/shard_map/attend_back/pallas_call | solution.py:690
  516.9 13.9 %collective-permute-done.45 = bf16[768,384]{1,0:T(8,128)(2,1)} collective-permute-done((bf16[768,384]{1,0:T(8,128)(2,1)}, bf16[768,384]{1,0:T(8,128)(2,1)}, u32[]{:S(2)}, u32[]{:S(2)}) %collective-permute-start.45) | collective-permute-done | bytes 589856 | tf_op jit(solution)/shard_map/ppermute | solution.py:847
  540.4 7.8 %last_norm.1 = (bf16[1024,1024]{1,0:T(8,128)(2,1)}, f32[1,1024]{1,0:T(1,128)}) custom-call(bf16[1024,1024]{1,0:T(8,128)(2,1)} %tokens.4, f32[1024,1024]{1,0:T(8,128)} %get-tuple-element.752.residual_grad, f32[1,1024]{1,0:T(1,128)} %bitcast.173, bf16[1024,1024]{1,0:T(8,128)(2,1)} %get-tuple-element.754.refs_0_, ...), custom_call_target="tpu_custom_call" | custom-call | flops 20000000 | bytes 12000000 | tf_op jit(solution)/shard_map/last_norm/pallas_call | solution.py:761
  549.9 6.5 all-gather.7.cloned.1.call-done
  560.9 6.1 collective-permute-done.49
  571.8 4.7 finish.3
  585.3 8.8 %collective-permute-done.53 = bf16[256,512]{1,0:T(8,128)(2,1)S(1)} collective-permute-done((bf16[256,512]{1,0:T(8,128)(2,1)S(1)}, bf16[256,512]{1,0:T(8,128)(2,1)S(1)}, u32[]{:S(2)}, u32[]{:S(2)}) %collective-permute-start.53) | collective-permute-done | bytes 262176 | tf_op jit(solution)/shard_map/ppermute | solution.py:847
  609.5 18.0 %collective-permute-done.57 = bf16[128,512]{1,0:T(8,128)(2,1)} collective-permute-done((bf16[128,512]{1,0:T(8,128)(2,1)}, bf16[128,512]{1,0:T(8,128)(2,1)}, u32[]{:S(2)}, u32[]{:S(2)}) %collective-permute-start.57) | collective-permute-done | bytes 131104 | tf_op jit(solution)/shard_map/ppermute | solution.py:847
  639.3 33.1 %collective-permute-done.63 = f32[1,2176]{1,0:T(1,128)S(1)} collective-permute-done((f32[1,2176]{1,0:T(1,128)S(1)}, f32[1,2176]{1,0:T(1,128)S(1)}, u32[]{:S(2)}, u32[]{:S(2)}) %collective-permute-start.63) | collective-permute-done | bytes 8736 | tf_op jit(solution)/shard_map/ppermute | solution.py:847
  675.9 4.5 finish.4
  693.0 4.5 finish.5
  700.7 3.9 collective-permute-done.69
  704.6 5.2 collective-permute-done.67
  (411 shorter events, 250.6 us)
Async XLA Ops:
  7.2 549.3 %all-gather.7.cloned.1.call-start = ((), (), s32[]{:S(2)}) async-start(), calls=%async_computation | async-start | bytes 2654208 | tf_op jit(solution)/shard_map/all_gather | solution.py:911
  11.3 38.8 %collective-permute-start.4 = (bf16[256,3072]{1,0:T(8,128)(2,1)}, bf16[256,3072]{1,0:T(8,128)(2,1)S(1)}, u32[]{:S(2)}, u32[]{:S(2)}) collective-permute-start(bf16[256,3072]{1,0:T(8,128)(2,1)} %get-tuple-element.488.own), channel_id=1, source_target_pairs={{0,1},{1,0},{2,3},{3,2},{4,5},{5,4},{6,7},{7,6},{8,9},{9,8},{10,11... | collective-permute-start | bytes 4718600 | tf_op jit(solution)/shard_map/ppermute | solution.py:840
  11.7 51.1 %collective-permute-start.8 = (bf16[256,4608]{1,0:T(8,128)(2,1)}, bf16[256,4608]{1,0:T(8,128)(2,1)}, u32[]{:S(2)}, u32[]{:S(2)}) collective-permute-start(bf16[256,4608]{1,0:T(8,128)(2,1)} %gate1.2), channel_id=1, source_target_pairs={{0,1},{1,0},{2,3},{3,2},{4,5},{5,4},{6,7},{7,6},{8,9},{9,8},{10,11... | collective-permute-start | bytes 7077896 | tf_op jit(solution)/shard_map/ppermute | solution.py:840
  11.8 51.1 %collective-permute-start.9 = (bf16[256,4608]{1,0:T(8,128)(2,1)}, bf16[256,4608]{1,0:T(8,128)(2,1)}, u32[]{:S(2)}, u32[]{:S(2)}) collective-permute-start(bf16[256,4608]{1,0:T(8,128)(2,1)} %up1.2), channel_id=1, source_target_pairs={{0,1},{1,0},{2,3},{3,2},{4,5},{5,4},{6,7},{7,6},{8,9},{9,8},{10,11... | collective-permute-start | bytes 7077896 | tf_op jit(solution)/shard_map/ppermute | solution.py:840
  147.4 47.7 %collective-permute-start.26 = (bf16[384,384]{1,0:T(8,128)(2,1)S(1)}, bf16[384,384]{1,0:T(8,128)(2,1)S(1)}, u32[]{:S(2)}, u32[]{:S(2)}) collective-permute-start(bf16[384,384]{1,0:T(8,128)(2,1)S(1)} %slice.221), channel_id=1, source_target_pairs={{0,4},{4,0},{8,12},{12,8},{16,20},{20,16},{24,28},{28,24},{1,5},{5... | collective-permute-start | bytes 884744 | tf_op jit(solution)/shard_map/ppermute | solution.py:847
  148.9 46.2 %collective-permute-start.25 = (bf16[384,384]{1,0:T(8,128)(2,1)S(1)}, bf16[384,384]{1,0:T(8,128)(2,1)S(1)}, u32[]{:S(2)}, u32[]{:S(2)}) collective-permute-start(bf16[384,384]{1,0:T(8,128)(2,1)S(1)} %slice.220), channel_id=1, source_target_pairs={{0,8},{4,12},{8,0},{12,4},{16,24},{20,28},{24,16},{28,20},{1,9},{5... | collective-permute-start | bytes 884744 | tf_op jit(solution)/shard_map/ppermute | solution.py:847
  198.2 46.9 %collective-permute-start.27 = (bf16[2,2,4,256,384]{4,3,2,1,0:T(8,128)(2,1)}, bf16[2,2,4,256,384]{4,3,2,1,0:T(8,128)(2,1)}, u32[]{:S(2)}, u32[]{:S(2)}) collective-permute-start(bf16[2,2,4,256,384]{4,3,2,1,0:T(8,128)(2,1)} %get-tuple-element.574), channel_id=1, source_target_pairs={{0,1},{1,0},{2,3},{3,2},{4,5},{5,4},{6,7},{7,6},{8,9},{9,8},{10,11... | collective-permute-start | bytes 9437192 | tf_op jit(solution)/shard_map/ppermute | solution.py:840
  199.8 45.3 %collective-permute-start.28 = (bf16[2,1024,384]{2,1,0:T(8,128)(2,1)}, bf16[2,1024,384]{2,1,0:T(8,128)(2,1)S(1)}, u32[]{:S(2)}, u32[]{:S(2)}) collective-permute-start(bf16[2,1024,384]{2,1,0:T(8,128)(2,1)} %get-tuple-element.575), channel_id=1, source_target_pairs={{0,1},{1,0},{2,3},{3,2},{4,5},{5,4},{6,7},{7,6},{8,9},{9,8},{10,11... | collective-permute-start | bytes 4718600 | tf_op jit(solution)/shard_map/ppermute | solution.py:840
  200.4 48.4 %collective-permute-start.29 = (bf16[4,768,384]{2,1,0:T(8,128)(2,1)}, bf16[4,768,384]{2,1,0:T(8,128)(2,1)}, u32[]{:S(2)}, u32[]{:S(2)}) collective-permute-start(bf16[4,768,384]{2,1,0:T(8,128)(2,1)} %pad_maximum_fusion.2.far), channel_id=1, source_target_pairs={{0,1},{1,0},{2,3},{3,2},{4,5},{5,4},{6,7},{7,6},{8,9},{9,8},{10,11... | collective-permute-start | bytes 7077896 | tf_op jit(solution)/shard_map/ppermute | solution.py:840
  251.0 56.4 %collective-permute-start.31 = (bf16[2,2,4,256,384]{4,3,2,1,0:T(8,128)(2,1)}, bf16[2,2,4,256,384]{4,3,2,1,0:T(8,128)(2,1)}, u32[]{:S(2)}, u32[]{:S(2)}) collective-permute-start(bf16[2,2,4,256,384]{4,3,2,1,0:T(8,128)(2,1)} %get-tuple-element.606), channel_id=1, source_target_pairs={{0,1},{1,0},{2,3},{3,2},{4,5},{5,4},{6,7},{7,6},{8,9},{9,8},{10,11... | collective-permute-start | bytes 9437192 | tf_op jit(solution)/shard_map/ppermute | solution.py:840
  253.4 47.5 %collective-permute-start.32 = (bf16[2,1024,384]{2,1,0:T(8,128)(2,1)}, bf16[2,1024,384]{2,1,0:T(8,128)(2,1)}, u32[]{:S(2)}, u32[]{:S(2)}) collective-permute-start(bf16[2,1024,384]{2,1,0:T(8,128)(2,1)} %get-tuple-element.607), channel_id=1, source_target_pairs={{0,1},{1,0},{2,3},{3,2},{4,5},{5,4},{6,7},{7,6},{8,9},{9,8},{10,11... | collective-permute-start | bytes 4718600 | tf_op jit(solution)/shard_map/ppermute | solution.py:840
  253.5 53.9 %collective-permute-start.30 = (bf16[3072,384]{1,0:T(8,128)(2,1)}, bf16[3072,384]{1,0:T(8,128)(2,1)}, u32[]{:S(2)}, u32[]{:S(2)}) collective-permute-start(bf16[3072,384]{1,0:T(8,128)(2,1)} %pad_maximum_fusion.3), channel_id=1, source_target_pairs={{0,2},{1,3},{2,0},{3,1},{4,6},{5,7},{6,4},{7,5},{8,10},{9,11},{10,... | collective-permute-start | bytes 7077896 | tf_op jit(solution)/shard_map/ppermute | solution.py:843
  312.3 33.6 %collective-permute-start.34 = (bf16[2,2,4,256,384]{4,3,2,1,0:T(8,128)(2,1)}, bf16[2,2,4,256,384]{4,3,2,1,0:T(8,128)(2,1)}, u32[]{:S(2)}, u32[]{:S(2)}) collective-permute-start(bf16[2,2,4,256,384]{4,3,2,1,0:T(8,128)(2,1)} %get-tuple-element.633), channel_id=1, source_target_pairs={{0,1},{1,0},{2,3},{3,2},{4,5},{5,4},{6,7},{7,6},{8,9},{9,8},{10,11... | collective-permute-start | bytes 9437192 | tf_op jit(solution)/shard_map/ppermute | solution.py:840
  312.3 33.5 %collective-permute-start.35 = (bf16[2,1024,384]{2,1,0:T(8,128)(2,1)}, bf16[2,1024,384]{2,1,0:T(8,128)(2,1)}, u32[]{:S(2)}, u32[]{:S(2)}) collective-permute-start(bf16[2,1024,384]{2,1,0:T(8,128)(2,1)} %get-tuple-element.634), channel_id=1, source_target_pairs={{0,1},{1,0},{2,3},{3,2},{4,5},{5,4},{6,7},{7,6},{8,9},{9,8},{10,11... | collective-permute-start | bytes 4718600 | tf_op jit(solution)/shard_map/ppermute | solution.py:840
  365.9 51.3 %collective-permute-start.36 = (bf16[768,384]{1,0:T(8,128)(2,1)}, bf16[768,384]{1,0:T(8,128)(2,1)}, u32[]{:S(2)}, u32[]{:S(2)}) collective-permute-start(bf16[768,384]{1,0:T(8,128)(2,1)} %add_convert_fusion.10), channel_id=1, source_target_pairs={{0,8},{4,12},{8,0},{12,4},{16,24},{20,28},{24,16},{28,20},{1,9},{5... | collective-permute-start | bytes 1769480 | tf_op jit(solution)/shard_map/ppermute | solution.py:847
  366.3 50.8 %collective-permute-start.39 = (bf16[2,256,1024]{2,1,0:T(8,128)(2,1)}, bf16[2,256,1024]{2,1,0:T(8,128)(2,1)}, u32[]{:S(2)}, u32[]{:S(2)}) collective-permute-start(bf16[2,256,1024]{2,1,0:T(8,128)(2,1)} %get-tuple-element.678), channel_id=1, source_target_pairs={{0,1},{1,0},{2,3},{3,2},{4,5},{5,4},{6,7},{7,6},{8,9},{9,8},{10,11... | collective-permute-start | bytes 3145736 | tf_op jit(solution)/shard_map/ppermute | solution.py:840
  366.3 54.0 %collective-permute-start.37 = (bf16[3072,384]{1,0:T(8,128)(2,1)}, bf16[3072,384]{1,0:T(8,128)(2,1)}, u32[]{:S(2)}, u32[]{:S(2)}) collective-permute-start(bf16[3072,384]{1,0:T(8,128)(2,1)} %pad_maximum_fusion.4), channel_id=1, source_target_pairs={{0,2},{1,3},{2,0},{3,1},{4,6},{5,7},{6,4},{7,5},{8,10},{9,11},{10,... | collective-permute-start | bytes 7077896 | tf_op jit(solution)/shard_map/ppermute | solution.py:843
  367.8 53.7 %collective-permute-start.38 = (bf16[2,1536,384]{2,1,0:T(8,128)(2,1)}, bf16[2,1536,384]{2,1,0:T(8,128)(2,1)}, u32[]{:S(2)}, u32[]{:S(2)}) collective-permute-start(bf16[2,1536,384]{2,1,0:T(8,128)(2,1)} %get-tuple-element.677), channel_id=1, source_target_pairs={{0,4},{4,0},{8,12},{12,8},{16,20},{20,16},{24,28},{28,24},{1,5},{5... | collective-permute-start | bytes 7077896 | tf_op jit(solution)/shard_map/ppermute | solution.py:847
  431.7 39.0 %collective-permute-start.40 = (bf16[384,384]{1,0:T(8,128)(2,1)}, bf16[384,384]{1,0:T(8,128)(2,1)}, u32[]{:S(2)}, u32[]{:S(2)}) collective-permute-start(bf16[384,384]{1,0:T(8,128)(2,1)} %add_convert_fusion.15), channel_id=1, source_target_pairs={{0,16},{4,20},{8,24},{12,28},{16,0},{20,4},{24,8},{28,12},{1,17},{... | collective-permute-start | bytes 884744 | tf_op jit(solution)/shard_map/ppermute | solution.py:847
  435.3 35.4 %collective-permute-start.43 = (bf16[2,256,1024]{2,1,0:T(8,128)(2,1)}, bf16[2,256,1024]{2,1,0:T(8,128)(2,1)}, u32[]{:S(2)}, u32[]{:S(2)}) collective-permute-start(bf16[2,256,1024]{2,1,0:T(8,128)(2,1)} %get-tuple-element.712), channel_id=1, source_target_pairs={{0,1},{1,0},{2,3},{3,2},{4,5},{5,4},{6,7},{7,6},{8,9},{9,8},{10,11... | collective-permute-start | bytes 3145736 | tf_op jit(solution)/shard_map/ppermute | solution.py:840
  435.3 35.4 %collective-permute-start.41 = (bf16[1536,384]{1,0:T(8,128)(2,1)}, bf16[1536,384]{1,0:T(8,128)(2,1)}, u32[]{:S(2)}, u32[]{:S(2)}) collective-permute-start(bf16[1536,384]{1,0:T(8,128)(2,1)} %add_convert_fusion.5), channel_id=1, source_target_pairs={{0,4},{4,0},{8,12},{12,8},{16,20},{20,16},{24,28},{28,24},{1,5},{5... | collective-permute-start | bytes 3538952 | tf_op jit(solution)/shard_map/ppermute | solution.py:847
  437.0 33.7 %collective-permute-start.42 = (bf16[1536,384]{1,0:T(8,128)(2,1)}, bf16[1536,384]{1,0:T(8,128)(2,1)}, u32[]{:S(2)}, u32[]{:S(2)}) collective-permute-start(bf16[1536,384]{1,0:T(8,128)(2,1)} %fusion.3), channel_id=1, source_target_pairs={{0,2},{1,3},{2,0},{3,1},{4,6},{5,7},{6,4},{7,5},{8,10},{9,11},{10,... | collective-permute-start | bytes 3538952 | tf_op jit(solution)/shard_map/ppermute | solution.py:843
  483.0 201.6 %all-gather.9.cloned.1.call-start = ((), (), s32[]{:S(2)}) async-start(), calls=%async_computation.1 | async-start | bytes 2654208 | tf_op jit(solution)/shard_map/all_gather | solution.py:911
  484.1 32.8 %collective-permute-start.47 = (bf16[2,256,512]{2,1,0:T(8,128)(2,1)}, bf16[2,256,512]{2,1,0:T(8,128)(2,1)}, u32[]{:S(2)}, u32[]{:S(2)}) collective-permute-start(bf16[2,256,512]{2,1,0:T(8,128)(2,1)} %get-tuple-element.745), channel_id=1, source_target_pairs={{0,1},{1,0},{2,3},{3,2},{4,5},{5,4},{6,7},{7,6},{8,9},{9,8},{10,11... | collective-permute-start | bytes 1572872 | tf_op jit(solution)/shard_map/ppermute | solution.py:840
  484.1 32.8 %collective-permute-start.44 = (bf16[768,384]{1,0:T(8,128)(2,1)}, bf16[768,384]{1,0:T(8,128)(2,1)}, u32[]{:S(2)}, u32[]{:S(2)}) collective-permute-start(bf16[768,384]{1,0:T(8,128)(2,1)} %add_convert_fusion.9), channel_id=1, source_target_pairs={{0,8},{4,12},{8,0},{12,4},{16,24},{20,28},{24,16},{28,20},{1,9},{5... | collective-permute-start | bytes 1769480 | tf_op jit(solution)/shard_map/ppermute | solution.py:847
  485.7 45.1 %collective-permute-start.45 = (bf16[768,384]{1,0:T(8,128)(2,1)}, bf16[768,384]{1,0:T(8,128)(2,1)}, u32[]{:S(2)}, u32[]{:S(2)}) collective-permute-start(bf16[768,384]{1,0:T(8,128)(2,1)} %fusion.8), channel_id=1, source_target_pairs={{0,8},{4,12},{8,0},{12,4},{16,24},{20,28},{24,16},{28,20},{1,9},{5... | collective-permute-start | bytes 1769480 | tf_op jit(solution)/shard_map/ppermute | solution.py:847
  486.1 44.7 %collective-permute-start.46 = (bf16[1024,512]{1,0:T(8,128)(2,1)}, bf16[1024,512]{1,0:T(8,128)(2,1)}, u32[]{:S(2)}, u32[]{:S(2)}) collective-permute-start(bf16[1024,512]{1,0:T(8,128)(2,1)} %pad_maximum_fusion.8), channel_id=1, source_target_pairs={{0,2},{1,3},{2,0},{3,1},{4,6},{5,7},{6,4},{7,5},{8,10},{9,11},{10,... | collective-permute-start | bytes 3145736 | tf_op jit(solution)/shard_map/ppermute | solution.py:843
  537.2 29.8 %collective-permute-start.49 = (bf16[384,384]{1,0:T(8,128)(2,1)S(1)}, bf16[384,384]{1,0:T(8,128)(2,1)}, u32[]{:S(2)}, u32[]{:S(2)}) collective-permute-start(bf16[384,384]{1,0:T(8,128)(2,1)S(1)} %fusion.19), channel_id=1, source_target_pairs={{0,16},{4,20},{8,24},{12,28},{16,0},{20,4},{24,8},{28,12},{1,17},{... | collective-permute-start | bytes 884744 | tf_op jit(solution)/shard_map/ppermute | solution.py:847
  636.2 36.2 %collective-permute-start.60 = (bf16[1536,384]{1,0:T(8,128)(2,1)}, bf16[1536,384]{1,0:T(8,128)(2,1)}, u32[]{:S(2)}, u32[]{:S(2)}) collective-permute-start(bf16[1536,384]{1,0:T(8,128)(2,1)} %pad_maximum_fusion.7), channel_id=1, source_target_pairs={{0,4},{4,0},{8,12},{12,8},{16,20},{20,16},{24,28},{28,24},{1,5},{5... | collective-permute-start | bytes 3538952 | tf_op jit(solution)/shard_map/ppermute | solution.py:847
  636.6 35.8 %collective-permute-start.61 = (bf16[128,512]{1,0:T(8,128)(2,1)}, bf16[128,512]{1,0:T(8,128)(2,1)S(1)}, u32[]{:S(2)}, u32[]{:S(2)}) collective-permute-start(bf16[128,512]{1,0:T(8,128)(2,1)} %add_convert_fusion.25), channel_id=1, source_target_pairs={{0,16},{4,20},{8,24},{12,28},{16,0},{20,4},{24,8},{28,12},{1,17},{... | collective-permute-start | bytes 393224 | tf_op jit(solution)/shard_map/ppermute | solution.py:847
  637.3 35.1 %collective-permute-start.62 = (bf16[128,512]{1,0:T(8,128)(2,1)}, bf16[128,512]{1,0:T(8,128)(2,1)S(1)}, u32[]{:S(2)}, u32[]{:S(2)}) collective-permute-start(bf16[128,512]{1,0:T(8,128)(2,1)} %add_convert_fusion.24), channel_id=1, source_target_pairs={{0,8},{4,12},{8,0},{12,4},{16,24},{20,28},{24,16},{28,20},{1,9},{5... | collective-permute-start | bytes 393224 | tf_op jit(solution)/shard_map/ppermute | solution.py:847
  637.3 35.1 %collective-permute-start.63 = (f32[1,2176]{1,0:T(1,128)S(1)}, f32[1,2176]{1,0:T(1,128)S(1)}, u32[]{:S(2)}, u32[]{:S(2)}) collective-permute-start(f32[1,2176]{1,0:T(1,128)S(1)} %add.666), channel_id=1, source_target_pairs={{0,4},{4,0},{8,12},{12,8},{16,20},{20,16},{24,28},{28,24},{1,5},{5... | collective-permute-start | bytes 26120 | tf_op jit(solution)/shard_map/ppermute | solution.py:847
  (112 other events, 1357.9 us)
Sparse Core Ops, SparseCore 0:
  483.1 73.2 all-gather.6
  603.3 65.1 all-gather.8
